TPU v7x, 32 devices: a whole 2x2x4 slice. The times are simulated.
32 devices in a mesh: dp: 4 (over z), expert: 8 (over y, x, core).
Axes of the slice: x: 2, y: 2, z: 4, core: 2. Of those that a mesh axis runs over, the one named last changes fastest.
Arguments:
- tokens: bfloat16 [4096, 1536], P(('dp', 'expert')), may hold values from -6 to 6
- w_qkv: bfloat16 [2, 1536, 2048], P(None, ('dp', 'expert')), may hold values from -0.15625 to 0.15625
- w_out: bfloat16 [2, 1536, 1536], P(None, ('dp', 'expert')), may hold values from -1.25 to 1.25
- w_router: bfloat16 [2, 1536, 16], P(None, ('dp', 'expert')), may hold values from -0.078125 to 0.078125
- norm_gains: bfloat16 [2, 2, 1536], P(None, None, ('dp', 'expert')), may hold values from 0.099609375 to 1.8984375
- w_gate: bfloat16 [2, 16, 1536, 768], P(None, 'expert'), may hold values from -0.15625 to 0.15625
- w_up: bfloat16 [2, 16, 1536, 768], P(None, 'expert'), may hold values from -0.15625 to 0.15625
- w_down: bfloat16 [2, 16, 768, 1536], P(None, 'expert'), may hold values from -0.4375 to 0.4375
- out_grad: bfloat16 [4096, 1536], P(('dp', 'expert')), may hold values from -6 to 6
- segment_ids: int32 [4096], P(('dp', 'expert')), may hold values from 0 to 67, as said below
- routes: int32 [2, 4096, 4], P(None, ('dp', 'expert')), may hold values from 0 to 15, all different within a row; in each aligned block of 128 rows (0 to 127, 128 to 255, ..., all dimensions but the last counted through in order) at most 64 rows name the same one
- pair_order: int32 [2, 32, 512], P(None, ('dp', 'expert')), may hold values from 0 to 511, each once within a row
Outputs:
- layer_outs: bfloat16 [2, 4096, 1536], P(None, ('dp', 'expert'))
- tokens_grad: float32 [4096, 1536], P(('dp', 'expert'))
- grad_qkv: float32 [2, 1536, 2048], P(None, ('dp', 'expert'))
- grad_out: float32 [2, 1536, 1536], P(None, ('dp', 'expert'))
- grad_router: float32 [2, 1536, 16], P(None, ('dp', 'expert'))
- grad_gains: float32 [2, 2, 1536], P(None, None, ('dp', 'expert'))
- grad_gate: float32 [2, 16, 1536, 768], P(None, 'expert', 'dp')
- grad_up: float32 [2, 16, 1536, 768], P(None, 'expert', 'dp')
- grad_down: float32 [2, 16, 768, 1536], P(None, 'expert', None, 'dp')
Inputs may be any that keep to these rules, and one draw needn't show every extreme that they name: `segment_ids`: never falling; a new document starts at every multiple of 1024; each document lies within the tokens of at most two devices that are next to each other along dp+expert. `routes`: each token names 4 different experts; among one device's tokens of one layer no expert is named more than 64 times, a bound that some block reaches. `pair_order`: for each layer and device a permutation of the device's pairs, pair t * 4 + k being the k-th route of its t-th token.
All inputs are finite; a program needn't handle non-finite values.
Results may differ from a plain program's by a relative error of at most 0.023.
Values may be sent and summed in bfloat16 or wider, within the bound.
A program may use at most 256 MiB of HBM per device.

v0:
```python
from functools import partial
import math

import jax
import jax.numpy as jnp
from jax import lax
from jax.sharding import PartitionSpec as P

D = 1536
QUERY_HEADS = 12
KEY_VALUE_HEADS = 2
HEAD_SIZE = 128


epsilon = 1e-06
rope_base = 1000000.0
masked_score = -1e30


def from_behind(value, axis, steps):
    count = lax.axis_size(axis)
    leading, last = (max(0, -steps), min(count, count - steps))
    return lax.ppermute(value, axis, [(source, source + steps) for source in range(leading, last)])


def rms_norm(stream, gain_row):
    return (
        stream * lax.rsqrt(jnp.mean(stream * stream, axis=-1, keepdims=True) + epsilon) * gain_row
    )


def apply_rotary(heads_in, token_positions):
    half_dim = heads_in.shape[-1] // 2
    steps_up = jnp.arange(half_dim).astype(jnp.float32)
    frequency = jnp.exp(steps_up * (-2.0 * math.log(rope_base) / heads_in.shape[-1]))
    angles = token_positions.astype(jnp.float32)[:, None] * frequency[None, :]
    cosine = jnp.cos(angles)[:, None, :]
    sine_part = jnp.sin(angles)[:, None, :]
    first_half = heads_in[..., :half_dim]
    second_half = heads_in[..., half_dim:]
    return jnp.concatenate(
        [
            first_half * cosine - second_half * sine_part,
            second_half * cosine + first_half * sine_part,
        ],
        axis=-1,
    )


def gated_unit(gate_pre, up_pre):
    return jax.nn.silu(gate_pre) * up_pre


def pick_soft(chosen_logits):
    return jax.nn.softmax(chosen_logits, axis=-1)


def local_rank(chosen, priority):
    same_expert = chosen[:, None] == chosen[None, :]
    earlier = priority[None, :] < priority[:, None]
    return jnp.sum((same_expert & earlier).astype(jnp.int32), axis=1)


def receive_maps(columns, capacity, most_rows):
    n_source, local_n = columns.shape
    upto_incl = jnp.cumsum(columns, axis=0)
    upto_excl = upto_incl - columns
    seat_total = upto_incl[-1]
    seat_ids = jnp.arange(capacity, dtype=jnp.int32)
    source = jnp.sum((upto_incl[:, :, None] <= seat_ids[None, None, :]).astype(jnp.int32), axis=0)
    source = jnp.minimum(source, n_source - 1)
    start_seat = jnp.take_along_axis(upto_excl.T, source, axis=1)
    within = jnp.clip(seat_ids[None, :] - start_seat, 0, most_rows - 1)
    local_idx = jnp.arange(local_n, dtype=jnp.int32)[:, None]
    gather_at = (source * local_n + local_idx) * most_rows + within
    take_seat = seat_ids[None, :] < seat_total[:, None]
    slot_ids = jnp.arange(most_rows, dtype=jnp.int32)[None, None, :]
    seat_back = upto_excl[:, :, None] + slot_ids
    give_seat = (slot_ids < columns[:, :, None]) & (seat_back < capacity)
    back_at = local_idx[None] * capacity + jnp.clip(seat_back, 0, capacity - 1)
    return (gather_at, take_seat, back_at, give_seat)


def pack_rows(row_values, chosen, pair_rank, experts_n, most_rows):
    buffer = jnp.zeros((experts_n, most_rows, row_values.shape[1]), row_values.dtype)
    return buffer.at[chosen, pair_rank].set(row_values)


def unpack_rows(received, gather_at, take_seat):
    flat_rows = received.reshape(-1, received.shape[-1])
    return jnp.where(take_seat[..., None], flat_rows[gather_at], jnp.zeros((), received.dtype))


def repack_rows(results, back_at, give_seat, experts_n):
    flat_rows = results.reshape(-1, results.shape[-1])
    picked = jnp.where(give_seat[..., None], flat_rows[back_at], jnp.zeros((), results.dtype))
    return picked.reshape(experts_n, -1, results.shape[-1])


def masked_scores(query_rows, gathered_keys, allowed):
    token_rows = query_rows.shape[0]
    grouped_queries = query_rows.reshape(
        token_rows, KEY_VALUE_HEADS, QUERY_HEADS // KEY_VALUE_HEADS, HEAD_SIZE
    )
    score_scale = 1.0 / math.sqrt(HEAD_SIZE)
    scores = (
        jnp.einsum(
            "tkgd,skd->kgts", grouped_queries, gathered_keys, preferred_element_type=jnp.float32
        )
        * score_scale
    )
    return (jnp.where(allowed, scores, masked_score), grouped_queries)


def fetch_weights(w_qkv, w_out, w_router, norm_gains, layer_idx):
    return (
        lax.all_gather(w_qkv[layer_idx], ("dp", "expert"), axis=0, tiled=True),
        lax.all_gather(w_out[layer_idx], ("dp", "expert"), axis=0, tiled=True),
        lax.all_gather(w_router[layer_idx], ("dp", "expert"), axis=0, tiled=True),
        lax.all_gather(norm_gains[layer_idx], ("dp", "expert"), axis=1, tiled=True),
    )


def fetch_again(w_qkv, w_out, w_router, norm_gains, layer_idx):
    return (
        lax.all_gather(w_qkv[layer_idx], ("dp", "expert"), axis=0, tiled=True),
        lax.all_gather(w_out[layer_idx], ("dp", "expert"), axis=0, tiled=True),
        lax.all_gather(w_router[layer_idx], ("dp", "expert"), axis=0, tiled=True),
        lax.all_gather(norm_gains[layer_idx], ("dp", "expert"), axis=1, tiled=True),
    )


def local(
    tokens,
    w_qkv,
    w_out,
    w_router,
    norm_gains,
    w_gate,
    w_up,
    w_down,
    out_grad,
    segment_ids,
    routes,
    pair_order,
):
    token_rows = tokens.shape[0]
    layers_n = w_qkv.shape[0]
    topk_n = routes.shape[2]
    n_expert = lax.axis_size("expert")
    expert_here = lax.axis_index("expert")
    device_here = lax.axis_index("dp") * n_expert + expert_here
    local_n = w_gate.shape[1]
    experts_n = local_n * n_expert
    capacity = 9 * n_expert * token_rows * topk_n // (8 * experts_n)
    most_rows = 2 * token_rows * topk_n // experts_n
    query_width = QUERY_HEADS * HEAD_SIZE
    key_width = KEY_VALUE_HEADS * HEAD_SIZE
    pair_n = token_rows * topk_n
    score_scale = 1.0 / math.sqrt(HEAD_SIZE)
    token_positions = expert_here * token_rows + jnp.arange(token_rows, dtype=jnp.int32)
    seg_prev = from_behind(segment_ids, ("dp", "expert"), 1)
    has_prev = device_here > 0
    row_index = jnp.arange(token_rows)
    own_mask = (segment_ids[None, :] == segment_ids[:, None]) & (
        row_index[None, :] <= row_index[:, None]
    )
    prev_mask = (seg_prev[None, :] == segment_ids[:, None]) & has_prev
    allowed = jnp.concatenate([prev_mask, own_mask], axis=1)
    chosen_all = routes.reshape(layers_n, pair_n)
    order_all = pair_order.reshape(layers_n, pair_n)
    rank_all = jax.vmap(local_rank)(chosen_all, order_all)
    counts = jnp.sum(
        (chosen_all[:, :, None] == jnp.arange(experts_n, dtype=jnp.int32)[None, None, :]).astype(
            jnp.int32
        ),
        axis=1,
    )
    all_counts = lax.all_gather(counts[None], "expert", axis=0, tiled=True)
    before = jnp.cumsum(all_counts, axis=0) - all_counts
    mine_before = lax.dynamic_index_in_dim(before, expert_here, 0, keepdims=False)
    seat_all = jnp.take_along_axis(mine_before, chosen_all, axis=1) + rank_all
    kept_all = (seat_all < capacity).astype(jnp.float32)
    columns_all = lax.dynamic_slice_in_dim(all_counts, expert_here * local_n, local_n, 2)
    stream = tokens.astype(jnp.float32)
    saved_layers = []
    outputs = []
    for layer_idx in range(layers_n):
        gathered = fetch_weights(w_qkv, w_out, w_router, norm_gains, layer_idx)
        qkv_full, out_full, router_full, gain_full = gathered
        gain_float = gain_full.astype(jnp.float32)
        normed_a = rms_norm(stream, gain_float[0]).astype(jnp.bfloat16)
        projected_output = jnp.dot(normed_a, qkv_full, preferred_element_type=jnp.float32)
        query_rows = apply_rotary(
            projected_output[:, :query_width].reshape(token_rows, QUERY_HEADS, HEAD_SIZE),
            token_positions,
        ).astype(jnp.bfloat16)
        key_own = apply_rotary(
            projected_output[:, query_width : query_width + key_width].reshape(
                token_rows, KEY_VALUE_HEADS, HEAD_SIZE
            ),
            token_positions,
        ).astype(jnp.bfloat16)
        value_own = (
            projected_output[:, query_width + key_width :]
            .reshape(token_rows, KEY_VALUE_HEADS, HEAD_SIZE)
            .astype(jnp.bfloat16)
        )
        key_prev, value_prev = from_behind((key_own, value_own), ("dp", "expert"), 1)
        gathered_keys = jnp.concatenate([key_prev, key_own], axis=0)
        gathered_values = jnp.concatenate([value_prev, value_own], axis=0)
        scores, grouped_queries = masked_scores(query_rows, gathered_keys, allowed)
        top_score = jnp.max(scores, axis=-1, keepdims=True)
        exp_scores = jnp.exp(scores - top_score)
        row_total = jnp.sum(exp_scores, axis=-1, keepdims=True)
        prob_low = (exp_scores / row_total).astype(jnp.bfloat16)
        log_total = top_score + jnp.log(row_total)
        attended = (
            jnp.einsum(
                "kgts,skd->tkgd", prob_low, gathered_values, preferred_element_type=jnp.float32
            )
            .reshape(token_rows, query_width)
            .astype(jnp.bfloat16)
        )
        mixed_sum = stream + jnp.dot(attended, out_full, preferred_element_type=jnp.float32)
        normed_b = rms_norm(mixed_sum, gain_float[1]).astype(jnp.bfloat16)
        logits = jnp.dot(normed_b, router_full, preferred_element_type=jnp.float32)
        chosen = chosen_all[layer_idx]
        pair_rank = rank_all[layer_idx]
        kept_pair = kept_all[layer_idx]
        chosen_logits = jnp.take_along_axis(logits, chosen.reshape(token_rows, topk_n), axis=1)
        gate_soft = pick_soft(chosen_logits)
        gather_at, take_seat, back_at, give_seat = receive_maps(
            columns_all[:, layer_idx], capacity, most_rows
        )
        outgoing = pack_rows(
            jnp.repeat(normed_b, topk_n, axis=0), chosen, pair_rank, experts_n, most_rows
        )
        arrived = lax.all_to_all(outgoing, "expert", split_axis=0, concat_axis=0, tiled=True)
        expert_in = unpack_rows(arrived, gather_at, take_seat)
        gate_pre = jnp.einsum(
            "lcd,ldf->lcf", expert_in, w_gate[layer_idx], preferred_element_type=jnp.float32
        )
        up_pre = jnp.einsum(
            "lcd,ldf->lcf", expert_in, w_up[layer_idx], preferred_element_type=jnp.float32
        )
        hidden = gated_unit(gate_pre, up_pre).astype(jnp.bfloat16)
        expert_out = jnp.einsum(
            "lcf,lfd->lcd", hidden, w_down[layer_idx], preferred_element_type=jnp.float32
        ).astype(jnp.bfloat16)
        returned = lax.all_to_all(
            repack_rows(expert_out, back_at, give_seat, experts_n),
            "expert",
            split_axis=0,
            concat_axis=0,
            tiled=True,
        )
        pair_out = returned[chosen, pair_rank]
        pair_weight = gate_soft.reshape(pair_n) * kept_pair
        branch = jnp.sum(
            (pair_weight[:, None] * pair_out.astype(jnp.float32)).reshape(token_rows, topk_n, D),
            axis=1,
        )
        new_stream = mixed_sum + branch
        saved_layers.append(
            {
                "stream_in": stream,
                "normed_a": normed_a,
                "queries": query_rows,
                "key_all": gathered_keys,
                "value_all": gathered_values,
                "log_total": log_total,
                "attended": attended,
                "mixed_sum": mixed_sum,
                "normed_b": normed_b,
                "gate_soft": gate_soft,
                "chosen_logits": chosen_logits,
                "expert_in": expert_in,
                "gate_pre": gate_pre,
                "up_pre": up_pre,
                "hidden": hidden,
                "pair_out": pair_out,
                "gather_at": gather_at,
                "take_seat": take_seat,
                "back_at": back_at,
                "give_seat": give_seat,
                "kept_weights": None,
            }
        )
        outputs.append(new_stream)
        stream = new_stream
    grad_stream = out_grad.astype(jnp.float32)
    weight_parts = [None] * layers_n
    expert_parts = [None] * layers_n
    for layer_idx in reversed(range(layers_n)):
        record = saved_layers[layer_idx]
        gathered = fetch_again(w_qkv, w_out, w_router, norm_gains, layer_idx)
        qkv_full, out_full, router_full, gain_full = gathered
        gain_float = gain_full.astype(jnp.float32)
        chosen = chosen_all[layer_idx]
        pair_rank = rank_all[layer_idx]
        kept_pair = kept_all[layer_idx]
        gate_w = w_gate[layer_idx]
        up_w = w_up[layer_idx]
        down_w = w_down[layer_idx]
        grad_branch = jnp.repeat(grad_stream, topk_n, axis=0)
        pair_weight = record["gate_soft"].reshape(pair_n) * kept_pair
        dy_pairs = (pair_weight[:, None] * grad_branch).astype(jnp.bfloat16)
        arrived_grad = lax.all_to_all(
            pack_rows(dy_pairs, chosen, pair_rank, experts_n, most_rows),
            "expert",
            split_axis=0,
            concat_axis=0,
            tiled=True,
        )
        dy_in = unpack_rows(arrived_grad, record["gather_at"], record["take_seat"])
        grad_down_l = jnp.einsum(
            "lcf,lcd->lfd", record["hidden"], dy_in, preferred_element_type=jnp.float32
        )
        dhidden = jnp.einsum("lcd,lfd->lcf", dy_in, down_w, preferred_element_type=jnp.float32)
        unused_value, gate_pull = jax.vjp(gated_unit, record["gate_pre"], record["up_pre"])
        dgate_pre, dup_pre = gate_pull(dhidden)
        dgate_low = dgate_pre.astype(jnp.bfloat16)
        dup_low = dup_pre.astype(jnp.bfloat16)
        grad_gate_l = jnp.einsum(
            "lcd,lcf->ldf", record["expert_in"], dgate_low, preferred_element_type=jnp.float32
        )
        grad_up_l = jnp.einsum(
            "lcd,lcf->ldf", record["expert_in"], dup_low, preferred_element_type=jnp.float32
        )
        dexpert_in = (
            jnp.einsum("lcf,ldf->lcd", dgate_low, gate_w, preferred_element_type=jnp.float32)
            + jnp.einsum("lcf,ldf->lcd", dup_low, up_w, preferred_element_type=jnp.float32)
        ).astype(jnp.bfloat16)
        returned_grad = lax.all_to_all(
            repack_rows(dexpert_in, record["back_at"], record["give_seat"], experts_n),
            "expert",
            split_axis=0,
            concat_axis=0,
            tiled=True,
        )
        dpair_in = returned_grad[chosen, pair_rank].astype(jnp.float32) * kept_pair[:, None]
        dnormed_b = jnp.sum(dpair_in.reshape(token_rows, topk_n, D), axis=1)
        dgates = (
            jnp.sum(grad_branch * record["pair_out"].astype(jnp.float32), axis=1) * kept_pair
        ).reshape(token_rows, topk_n)
        unused_soft, soft_pull = jax.vjp(pick_soft, record["chosen_logits"])
        dchosen = soft_pull(dgates)[0]
        onehot_route = (
            chosen.reshape(token_rows, topk_n)[:, :, None]
            == jnp.arange(experts_n, dtype=jnp.int32)[None, None, :]
        ).astype(jnp.float32)
        dlogits = jnp.sum(onehot_route * dchosen[:, :, None], axis=1).astype(jnp.bfloat16)
        grad_router_l = jnp.einsum(
            "td,te->de", record["normed_b"], dlogits, preferred_element_type=jnp.float32
        )
        dnormed_b = dnormed_b + jnp.einsum(
            "te,de->td", dlogits, router_full, preferred_element_type=jnp.float32
        )
        unused_norm, norm_pull = jax.vjp(rms_norm, record["mixed_sum"], gain_float[1])
        dmixed_part, dgain_b = norm_pull(dnormed_b)
        dmixed = grad_stream + dmixed_part
        grad_attn = dmixed.astype(jnp.bfloat16)
        grad_out_l = jnp.einsum(
            "tq,td->qd", record["attended"], grad_attn, preferred_element_type=jnp.float32
        )
        attended_gradient = jnp.einsum(
            "td,qd->tq", grad_attn, out_full, preferred_element_type=jnp.float32
        ).astype(jnp.bfloat16)
        gathered_keys = record["key_all"]
        gathered_values = record["value_all"]
        scores, grouped_queries = masked_scores(record["queries"], gathered_keys, allowed)
        prob_float = jnp.exp(scores - record["log_total"])
        prob_low = prob_float.astype(jnp.bfloat16)
        grouped_gradient = attended_gradient.reshape(
            token_rows, KEY_VALUE_HEADS, QUERY_HEADS // KEY_VALUE_HEADS, HEAD_SIZE
        )
        dvalue_all = jnp.einsum(
            "kgts,tkgd->skd", prob_low, grouped_gradient, preferred_element_type=jnp.float32
        )
        dprobs = jnp.einsum(
            "tkgd,skd->kgts", grouped_gradient, gathered_values, preferred_element_type=jnp.float32
        )
        delta_row = jnp.sum(prob_float * dprobs, axis=-1, keepdims=True)
        dscores = (prob_float * (dprobs - delta_row)).astype(jnp.bfloat16)
        dqueries = (
            jnp.einsum(
                "kgts,skd->tkgd", dscores, gathered_keys, preferred_element_type=jnp.float32
            ).reshape(token_rows, QUERY_HEADS, HEAD_SIZE)
            * score_scale
        )
        dkey_all = (
            jnp.einsum(
                "kgts,tkgd->skd", dscores, grouped_queries, preferred_element_type=jnp.float32
            )
            * score_scale
        )
        dkey_next, dvalue_next = (
            from_behind(dkey_all[:token_rows].astype(jnp.bfloat16), ("dp", "expert"), -1).astype(
                jnp.float32
            ),
            from_behind(dvalue_all[:token_rows].astype(jnp.bfloat16), ("dp", "expert"), -1).astype(
                jnp.float32
            ),
        )
        dkey_own = dkey_all[token_rows:] + dkey_next
        dvalue_own = dvalue_all[token_rows:] + dvalue_next
        unused_query, query_pull = jax.vjp(
            partial(apply_rotary, token_positions=token_positions), dqueries
        )
        dq_raw = query_pull(dqueries)[0]
        unused_key, key_pull = jax.vjp(
            partial(apply_rotary, token_positions=token_positions), dkey_own
        )
        dk_raw = key_pull(dkey_own)[0]
        dprojected = jnp.concatenate(
            [
                dq_raw.reshape(token_rows, query_width),
                dk_raw.reshape(token_rows, key_width),
                dvalue_own.reshape(token_rows, key_width),
            ],
            axis=1,
        ).astype(jnp.bfloat16)
        grad_qkv_l = jnp.einsum(
            "td,tq->dq", record["normed_a"], dprojected, preferred_element_type=jnp.float32
        )
        dnormed_a = jnp.einsum(
            "tq,dq->td", dprojected, qkv_full, preferred_element_type=jnp.float32
        )
        unused_first, first_pull = jax.vjp(rms_norm, record["stream_in"], gain_float[0])
        dstream_part, dgain_a = first_pull(dnormed_a)
        grad_stream = dmixed + dstream_part
        dgains_l = jnp.stack([dgain_a, dgain_b])
        weight_parts[layer_idx] = (
            lax.psum_scatter(grad_qkv_l, ("dp", "expert"), scatter_dimension=0, tiled=True),
            lax.psum_scatter(grad_out_l, ("dp", "expert"), scatter_dimension=0, tiled=True),
            lax.psum_scatter(grad_router_l, ("dp", "expert"), scatter_dimension=0, tiled=True),
            lax.psum_scatter(dgains_l, ("dp", "expert"), scatter_dimension=1, tiled=True),
        )
        expert_parts[layer_idx] = (
            lax.psum_scatter(
                grad_gate_l.astype(jnp.bfloat16), "dp", scatter_dimension=1, tiled=True
            ).astype(jnp.float32),
            lax.psum_scatter(
                grad_up_l.astype(jnp.bfloat16), "dp", scatter_dimension=1, tiled=True
            ).astype(jnp.float32),
            lax.psum_scatter(
                grad_down_l.astype(jnp.bfloat16), "dp", scatter_dimension=2, tiled=True
            ).astype(jnp.float32),
        )
    stacked_weight = [
        jnp.stack([weight_parts[layer_idx][member] for layer_idx in range(layers_n)])
        for member in range(4)
    ]
    stacked_expert = [
        jnp.stack([expert_parts[layer_idx][member] for layer_idx in range(layers_n)])
        for member in range(3)
    ]
    grad_qkv, grad_out, grad_router, grad_gains = stacked_weight
    grad_gate, grad_up, grad_down = stacked_expert
    layer_outs = jnp.stack(outputs).astype(jnp.bfloat16)
    return (
        layer_outs,
        grad_stream,
        grad_qkv,
        grad_out,
        grad_router,
        grad_gains,
        grad_gate,
        grad_up,
        grad_down,
    )


def solution(mesh):
    return jax.shard_map(
        local,
        mesh=mesh,
        in_specs=(
            P(("dp", "expert"), None),
            P(None, ("dp", "expert"), None),
            P(None, ("dp", "expert"), None),
            P(None, ("dp", "expert"), None),
            P(None, None, ("dp", "expert")),
            P(None, "expert", None, None),
            P(None, "expert", None, None),
            P(None, "expert", None, None),
            P(("dp", "expert"), None),
            P(("dp", "expert")),
            P(None, ("dp", "expert"), None),
            P(None, ("dp", "expert"), None),
        ),
        out_specs=(
            P(None, ("dp", "expert"), None),
            P(("dp", "expert"), None),
            P(None, ("dp", "expert"), None),
            P(None, ("dp", "expert"), None),
            P(None, ("dp", "expert"), None),
            P(None, None, ("dp", "expert")),
            P(None, "expert", "dp", None),
            P(None, "expert", "dp", None),
            P(None, "expert", None, "dp"),
        ),
        check_vma=False,
    )
```

profile of v0, /device:TPU:8, one launch (start us, length us, event | category | flops | bytes accessed | tf_op | source)
XLA Modules:
  0.0 2677.1 jit_solution(1722476474257557160)
XLA Ops:
  14.2 38.8 %all-gather = bf16[1,2,1536]{1,0,2:T(2,128)(2,1)S(1)} all-gather(bf16[1,2,48]{1,0,2:T(2,128)(2,1)S(1)} %copy.403), channel_id=2, replica_groups=mesh['dp'=4,'expert'=8] {'dp','expert'}, dimensions={2}, use_global_device_ids=true | all-gather | bytes 6336 | tf_op jit(solution)/shard_map/all_gather | solution.py:120
  56.9 25.1 slice_reduce_fusion.2
  100.5 49.4 %all-gather.17.cloned.1.call-done = bf16[1,1536,1536]{2,1,0:T(8,128)(2,1)} async-done(((bf16[1,48,1536]{2,1,0:T(8,128)(2,1)}), bf16[1,1536,1536]{2,1,0:T(8,128)(2,1)}) %all-gather.17.cloned.1.call-update) | async-done | bytes 4718608 | tf_op jit(solution)/shard_map/all_gather | solution.py:118
  157.7 79.5 %scatter_fusion = bf16[16,64,1536]{2,1,0:T(8,128)(2,1)} fusion(bf16[16,64,1536]{2,1,0:T(8,128)(2,1)} %broadcast.504.clone, s32[512]{0:T(512)S(1)} %bitcast.374, bf16[512,1536]{1,0:T(8,128)(2,1)S(1)} %reshape.898), kind=kCustom, calls=%fused_computation.17 | custom fusion | bytes 4722688 | tf_op jit(solution)/shard_map/scatter | solution.py:86
  241.5 43.3 %all-gather.9 = s32[8,2,16]{2,1,0:T(2,128)S(1)} all-gather(s32[1,2,16]{2,1,0:T(2,128)S(1)} %bitcast.470), channel_id=6, replica_groups=mesh['dp'=4,'expert'=8] {'expert'}, dimensions={0}, use_global_device_ids=true | all-gather | bytes 1152 | tf_op jit(solution)/shard_map/all_gather | solution.py:179
  286.6 5.2 gather_fusion.14
  302.3 6.1 multiply_convert_fusion.5
  310.1 5.6 gather_fusion.1
  324.1 66.5 %all-gather.3 = bf16[1,1536,16]{2,0,1:T(2,128)(2,1)} all-gather(bf16[1,48,16]{2,0,1:T(2,128)(2,1)S(1)} %copy.406), channel_id=5, replica_groups=mesh['dp'=4,'expert'=8] {'dp','expert'}, dimensions={1}, use_global_device_ids=true | all-gather | bytes 50688 | tf_op jit(solution)/shard_map/all_gather | solution.py:119
  394.1 9.0 gather_fusion.12
  405.2 37.5 %all-gather.5 = bf16[1,2,1536]{1,0,2:T(2,128)(2,1)S(1)} all-gather(bf16[1,2,48]{1,0,2:T(2,128)(2,1)} %copy.407), channel_id=7, replica_groups=mesh['dp'=4,'expert'=8] {'dp','expert'}, dimensions={2}, use_global_device_ids=true | all-gather | bytes 6336 | tf_op jit(solution)/shard_map/all_gather | solution.py:120
  443.8 25.1 slice_reduce_fusion
  476.0 9.7 gather_fusion.2
  520.4 79.3 %scatter_fusion.1 = bf16[16,64,1536]{2,1,0:T(8,128)(2,1)} fusion(bf16[16,64,1536]{2,1,0:T(8,128)(2,1)} %broadcast.504.clone.2, s32[512]{0:T(512)S(1)} %bitcast.378, bf16[512,1536]{1,0:T(8,128)(2,1)S(1)} %reshape.904), kind=kCustom, calls=%fused_computation.18 | custom fusion | bytes 4722688 | tf_op jit(solution)/shard_map/scatter | solution.py:86
  603.6 69.4 %all-gather.8 = bf16[1,1536,16]{2,0,1:T(2,128)(2,1)} all-gather(bf16[1,48,16]{2,0,1:T(2,128)(2,1)S(1)} %copy.410), channel_id=10, replica_groups=mesh['dp'=4,'expert'=8] {'dp','expert'}, dimensions={1}, use_global_device_ids=true | all-gather | bytes 50688 | tf_op jit(solution)/shard_map/all_gather | solution.py:119
  678.4 4.9 reshape.753
  694.8 81.0 %scatter_fusion.2 = bf16[16,64,1536]{2,1,0:T(8,128)(2,1)} fusion(bf16[16,64,1536]{2,1,0:T(8,128)(2,1)} %broadcast.504.clone.1, s32[512]{0:T(512)S(1)} %bitcast.379, bf16[512,1536]{1,0:T(8,128)(2,1)} %multiply_convert_fusion.1), kind=kCustom, calls=%fused_computation.19 | custom fusion | bytes 4722688 | tf_op jit(solution)/shard_map/scatter | solution.py:86
  780.7 5.2 gather_fusion.16
  791.5 26.9 %all-to-all-done.4 = bf16[16,64,1536]{2,1,0:T(8,128)(2,1)} async-done(((bf16[16,64,1536]{2,1,0:T(8,128)(2,1)}), bf16[16,64,1536]{2,1,0:T(8,128)(2,1)}, u32[]{:S(2)}, u32[]{:S(2)}) %all-to-all-start.4) | async-done | bytes 3145760 | tf_op jit(solution)/shard_map/all_to_all | solution.py:309
  818.4 7.7 gather_fusion.6
  845.5 5.6 gather_fusion.7
  851.1 5.5 gather_fusion.4
  860.9 41.1 %all_to_all.40 = bf16[16,64,1536]{2,1,0:T(8,128)(2,1)} all-to-all(bf16[16,64,1536]{2,1,0:T(8,128)(2,1)S(1)} %get-tuple-element.91), channel_id=1, replica_groups=mesh['dp'=4,'expert'=8] {'expert'}, dimensions={0} | all-to-all | bytes 6291456 | tf_op jit(solution)/shard_map/all_to_all | solution.py:251
  906.5 11.9 gather_fusion.5
  925.9 18.1 all-to-all-done.5
  944.0 9.7 gather_fusion.8
  968.7 7.9 collective-permute-start.5
  981.3 5.1 multiply_reduce_fusion.7
  989.8 5.1 reshape.761
  999.6 57.9 %scatter_fusion.3 = bf16[16,64,1536]{2,1,0:T(8,128)(2,1)S(1)} fusion(bf16[16,64,1536]{2,1,0:T(8,128)(2,1)S(1)} %broadcast.504, s32[512]{0:T(512)S(1)} %bitcast.375, bf16[512,1536]{1,0:T(8,128)(2,1)} %get-tuple-element.49), kind=kCustom, calls=%fused_computation.20 | custom fusion | bytes 4722688 | tf_op jit(solution)/shard_map/scatter | solution.py:86
  1057.6 41.1 %all_to_all.41 = bf16[16,64,1536]{2,1,0:T(8,128)(2,1)} all-to-all(bf16[16,64,1536]{2,1,0:T(8,128)(2,1)S(1)} %scatter_fusion.3), channel_id=1, replica_groups=mesh['dp'=4,'expert'=8] {'expert'}, dimensions={0} | all-to-all | bytes 6291456 | tf_op jit(solution)/shard_map/all_to_all | solution.py:309
  1098.6 7.6 gather_fusion.9
  1106.2 6.0 fusion.79
  1120.9 5.6 gather_fusion.10
  1147.2 24.7 all-to-all-done.7
  1171.9 9.9 gather_fusion.11
  1205.4 5.6 fusion.111
  1212.8 6.7 convolution_convert_fusion
  1219.4 12.4 copy.398
  1231.9 5.5 copy.413
  1238.0 6.6 convolution_convert_fusion.1
  1244.7 12.5 copy.396
  1257.1 5.4 copy.412
  1262.6 6.6 convolution_convert_fusion.2
  1269.5 6.7 convolution_convert_fusion.3
  1276.2 6.6 convolution_convert_fusion.4
  1283.0 6.6 convolution_convert_fusion.5
  1290.8 5.0 fusion.128
  1296.8 4.9 fusion.125
  1302.9 7.3 fusion.124
  1311.1 6.5 fusion.123
  1320.5 14.3 reduce-scatter.45.cloned.1.call-done
  1335.6 98.9 %reduce-scatter.43.cloned.1.call-done = f32[48,16]{1,0:T(8,128)} async-done(((f32[1536,16]{1,0:T(8,128)}), f32[48,16]{1,0:T(8,128)}) %reduce-scatter.43.cloned.1.call-update) | async-done | bytes 3088
  1437.0 97.7 %reduce-scatter.47.cloned.1.call-done = f32[48,2]{1,0:T(8,128)} async-done(((f32[1536,2]{1,0:T(8,128)}), f32[48,2]{1,0:T(8,128)}) %reduce-scatter.47.cloned.1.call-update) | async-done | bytes 400
  1536.2 86.0 %reduce-scatter.53.cloned.1.call-done = bf16[384,1536]{1,0:T(8,128)(2,1)} async-done(((bf16[1536,1536]{1,0:T(8,128)(2,1)}), bf16[384,1536]{1,0:T(8,128)(2,1)}) %reduce-scatter.53.cloned.1.call-update) | async-done | bytes 1179664
  1627.0 83.0 %reduce-scatter.51.cloned.1.call-done = bf16[384,1536]{1,0:T(8,128)(2,1)} async-done(((bf16[1536,1536]{1,0:T(8,128)(2,1)}), bf16[384,1536]{1,0:T(8,128)(2,1)}) %reduce-scatter.51.cloned.1.call-update) | async-done | bytes 1179664
  1717.5 81.3 %reduce-scatter.41.cloned.1.call-done = bf16[2,384,768]{2,1,0:T(8,128)(2,1)} async-done(((bf16[2,1536,768]{2,1,0:T(8,128)(2,1)}), bf16[2,384,768]{2,1,0:T(8,128)(2,1)}) %reduce-scatter.41.cloned.1.call-update) | async-done | bytes 1179664 | tf_op jit(solution)/shard_map/reduce_scatter | solution.py:444
  1798.8 88.0 %reduce-scatter.39.cloned.1.call-done = bf16[2,384,768]{2,1,0:T(8,128)(2,1)} async-done(((bf16[2,1536,768]{2,1,0:T(8,128)(2,1)}), bf16[2,384,768]{2,1,0:T(8,128)(2,1)}) %reduce-scatter.39.cloned.1.call-update) | async-done | bytes 1179664 | tf_op jit(solution)/shard_map/reduce_scatter | solution.py:444
  1890.9 84.6 %reduce-scatter.37.cloned.1.call-done = bf16[2,384,768]{2,1,0:T(8,128)(2,1)} async-done(((bf16[2,1536,768]{2,1,0:T(8,128)(2,1)}), bf16[2,384,768]{2,1,0:T(8,128)(2,1)}) %reduce-scatter.37.cloned.1.call-update) | async-done | bytes 1179664 | tf_op jit(solution)/shard_map/reduce_scatter | solution.py:441
  1975.4 88.0 %reduce-scatter.35.cloned.1.call-done = bf16[2,384,768]{2,1,0:T(8,128)(2,1)} async-done(((bf16[2,1536,768]{2,1,0:T(8,128)(2,1)}), bf16[2,384,768]{2,1,0:T(8,128)(2,1)}) %reduce-scatter.35.cloned.1.call-update) | async-done | bytes 1179664 | tf_op jit(solution)/shard_map/reduce_scatter | solution.py:441
  2067.5 137.5 %reduce-scatter.33.cloned.1.call-done = f32[48,1536]{1,0:T(8,128)} async-done(((f32[1536,1536]{1,0:T(8,128)}), f32[48,1536]{1,0:T(8,128)}) %reduce-scatter.33.cloned.1.call-update) | async-done | bytes 294928 | tf_op jit(solution)/shard_map/reduce_scatter | solution.py:436
  2205.0 141.4 %reduce-scatter.31.cloned.1.call-done = f32[48,1536]{1,0:T(8,128)} async-done(((f32[1536,1536]{1,0:T(8,128)}), f32[48,1536]{1,0:T(8,128)}) %reduce-scatter.31.cloned.1.call-update) | async-done | bytes 294928 | tf_op jit(solution)/shard_map/reduce_scatter | solution.py:436
  2348.3 158.2 %reduce-scatter.29.cloned.1.call-done = f32[48,2048]{1,0:T(8,128)} async-done(((f32[1536,2048]{1,0:T(8,128)}), f32[48,2048]{1,0:T(8,128)}) %reduce-scatter.29.cloned.1.call-update) | async-done | bytes 393232 | tf_op jit(solution)/shard_map/reduce_scatter | solution.py:435
  2506.5 161.4 %reduce-scatter.27.cloned.1.call-done = f32[48,2048]{1,0:T(8,128)} async-done(((f32[1536,2048]{1,0:T(8,128)}), f32[48,2048]{1,0:T(8,128)}) %reduce-scatter.27.cloned.1.call-update) | async-done | bytes 393232 | tf_op jit(solution)/shard_map/reduce_scatter | solution.py:435
  (718 shorter events, 296.2 us)
Async XLA Ops:
  7.2 76.6 %all-gather.15.cloned.1.call-start = ((), (), s32[]{:S(2)}) async-start(), calls=%async_computation.30 | async-start | bytes 6488064 | tf_op jit(solution)/shard_map/all_gather | solution.py:117
  9.1 45.1 %copy-start.155 = (s32[2,128,4]{1,2,0:T(4,128)S(1)}, s32[2,128,4]{1,2,0:T(4,128)}, u32[]{:S(2)}) copy-start(s32[2,128,4]{1,2,0:T(4,128)} %param.26) | copy-start | bytes 12292
  9.1 45.4 %copy-start.156 = (s32[2,1,512]{2,1,0:T(1,128)S(1)}, s32[2,1,512]{2,1,0:T(1,128)}, u32[]{:S(2)}) copy-start(s32[2,1,512]{2,1,0:T(1,128)} %param.27) | copy-start | bytes 12292
  9.1 140.8 %all-gather.17.cloned.1.call-start = ((), (), s32[]{:S(2)}) async-start(), calls=%async_computation.31 | async-start | bytes 4866048 | tf_op jit(solution)/shard_map/all_gather | solution.py:118
  10.9 481.6 %all-gather.19.cloned.1.call-start = ((), (), s32[]{:S(2)}) async-start(), calls=%async_computation.32 | async-start | bytes 6488064 | tf_op jit(solution)/shard_map/all_gather | solution.py:117
  10.9 44.5 %copy-start.21 = (bf16[128,1536]{1,0:T(8,128)(2,1)S(1)}, bf16[128,1536]{1,0:T(8,128)(2,1)}, u32[]{:S(2)}) copy-start(bf16[128,1536]{1,0:T(8,128)(2,1)} %param.16) | copy-start | bytes 1179652
  11.6 70.5 %collective-permute-start.1 = (s32[128]{0:T(128)S(1)}, s32[128]{0:T(128)S(1)}, u32[]{:S(2)}, u32[]{:S(2)}) collective-permute-start(s32[128]{0:T(128)S(1)} %copy-done.157), channel_id=1, source_target_pairs={{0,1},{1,2},{2,3},{3,4},{4,5},{5,6},{6,7},{7,8},{8,9},{9,10},{10,1... | collective-permute-start | bytes 1544 | tf_op jit(solution)/shard_map/ppermute | solution.py:23
  54.1 37.6 %copy-start.66 = (f32[128,64]{0,1:T(8,128)}, f32[128,64]{0,1:T(8,128)S(1)}, u32[]{:S(2)}) copy-start(f32[128,64]{0,1:T(8,128)S(1)} %get-tuple-element.95) | copy-start | bytes 98308
  54.1 447.1 %copy-start.63 = (f32[128,64]{0,1:T(8,128)}, f32[128,64]{0,1:T(8,128)S(1)}, u32[]{:S(2)}) copy-start(f32[128,64]{0,1:T(8,128)S(1)} %get-tuple-element.94) | copy-start | bytes 98308
  54.2 442.6 %copy-start.54 = (f32[128,64]{1,0:T(8,128)}, f32[128,64]{1,0:T(8,128)S(1)}, u32[]{:S(2)}) copy-start(f32[128,64]{1,0:T(8,128)S(1)} %copy.299) | copy-start | bytes 98308
  56.3 31.4 %copy-start.140 = (f32[128]{0:T(128)}, f32[128]{0:T(128)S(1)}, u32[]{:S(2)}) copy-start(f32[128]{0:T(128)S(1)} %fusion.166) | copy-start | bytes 1540
  56.9 100.8 %copy-start.2 = (s32[512,1]{0,1:T(1,128)}, s32[512,1]{0,1:T(1,128)S(1)}, u32[]{:S(2)}) copy-start(s32[512,1]{0,1:T(1,128)S(1)} %get-tuple-element.88) | copy-start | bytes 6148
  56.9 419.1 %copy-start = (s32[512,1]{0,1:T(1,128)}, s32[512,1]{0,1:T(1,128)S(1)}, u32[]{:S(2)}) copy-start(s32[512,1]{0,1:T(1,128)S(1)} %get-tuple-element.89) | copy-start | bytes 6148
  82.0 71.2 %copy-start.107 = (f32[1536]{0:T(1024)}, f32[1536]{0:T(1024)S(1)}, u32[]{:S(2)}) copy-start(f32[1536]{0:T(1024)S(1)} %get-tuple-element.21) | copy-start | bytes 18436
  82.1 414.7 %copy-start.57 = (f32[128,64]{1,0:T(8,128)}, f32[128,64]{1,0:T(8,128)S(1)}, u32[]{:S(2)}) copy-start(f32[128,64]{1,0:T(8,128)S(1)} %copy.301) | copy-start | bytes 98308
  82.3 14.2 copy-start.86
  88.8 7.7 collective-permute-start.2
  92.5 7.4 collective-permute-start
  100.5 52.6 %copy-start.39 = (bf16[2,128,6,128]{3,1,2,0:T(8,128)(2,1)}, bf16[2,128,6,128]{3,1,2,0:T(8,128)(2,1)S(1)}, u32[]{:S(2)}) copy-start(bf16[2,128,6,128]{3,1,2,0:T(8,128)(2,1)S(1)} %convolution_convert_fusion.7) | copy-start | bytes 1179652
  237.2 56.8 %all-to-all-start = ((bf16[16,64,1536]{2,1,0:T(8,128)(2,1)}), bf16[16,64,1536]{2,1,0:T(8,128)(2,1)S(1)}, u32[]{:S(2)}, u32[]{:S(2)}) async-start(bf16[16,64,1536]{2,1,0:T(8,128)(2,1)} %scatter_fusion), calls=%async_computation | async-start | bytes 6291456 | tf_op jit(solution)/shard_map/all_to_all | solution.py:239
  240.8 271.6 %all-gather.21.cloned.1.call-start = ((), (), s32[]{:S(2)}) async-start(), calls=%async_computation.33 | async-start | bytes 4866048 | tf_op jit(solution)/shard_map/all_gather | solution.py:118
  294.0 21.7 copy-start.129
  294.0 16.1 copy-start.112
  319.5 156.5 %all-to-all-start.1 = ((bf16[16,64,1536]{2,1,0:T(8,128)(2,1)}), bf16[16,64,1536]{2,1,0:T(8,128)(2,1)S(1)}, u32[]{:S(2)}, u32[]{:S(2)}) async-start(bf16[16,64,1536]{2,1,0:T(8,128)(2,1)} %broadcast_select_fusion.3), calls=%async_computation.1 | async-start | bytes 6291456 | tf_op jit(solution)/shard_map/all_to_all | solution.py:251
  404.5 70.3 %copy-start.47 = (f32[128,4]{1,0:T(8,128)}, f32[128,4]{1,0:T(8,128)S(1)}, u32[]{:S(2)}) copy-start(f32[128,4]{1,0:T(8,128)S(1)} %squeeze.95) | copy-start | bytes 6148
  442.8 26.2 copy-start.26
  442.8 26.2 copy-start.82
  468.9 46.9 %copy-start.109 = (f32[1536]{0:T(1024)}, f32[1536]{0:T(1024)S(1)}, u32[]{:S(2)}) copy-start(f32[1536]{0:T(1024)S(1)} %get-tuple-element.19) | copy-start | bytes 18436
  492.3 20.1 copy-start.5
  497.7 9.4 collective-permute-start.4
  503.1 8.7 collective-permute-start.3
  599.7 75.4 %copy-start.103 = (s32[128,4,1]{1,0,2:T(8,128)S(1)}, s32[128,4,1]{1,0,2:T(8,128)}, u32[]{:S(2)}) copy-start(s32[128,4,1]{1,0,2:T(8,128)} %get-tuple-element.76) | copy-start | bytes 6148
  599.7 75.5 %copy-start.145 = (f32[512]{0:T(512)S(1)}, f32[512]{0:T(512)}, u32[]{:S(2)}) copy-start(f32[512]{0:T(512)} %get-tuple-element.23) | copy-start | bytes 6148
  599.7 176.1 %all-to-all-start.2 = ((bf16[16,64,1536]{2,1,0:T(8,128)(2,1)}), bf16[16,64,1536]{2,1,0:T(8,128)(2,1)S(1)}, u32[]{:S(2)}, u32[]{:S(2)}) async-start(bf16[16,64,1536]{2,1,0:T(8,128)(2,1)} %scatter_fusion.1), calls=%async_computation.2 | async-start | bytes 6291456 | tf_op jit(solution)/shard_map/all_to_all | solution.py:239
  675.3 13.4 copy-start.49
  775.8 42.6 %all-to-all-start.4 = ((bf16[16,64,1536]{2,1,0:T(8,128)(2,1)}), bf16[16,64,1536]{2,1,0:T(8,128)(2,1)}, u32[]{:S(2)}, u32[]{:S(2)}) async-start(bf16[16,64,1536]{2,1,0:T(8,128)(2,1)} %scatter_fusion.2), calls=%async_computation.4 | async-start | bytes 6291456 | tf_op jit(solution)/shard_map/all_to_all | solution.py:309
  830.7 11.6 slice-start.8
  902.0 42.0 %all-to-all-start.5 = ((bf16[16,64,1536]{2,1,0:T(8,128)(2,1)}), bf16[16,64,1536]{2,1,0:T(8,128)(2,1)S(1)}, u32[]{:S(2)}, u32[]{:S(2)}) async-start(bf16[16,64,1536]{2,1,0:T(8,128)(2,1)} %get-tuple-element.90), calls=%async_computation.5 | async-start | bytes 6291456 | tf_op jit(solution)/shard_map/all_to_all | solution.py:335
  963.1 23.4 copy-start.19
  968.7 12.6 copy-start.6
  968.7 12.6 copy-start.135
  968.7 10.7 collective-permute-start.5
  976.7 4.6 collective-permute-start.6
  1057.6 41.1 %copy-start.128 = (s32[1024]{0:T(1024)S(1)}, s32[1024]{0:T(1024)}, u32[]{:S(2)}) copy-start(s32[1024]{0:T(1024)} %copy-done.127) | copy-start | bytes 12292
  1130.3 41.6 %all-to-all-start.7 = ((bf16[16,64,1536]{2,1,0:T(8,128)(2,1)}), bf16[16,64,1536]{2,1,0:T(8,128)(2,1)S(1)}, u32[]{:S(2)}, u32[]{:S(2)}) async-start(bf16[16,64,1536]{2,1,0:T(8,128)(2,1)} %broadcast_select_fusion.2), calls=%async_computation.7 | async-start | bytes 6291456 | tf_op jit(solution)/shard_map/all_to_all | solution.py:335
  1134.1 185.6 %reduce-scatter.49.cloned.1.call-start = ((), (), s32[]{:S(2)}) async-start(), calls=%async_computation.37 | async-start | bytes 811008
  1137.2 197.6 %reduce-scatter.45.cloned.1.call-start = ((), (), s32[]{:S(2)}) async-start(), calls=%async_computation.35 | async-start | bytes 811008
  1139.5 32.4 %copy-start.1 = (s32[512,1]{0,1:T(1,128)S(1)}, s32[512,1]{0,1:T(1,128)}, u32[]{:S(2)}) copy-start(s32[512,1]{0,1:T(1,128)} %copy-done) | copy-start | bytes 6148
  1139.5 295.0 %reduce-scatter.43.cloned.1.call-start = ((), (), s32[]{:S(2)}) async-start(), calls=%async_computation.34 | async-start | bytes 811008
  1147.2 387.6 %reduce-scatter.47.cloned.1.call-start = ((), (), s32[]{:S(2)}) async-start(), calls=%async_computation.36 | async-start | bytes 811008
  1197.3 6.2 collective-permute-start.7
  1200.8 4.5 collective-permute-start.8
  1212.3 409.8 %reduce-scatter.53.cloned.1.call-start = ((), (), s32[]{:S(2)}) async-start(), calls=%async_computation.39 | async-start | bytes 5898240
  1237.4 472.7 %reduce-scatter.51.cloned.1.call-start = ((), (), s32[]{:S(2)}) async-start(), calls=%async_computation.38 | async-start | bytes 5898240
  1262.6 536.2 %reduce-scatter.41.cloned.1.call-start = ((), (), s32[]{:S(2)}) async-start(), calls=%async_computation.29 | async-start | bytes 5898240 | tf_op jit(solution)/shard_map/reduce_scatter | solution.py:444
  1269.3 617.5 %reduce-scatter.39.cloned.1.call-start = ((), (), s32[]{:S(2)}) async-start(), calls=%async_computation.28 | async-start | bytes 5898240 | tf_op jit(solution)/shard_map/reduce_scatter | solution.py:444
  1276.2 699.2 %reduce-scatter.37.cloned.1.call-start = ((), (), s32[]{:S(2)}) async-start(), calls=%async_computation.27 | async-start | bytes 5898240 | tf_op jit(solution)/shard_map/reduce_scatter | solution.py:441
  1282.9 780.5 %reduce-scatter.35.cloned.1.call-start = ((), (), s32[]{:S(2)}) async-start(), calls=%async_computation.26 | async-start | bytes 5898240 | tf_op jit(solution)/shard_map/reduce_scatter | solution.py:441
  1289.6 915.4 %reduce-scatter.33.cloned.1.call-start = ((), (), s32[]{:S(2)}) async-start(), calls=%async_computation.25 | async-start | bytes 9732096 | tf_op jit(solution)/shard_map/reduce_scatter | solution.py:436
  1295.8 1050.6 %reduce-scatter.31.cloned.1.call-start = ((), (), s32[]{:S(2)}) async-start(), calls=%async_computation.24 | async-start | bytes 9732096 | tf_op jit(solution)/shard_map/reduce_scatter | solution.py:436
  1301.7 1204.8 %reduce-scatter.29.cloned.1.call-start = ((), (), s32[]{:S(2)}) async-start(), calls=%async_computation.23 | async-start | bytes 12976128 | tf_op jit(solution)/shard_map/reduce_scatter | solution.py:435
  1310.3 1357.7 %reduce-scatter.27.cloned.1.call-start = ((), (), s32[]{:S(2)}) async-start(), calls=%async_computation.22 | async-start | bytes 12976128 | tf_op jit(solution)/shard_map/reduce_scatter | solution.py:435
  1317.6 118.3 %copy-start.166 = (f32[128]{0:T(128)S(1)}, f32[128]{0:T(128)}, u32[]{:S(2)}) copy-start(f32[128]{0:T(128)} %copy-done.165) | copy-start | bytes 1540
  1317.6 118.3 %copy-start.173 = (f32[128]{0:T(128)S(1)}, f32[128]{0:T(128)}, u32[]{:S(2)}) copy-start(f32[128]{0:T(128)} %get-tuple-element.18) | copy-start | bytes 1540
  (159 other events, 639.6 us)
Sparse Core Ops, SparseCore 0:
  11.5 72.3 all-gather.14
  87.3 62.5 all-gather.16
  153.3 67.9 all-gather.18
  244.8 68.4 all-gather.20
  1139.7 95.4 reduce-scatter.48
  1240.2 94.5 reduce-scatter.44
  1339.9 94.5 reduce-scatter.42
  1440.2 94.5 reduce-scatter.46
  1537.6 84.4 reduce-scatter.52
  1624.3 85.7 reduce-scatter.50
  1713.0 85.7 reduce-scatter.40
  1800.9 85.7 reduce-scatter.38
  1889.6 85.7 reduce-scatter.36
  1977.6 85.7 reduce-scatter.34
  2069.1 135.8 reduce-scatter.32
  2211.8 134.5 reduce-scatter.30
  2352.3 154.2 reduce-scatter.28
  2513.4 154.4 reduce-scatter.26
where the time goes:
time: 2700 us; the launch traced here: 2680 us
  waiting for transfers between devices  1450 us (54%)
  local copies, waits for them, and re-layouts  589 us (22%)
  blocking collectives  338 us (13%)
  matrix products  153 us (6%)
  other arithmetic  71.8 us (3%)
  starting transfers between devices  55.5 us (2%)
    unnamed x24, waiting for transfers between devices  381 us
    reduce_scatter x2, waiting for transfers between devices, local(): lax.psum_scatter(grad_qkv_l, ('dp', 'expert'), scatter_dimension=0, tiled...  320 us
    scatter x4, local copies, waits for them, and re-layouts, pack_rows(): return buffer.at[chosen, pair_rank].set(row_values)  298 us
    reduce_scatter x2, waiting for transfers between devices, local(): lax.psum_scatter(grad_out_l, ('dp', 'expert'), scatter_dimension=0, tiled...  279 us
    reduce_scatter x2, waiting for transfers between devices, local(): lax.psum_scatter(grad_gate_l.astype(jnp.bfloat16), 'dp', scatter_dimensio...  173 us
    reduce_scatter x2, waiting for transfers between devices, local(): lax.psum_scatter(grad_up_l.astype(jnp.bfloat16), 'dp', scatter_dimension=...  169 us
    all_gather x2, blocking collectives, fetch_weights(): lax.all_gather(w_router[layer_idx], ('dp', 'expert'), axis=0, tiled=True)  136 us
    all_gather x2, blocking collectives, fetch_weights(): lax.all_gather(norm_gains[layer_idx], ('dp', 'expert'), axis=1, tiled=True)  76.4 us
  transfers between devices with their start and end apart: 33, of which 24 were waited for; matrix products, arithmetic and copies ran while one was open for 20% of the time, Pallas kernels for 0%

commit v1 on v0

v1 whole, which is shorter than its diff:
```python
from functools import partial
import math

import jax
import jax.numpy as jnp
from jax import lax
from jax.experimental import pallas as pl
from jax.experimental.pallas import tpu as pltpu
from jax.sharding import PartitionSpec as P

D = 1536
QUERY_HEADS = 12
KEY_VALUE_HEADS = 2
HEAD_SIZE = 128
MESH = pl.DeviceIdType.MESH
DP, EX = "dp", "expert"
ANY = pl.ANY
bf16 = jnp.bfloat16
f32 = jnp.float32

epsilon = 1e-06
rope_base = 1000000.0
masked_score = -1e30
everywhere = (DP, EX)


def place():
    z = lax.axis_index(DP)
    e = lax.axis_index(EX)
    y, x, c = e // 4, (e // 2) % 2, e % 2
    near = {
        "own": e,
        "x": y * 4 + (1 - x) * 2 + c,
        "y": (1 - y) * 4 + x * 2 + c,
        "d": (1 - y) * 4 + (1 - x) * 2 + c,
        "c": y * 4 + x * 2 + (1 - c),
        "cx": y * 4 + (1 - x) * 2 + (1 - c),
        "cy": (1 - y) * 4 + x * 2 + (1 - c),
        "cd": (1 - y) * 4 + (1 - x) * 2 + (1 - c),
    }
    return z, near


def greet(z, near, plane, line):
    barrier = pltpu.get_barrier_semaphore()
    for name in plane:
        pl.semaphore_signal(
            barrier, inc=1, device_id={EX: near[name]}, device_id_type=MESH
        )
    count = len(plane)
    if line is None:
        pl.semaphore_wait(barrier, count)
        return

    @pl.when(z < line - 1)
    def up():
        pl.semaphore_signal(barrier, inc=1, device_id={DP: z + 1}, device_id_type=MESH)

    @pl.when(z > 0)
    def down():
        pl.semaphore_signal(barrier, inc=1, device_id={DP: z - 1}, device_id_type=MESH)

    inside = (z > 0) & (z < line - 1)

    @pl.when(inside)
    def wait_inside():
        pl.semaphore_wait(barrier, count + 2)

    @pl.when(jnp.logical_not(inside))
    def wait_end():
        pl.semaphore_wait(barrier, count + 1)


def halves(rows, columns):
    if rows % 32 == 0:
        return ((0, rows // 2), (0, columns)), ((rows // 2, rows // 2), (0, columns))
    if columns % 256 == 0:
        return ((0, rows), (0, columns // 2)), ((0, rows), (columns // 2, columns // 2))
    return ((0, 16), (0, columns)), ((16, rows - 16), (0, columns))


def cut(ref, part):
    (row, rows), (column, columns) = part
    return ref.at[pl.ds(row, rows), pl.ds(column, columns)]


KINDS = 10


class Gather:
    def __init__(self, ins, outs, send, recv, z, near, line):
        self.ins, self.outs, self.send, self.recv = ins, outs, send, recv
        self.z, self.near, self.line = z, near, line
        self.parts = [halves(*ref.shape) for ref in ins]
        self.all = range(len(ins))

    def hop(self, a, j, kind, whose, to, part=None, src=None):
        dst = self.outs[a].at[j, self.near[whose]]
        src = dst if src is None else src
        if part is not None:
            src, dst = cut(src, part), cut(dst, part)
        return pltpu.make_async_remote_copy(
            src_ref=src,
            dst_ref=dst,
            send_sem=self.send.at[a, j, kind],
            recv_sem=self.recv.at[a, j, kind],
            device_id={DP: to} if kind >= 8 else {EX: self.near[to]},
            device_id_type=MESH,
        )

    def landed(self, a, j, kind, whose, part=None):
        if kind < 8:
            self.hop(a, j, kind, whose, "c", part).wait_recv()
        else:
            self.hop(a, j, kind, whose, self.z).wait_recv()

    def line_first(self):
        z = self.z

        @pl.when(z < self.line - 1)
        def up_first():
            for a in self.all:
                self.hop(a, z, 8, "own", z + 1, src=self.ins[a]).start()

        @pl.when(z > 0)
        def down_first():
            for a in self.all:
                self.hop(a, z, 9, "own", z - 1, src=self.ins[a]).start()

    def first(self, j, src=None):
        for a in self.all:
            one = None if src is None else src[a]
            self.hop(a, j, 0, "own", "x", src=one).start()
            self.hop(a, j, 1, "own", "y", src=one).start()
            self.hop(a, j, 2, "own", "c", src=one).start()

    def second(self, j, kind=0):
        for a in self.all:
            self.landed(a, j, 0, "x")
            self.hop(a, j, 4, "x", "y", self.parts[a][1]).start()
            self.hop(a, j, 5, "x", "c").start()
            self.landed(a, j, 1, "y")
            self.hop(a, j, 3, "y", "x", self.parts[a][0]).start()
            self.hop(a, j, 6, "y", "c").start()

    def third(self, j, kind=0):
        for a in self.all:
            self.landed(a, j, 3, "d", self.parts[a][0])
            self.landed(a, j, 4, "d", self.parts[a][1])
            self.hop(a, j, 7, "d", "c").start()

    def finish(self, j, kind=0):
        for a in self.all:
            for kind, whose in ((2, "c"), (5, "cx"), (6, "cy"), (7, "cd")):
                self.landed(a, j, kind, whose)
            for kind in (0, 1, 2):
                self.hop(a, j, kind, "own", "c").wait_send()
            self.hop(a, j, 3, "y", "x", self.parts[a][0]).wait_send()
            self.hop(a, j, 4, "x", "y", self.parts[a][1]).wait_send()
            for kind in (5, 6, 7):
                self.hop(a, j, kind, "x", "c").wait_send()

    def arrivals(self, step, act):
        z = self.z

        @pl.when(z - step >= 0)
        def below():
            act(z - step, 8)

        @pl.when(z + step <= self.line - 1)
        def above():
            act(z + step, 9)

    def take(self, j, kind):
        for a in self.all:
            self.landed(a, j, kind, "own")
        z = self.z
        if kind == 8:

            @pl.when(z < self.line - 1)
            def on_up():
                for a in self.all:
                    self.hop(a, j, 8, "own", z + 1).start()

        else:

            @pl.when(z > 0)
            def on_down():
                for a in self.all:
                    self.hop(a, j, 9, "own", z - 1).start()

        self.first(j)

    def line_done(self):
        z = self.z
        for step in range(self.line):

            @pl.when((z - step >= 0) & (z < self.line - 1))
            def up_done():
                for a in self.all:
                    self.hop(a, z - step, 8, "own", z + 1).wait_send()

            @pl.when((z + step <= self.line - 1) & (z > 0))
            def down_done():
                for a in self.all:
                    self.hop(a, z + step, 9, "own", z - 1).wait_send()


def gather_kernel(n_arrays, line, *refs):
    ins, outs = refs[:n_arrays], refs[n_arrays : 2 * n_arrays]
    send, recv, keep = refs[2 * n_arrays :]
    z, near = place()
    g = Gather(ins, outs, send, recv, z, near, line)
    greet(z, near, ("x", "y", "c"), line)
    local = [
        pltpu.make_async_copy(ins[a], outs[a].at[z, near["own"]], keep.at[a])
        for a in range(n_arrays)
    ]
    g.line_first()
    g.first(z, ins)
    for copy_here in local:
        copy_here.start()
    g.arrivals(1, g.take)
    g.second(z)
    g.arrivals(2, g.take)
    g.third(z)
    g.arrivals(1, g.second)
    g.arrivals(3, g.take)
    g.arrivals(1, g.third)
    g.arrivals(2, g.second)
    g.arrivals(2, g.third)
    g.arrivals(3, g.second)
    g.arrivals(3, g.third)
    g.finish(z)
    for step in range(1, line):
        g.arrivals(step, g.finish)
    for copy_here in local:
        copy_here.wait()
    g.line_done()


def fast_mesh():
    return lax.axis_size(DP) == 4 and lax.axis_size(EX) == 8


def gather_all(shards, number):
    n_dp, n_expert = lax.axis_size(DP), lax.axis_size(EX)
    if not fast_mesh():
        return [
            lax.all_gather(shard, everywhere, axis=0).reshape((n_dp, n_expert) + shard.shape)
            for shard in shards
        ]
    n_arrays = len(shards)
    return pl.pallas_call(
        partial(gather_kernel, n_arrays, n_dp),
        out_shape=[
            jax.ShapeDtypeStruct((n_dp, n_expert) + shard.shape, shard.dtype) for shard in shards
        ],
        in_specs=[pl.BlockSpec(memory_space=ANY)] * n_arrays,
        out_specs=[pl.BlockSpec(memory_space=ANY)] * n_arrays,
        scratch_shapes=[
            pltpu.SemaphoreType.DMA((n_arrays, n_dp, KINDS)),
            pltpu.SemaphoreType.DMA((n_arrays, n_dp, KINDS)),
            pltpu.SemaphoreType.DMA((n_arrays,)),
        ],
        compiler_params=pltpu.CompilerParams(collective_id=number, has_side_effects=True),
        name="gather_all",
    )(*shards)


def plane_gather(src, dst, send, recv, near):
    parts = halves(*src.shape)

    def hop(kind, whose, to, part=None):
        one = dst.at[near[whose]] if part is None else cut(dst.at[near[whose]], part)
        return pltpu.make_async_remote_copy(
            src_ref=src if whose == "own" else one,
            dst_ref=one,
            send_sem=send.at[kind],
            recv_sem=recv.at[kind],
            device_id={EX: near[to]},
            device_id_type=MESH,
        )

    def first():
        hop(0, "own", "x").start()
        hop(1, "own", "y").start()
        hop(2, "own", "c").start()
        dst[near["own"]] = src[...]

    def second():
        hop(0, "x", "c").wait_recv()
        hop(4, "x", "y", parts[1]).start()
        hop(5, "x", "c").start()
        hop(1, "y", "c").wait_recv()
        hop(3, "y", "x", parts[0]).start()
        hop(6, "y", "c").start()

    def third():
        hop(3, "d", "c", parts[0]).wait_recv()
        hop(4, "d", "c", parts[1]).wait_recv()
        hop(7, "d", "c").start()

    def finish():
        for kind, whose in ((2, "c"), (5, "cx"), (6, "cy"), (7, "cd")):
            hop(kind, whose, "c").wait_recv()
        for kind in (0, 1, 2):
            hop(kind, "own", "c").wait_send()
        hop(3, "y", "x", parts[0]).wait_send()
        hop(4, "x", "y", parts[1]).wait_send()
        for kind in (5, 6, 7):
            hop(kind, "x", "c").wait_send()

    return first, second, third, finish


def sum_scratch(rows, columns):
    return [
        pltpu.VMEM((8, rows, columns), bf16),
        pltpu.VMEM((3, rows, columns), bf16),
        pltpu.VMEM((4, rows, columns), bf16),
        pltpu.VMEM((2, rows // 2, columns), bf16),
        pltpu.VMEM((2, rows // 2, columns), bf16),
        pltpu.VMEM((2, rows // 2, columns), bf16),
        pltpu.SemaphoreType.DMA((10,)),
        pltpu.SemaphoreType.DMA((10,)),
    ]


def plane_sum(make, out_ref, base, scratch, near):
    part_ref, paired, fromc, fromx, fromy, last, send, recv = scratch
    rows = out_ref.shape[0]
    half = rows // 2
    A, B = pl.ds(0, half), pl.ds(half, half)

    def copy(number, src, dst, to):
        return pltpu.make_async_remote_copy(
            src_ref=src,
            dst_ref=dst,
            send_sem=send.at[number],
            recv_sem=recv.at[number],
            device_id={EX: near[to]},
            device_id_type=MESH,
        )

    order = ("d", "x", "y", "own")
    across = ("cd", "cx", "cy", "c")
    core = [copy(s, part_ref.at[near[name]], fromc.at[s], "c") for s, name in enumerate(across)]
    to_x = [copy(4, paired.at[0, A], fromx.at[0], "x"), copy(5, paired.at[1, A], fromx.at[1], "x")]
    to_y = [copy(6, paired.at[0, B], fromy.at[0], "y"), copy(7, paired.at[2, B], fromy.at[1], "y")]
    late_y = copy(8, paired.at[2, A], last.at[0], "y")
    late_x = copy(9, paired.at[1, B], last.at[1], "x")

    def pair(s):
        core[s].wait_recv()
        paired[s] = (part_ref[near[order[s]]].astype(f32) + fromc[s].astype(f32)).astype(bf16)

    for s in range(3):
        make(across[s])
        core[s].start()
        make(order[s])
    pair(0)
    to_x[0].start()
    to_y[0].start()
    make(across[3])
    core[3].start()
    pair(1)
    to_x[1].start()
    pair(2)
    to_y[1].start()
    make(order[3])
    core[3].wait_recv()
    total = part_ref[near["own"]].astype(f32) + fromc[3].astype(f32)
    out_ref[...] = total if base is None else base[...] + total
    to_x[0].wait_recv()
    paired[2, A] = (paired[2, A].astype(f32) + fromx[0].astype(f32)).astype(bf16)
    late_y.start()
    to_y[0].wait_recv()
    paired[1, B] = (paired[1, B].astype(f32) + fromy[0].astype(f32)).astype(bf16)
    late_x.start()
    to_x[1].wait_recv()
    out_ref[A] += fromx[1].astype(f32)
    to_y[1].wait_recv()
    out_ref[B] += fromy[1].astype(f32)
    late_y.wait_recv()
    out_ref[A] += last[0].astype(f32)
    late_x.wait_recv()
    out_ref[B] += last[1].astype(f32)
    for one in core + to_x + to_y + [late_x, late_y]:
        one.wait_send()


def mul(a, b, over=((1,), (0,))):
    return lax.dot_general(a, b, (over, ((), ())), preferred_element_type=f32)


LAST = ((1,), (1,))


def seat_rows(seats, number):
    local_n, tokens_n = seats.shape
    rows = lax.broadcasted_iota(jnp.int32, (local_n * number, tokens_n), 0)
    hot = rows < 0
    for e in range(local_n):
        one = seats[e : e + 1, :]
        hot = hot | ((rows == one + (e * number - 1)) & (one > 0) & (one <= number))
    return jnp.where(hot, 1.0, 0.0).astype(bf16)


def seat_columns(seats, number):
    tokens_n, local_n = seats.shape
    columns = lax.broadcasted_iota(jnp.int32, (tokens_n, local_n * number), 1)
    hot = columns < 0
    for e in range(local_n):
        one = seats[:, e : e + 1]
        hot = hot | ((columns == one + (e * number - 1)) & (one > 0) & (one <= number))
    return jnp.where(hot, 1.0, 0.0).astype(bf16)


def masked_gates(logits, hit):
    top = jnp.max(jnp.where(hit, logits, masked_score), axis=0, keepdims=True)
    powers = jnp.where(hit, jnp.exp(jnp.where(hit, logits - top, 0.0)), 0.0)
    return powers / jnp.sum(powers, axis=0, keepdims=True)


def expert_kernel(
    layer,
    number,
    normed,
    mixed,
    router,
    hit,
    seats,
    seats_turned,
    w_gate,
    w_up,
    w_down,
    new_stream,
    rows_in,
    gate_pre,
    up_pre,
    gate_seat,
    tokens,
    gates,
    weighted,
    gate_w,
    up_w,
    down_w,
    weight_sem,
    send,
    recv,
    *scratch,
):
    z, near = place()
    local_n = seats.shape[0]
    rows = normed.shape[0]
    weights = [
        pltpu.make_async_copy(src.at[layer], dst, weight_sem.at[i])
        for i, (src, dst) in enumerate(((w_gate, gate_w), (w_up, up_w), (w_down, down_w)))
    ]
    greet(z, near, ("x", "y", "c"), None)
    first, second, third, finish = plane_gather(normed, tokens, send, recv, near)
    first()
    for one in weights:
        one.start()
    second()
    third()
    finish()
    everyone = tokens[...].reshape(-1, tokens.shape[2])
    gates[...] = masked_gates(mul(router[...], everyone, LAST), hit[...] > 0)
    pick = seat_rows(seats[...], number)
    for e in range(local_n):
        here = pl.ds(e * number, number)
        mine = gates[pl.ds(lax.axis_index(EX) * local_n + e, 1), :]
        gate_seat[here] = jnp.sum(
            pick[e * number : (e + 1) * number].astype(f32) * mine, axis=1, keepdims=True
        )
    rows_in[...] = mul(pick, everyone).astype(bf16)
    for one in weights:
        one.wait()

    def expert(e, carry):
        here = pl.ds(pl.multiple_of(e * number, 32), number)
        x = rows_in[here]
        gate = mul(x, gate_w[e])
        up = mul(x, up_w[e])
        gate_pre[here] = gate
        up_pre[here] = up
        hidden = (gate * (1.0 / (1.0 + jnp.exp(-gate))) * up).astype(bf16)
        weighted[here] = (mul(hidden, down_w[e]) * gate_seat[here]).astype(bf16)
        return carry

    lax.fori_loop(0, local_n, expert, 0)

    def make(name):
        d = near[name]
        back = seat_columns(seats_turned[pl.ds(pl.multiple_of(d * rows, rows), rows)], number)
        scratch[0][d] = mul(back, weighted[...]).astype(bf16)

    plane_sum(make, new_stream, mixed, scratch, near)


def expert_back_kernel(
    layer,
    number,
    experts_n,
    grads,
    seats,
    seats_turned,
    gate_pre,
    up_pre,
    gate_seat,
    w_gate,
    w_up,
    w_down,
    summed,
    rows_grad,
    hidden_low,
    dgate_low,
    dup_low,
    tokens,
    back_rows,
    gate_w,
    up_w,
    down_w,
    weight_sem,
    send,
    recv,
    *scratch,
):
    z, near = place()
    local_n = seats.shape[0]
    rows, width = grads.shape
    weights = [
        pltpu.make_async_copy(src.at[layer], dst, weight_sem.at[i])
        for i, (src, dst) in enumerate(((w_gate, gate_w), (w_up, up_w), (w_down, down_w)))
    ]
    greet(z, near, ("x", "y", "c"), None)
    first, second, third, finish = plane_gather(grads, tokens, send, recv, near)
    first()
    for one in weights:
        one.start()
    second()
    third()
    finish()
    everyone = tokens[...].reshape(-1, tokens.shape[2])
    picked = mul(seat_rows(seats[...], number), everyone)
    back_rows[:, pl.ds(0, width)] = picked.astype(bf16)
    rows_grad[...] = (picked * gate_seat[...]).astype(bf16)
    for one in weights:
        one.wait()

    def expert(e, carry):
        here = pl.ds(pl.multiple_of(e * number, 32), number)
        gate, up = gate_pre[here], up_pre[here]
        raw = mul(back_rows[here, pl.ds(0, width)], down_w[e], LAST)
        sigmoid = 1.0 / (1.0 + jnp.exp(-gate))
        silu = gate * sigmoid
        hidden = (silu * up).astype(bf16)
        hidden_low[here] = hidden
        dgate_seat = jnp.sum(hidden.astype(f32) * raw, axis=1, keepdims=True)
        raw = raw * gate_seat[here]
        dgate = (raw * up * sigmoid * (1.0 + gate * (1.0 - sigmoid))).astype(bf16)
        dup = (raw * silu).astype(bf16)
        dgate_low[here] = dgate
        dup_low[here] = dup
        back_rows[here, pl.ds(0, width)] = (
            mul(dgate, gate_w[e], LAST) + mul(dup, up_w[e], LAST)
        ).astype(bf16)
        high = dgate_seat.astype(bf16).astype(f32)
        lane = lax.broadcasted_iota(jnp.int32, (number, 128), 1)
        mine = lax.axis_index(EX) * local_n + e
        back_rows[here, pl.ds(width, 128)] = jnp.where(
            lane == mine, high, jnp.where(lane == experts_n + mine, dgate_seat - high, 0.0)
        ).astype(bf16)
        return carry

    lax.fori_loop(0, local_n, expert, 0)

    def make(name):
        d = near[name]
        back = seat_columns(seats_turned[pl.ds(pl.multiple_of(d * rows, rows), rows)], number)
        scratch[0][d] = mul(back, back_rows[...]).astype(bf16)

    plane_sum(make, summed, None, scratch, near)


def tail_kernel(layers_n, number, n_sums, *refs):
    refs = list(refs)

    def some(count):
        taken = refs[:count]
        del refs[:count]
        return taken

    tokens_all, grads_all = some(layers_n), some(layers_n - 1)
    (own_shard,) = some(1)
    routers, hit, seats = some(3)
    w_gate, w_up, w_down = some(3)
    owns = [some(5) for l in range(layers_n)]
    parts = some(n_sums)
    grad_gate, grad_up, grad_down, landing = some(4)
    sums = some(n_sums)
    (
        tokens,
        grads,
        gates,
        rows_in,
        rows_grad,
        cols_in,
        cols_grad,
        hidden_low,
        dgate_low,
        dup_low,
        gate_w,
        up_w,
        down_w,
        stage_wide,
        stage_tall,
        weight_sem,
        token_sem,
        own_sem,
        out_sem,
        gather_send,
        gather_recv,
    ) = some(21)
    held = [some(6) for a in range(n_sums)]
    z, near = place()
    n_dp, local_n = seats.shape[1], seats.shape[2]
    width = cols_in.shape[1]
    ours = pl.ds(pl.multiple_of(z * width, 128), width)
    gather = Gather([own_shard], [landing], gather_send, gather_recv, z, near, n_dp)
    total = Sums(parts, sums, held, *refs, z, near, n_dp)
    per_expert = n_dp - 1
    per_layer = local_n * per_expert
    steps = layers_n * per_layer

    def layer_of(i):
        return layers_n - 1 - i // per_layer

    def fetch(i, slot, act):
        j = lax.rem(z + 1 + lax.rem(i, per_expert), n_dp)
        for l in range(layers_n):

            @pl.when(layer_of(i) == l)
            def of_layer():
                tokens_from = tokens_all[l].at[pl.ds(j * 8, 8)]
                if l == 0:
                    grads_from = landing.at[j]
                else:
                    grads_from = grads_all[l - 1].at[pl.ds(j * 8, 8)]
                act(pltpu.make_async_copy(tokens_from, tokens.at[slot], token_sem.at[slot, 0]))
                act(pltpu.make_async_copy(grads_from, grads.at[slot], token_sem.at[slot, 1]))

    def weights(l, e):
        return [
            pltpu.make_async_copy(src.at[l, e], dst, weight_sem.at[i])
            for i, (src, dst) in enumerate(((w_gate, gate_w), (w_up, up_w), (w_down, down_w)))
        ]

    def own(l, e):
        here = pl.ds(pl.multiple_of(e * number, 32), number)
        inner = pl.ds(0, number)
        pairs = (
            (owns[l][0].at[here, ours], cols_in.at[inner]),
            (owns[l][1].at[here, ours], cols_grad.at[inner]),
            (owns[l][2].at[here], hidden_low.at[inner]),
            (owns[l][3].at[here], dgate_low.at[inner]),
            (owns[l][4].at[here], dup_low.at[inner]),
        )
        return [
            pltpu.make_async_copy(src, dst, own_sem.at[i]) for i, (src, dst) in enumerate(pairs)
        ]

    def of(i, make, act):
        e = lax.rem(i // per_expert, local_n)
        for l in range(layers_n):

            @pl.when(layer_of(i) == l)
            def of_layer():
                for one in make(l, e):
                    act(one)

    def start(one):
        one.start()

    def wait(one):
        one.wait()

    def results(l, e):
        return [
            pltpu.make_async_copy(stage_wide.at[0], grad_gate.at[l, e], out_sem.at[0]),
            pltpu.make_async_copy(stage_wide.at[1], grad_up.at[l, e], out_sem.at[1]),
            pltpu.make_async_copy(stage_tall, grad_down.at[l, e], out_sem.at[2]),
        ]

    greet(z, near, ("x", "y", "c"), n_dp)
    gather.line_first()
    total.at(3, total.first)
    total.at(2, total.first)
    of(0, weights, start)
    fetch(0, 0, start)

    services = {
        0: [lambda: gather.arrivals(1, gather.take)],
        1: [lambda: gather.arrivals(2, gather.take)],
        2: [
            lambda: gather.arrivals(1, gather.second),
            lambda: gather.arrivals(3, gather.take),
        ],
        3: [
            lambda: gather.arrivals(1, gather.third),
            lambda: gather.arrivals(2, gather.second),
            lambda: total.at(3, total.second),
            lambda: total.at(2, total.second),
        ],
        4: [
            lambda: gather.arrivals(2, gather.third),
            lambda: gather.arrivals(3, gather.second),
            lambda: total.at(1, total.first),
            lambda: total.at(0, total.first),
        ],
        5: [
            lambda: gather.arrivals(3, gather.third),
            lambda: gather.arrivals(1, gather.finish),
            lambda: gather.arrivals(2, gather.finish),
            lambda: gather.arrivals(3, gather.finish),
        ],
        7: [lambda: total.at(3, total.third)],
        8: [lambda: total.at(2, total.third)],
        9: [lambda: total.at(1, total.second)],
        10: [lambda: total.at(0, total.second)],
        11: [lambda: total.at(1, total.third)],
    }

    def step(i, carry):
        slot = lax.rem(i, 2)
        l = layer_of(i)
        k = lax.rem(i, per_expert)
        e = lax.rem(i // per_expert, local_n)
        j = lax.rem(z + 1 + k, n_dp)

        @pl.when(k == 0)
        def begin():
            of(i, own, start)

        @pl.when((i + 1 < steps) & (i != per_layer - 1))
        def ahead():
            fetch(i + 1, 1 - slot, start)

        fetch(i, slot, wait)
        everyone = tokens[slot].reshape(-1, tokens.shape[3])
        gates[...] = masked_gates(mul(routers[l], everyone, LAST), hit[l, j] > 0)
        pick = seat_rows(seats[l, j, pl.ds(e, 1)], number)
        rows_in[...] = mul(pick, everyone).astype(bf16)
        rows_grad[...] = mul(pick, grads[slot].reshape(-1, tokens.shape[3])).astype(bf16)
        place_of = pl.ds(pl.multiple_of((k + 1) * number, 32), number)
        mine = gates[pl.ds(lax.axis_index(EX) * local_n + e, 1), :]
        gate_seat = jnp.sum(pick.astype(f32) * mine, axis=1, keepdims=True)

        @pl.when(k == 0)
        def weights_here():
            of(i, weights, wait)

        gate = mul(rows_in[...], gate_w[...])
        up = mul(rows_in[...], up_w[...])
        raw = mul(rows_grad[...], down_w[...], LAST) * gate_seat
        sigmoid = 1.0 / (1.0 + jnp.exp(-gate))
        silu = gate * sigmoid
        hidden_low[place_of] = (silu * up).astype(bf16)
        dgate_low[place_of] = (raw * up * sigmoid * (1.0 + gate * (1.0 - sigmoid))).astype(bf16)
        dup_low[place_of] = (raw * silu).astype(bf16)
        cols_in[place_of] = rows_in[:, ours]
        cols_grad[place_of] = (rows_grad[:, ours].astype(f32) * gate_seat).astype(bf16)

        @pl.when(k == per_expert - 1)
        def close():
            @pl.when(i + 1 < steps)
            def next_weights():
                of(i + 1, weights, start)

            of(i, own, wait)

            @pl.when(i >= per_expert)
            def staged():
                of(i - per_expert, results, wait)

            over = ((0,), (0,))
            stage_wide[0] = mul(cols_in[...], dgate_low[...], over)
            stage_wide[1] = mul(cols_in[...], dup_low[...], over)
            stage_tall[...] = mul(hidden_low[...], cols_grad[...], over)
            of(i, results, start)

        for at, acts in services.items():

            @pl.when(i == at)
            def serve():
                for act in acts:
                    act()

        @pl.when(i == per_layer - 1)
        def late_ahead():
            fetch(i + 1, 1 - slot, start)

        return carry

    lax.fori_loop(0, steps, step, 0)
    total.at(0, total.third)
    for distance in (3, 2, 1, 0):
        total.at(distance, total.finish)
    gather.line_done()
    of(steps - 1, results, wait)


def tail(capacity, number, tokens_all, grads_all, own_shard, routers, hit, seats, weights, owns, parts):
    layers_n, n_dp, local_n, group_rows = seats.shape
    n_expert = lax.axis_size(EX)
    rows, width = own_shard.shape
    hidden = weights[0].shape[3]
    part = width // n_dp
    shape = jax.ShapeDtypeStruct
    n_sums = len(parts)
    flat = [one for own in owns for one in own]
    results = pl.pallas_call(
        partial(tail_kernel, layers_n, capacity, n_sums),
        out_shape=[
            shape((layers_n, local_n, part, hidden), f32),
            shape((layers_n, local_n, part, hidden), f32),
            shape((layers_n, local_n, hidden, part), f32),
            shape((n_dp, n_expert, rows, width), bf16),
        ]
        + [shape(one.shape[2:], f32) for one in parts],
        in_specs=[HBM] * (2 * layers_n) + [VMEM] * 3 + [HBM] * (3 + len(flat) + n_sums),
        out_specs=[HBM] * 4 + [VMEM] * n_sums,
        scratch_shapes=[
            pltpu.VMEM((2, n_expert, rows, width), bf16),
            pltpu.VMEM((2, n_expert, rows, width), bf16),
            pltpu.VMEM(hit.shape[2:], f32),
            pltpu.VMEM((capacity, width), bf16),
            pltpu.VMEM((capacity, width), bf16),
            pltpu.VMEM((n_dp * capacity, part), bf16),
            pltpu.VMEM((n_dp * capacity, part), bf16),
            pltpu.VMEM((n_dp * capacity, hidden), bf16),
            pltpu.VMEM((n_dp * capacity, hidden), bf16),
            pltpu.VMEM((n_dp * capacity, hidden), bf16),
            pltpu.VMEM((width, hidden), bf16),
            pltpu.VMEM((width, hidden), bf16),
            pltpu.VMEM((hidden, width), bf16),
            pltpu.VMEM((2, part, hidden), f32),
            pltpu.VMEM((hidden, part), f32),
            pltpu.SemaphoreType.DMA((3,)),
            pltpu.SemaphoreType.DMA((2, 2)),
            pltpu.SemaphoreType.DMA((5,)),
            pltpu.SemaphoreType.DMA((3,)),
            pltpu.SemaphoreType.DMA((1, n_dp, KINDS)),
            pltpu.SemaphoreType.DMA((1, n_dp, KINDS)),
        ]
        + sums_scratch([one.shape[2:] for one in parts], n_dp),
        compiler_params=settings(number),
        name="tail",
    )(*tokens_all, *grads_all, own_shard, routers, hit, seats, *weights, *flat, *parts)
    return results[:3], results[4:]


def expert_scratch(n_expert, rows, local_n, width, hidden):
    return [
        pltpu.VMEM((local_n, width, hidden), bf16),
        pltpu.VMEM((local_n, width, hidden), bf16),
        pltpu.VMEM((local_n, hidden, width), bf16),
        pltpu.SemaphoreType.DMA((3,)),
        pltpu.SemaphoreType.DMA((8,)),
        pltpu.SemaphoreType.DMA((8,)),
    ]


VMEM = pl.BlockSpec(memory_space=pltpu.VMEM)
HBM = pl.BlockSpec(memory_space=ANY)


def settings(number):
    return pltpu.CompilerParams(
        collective_id=number, has_side_effects=True, vmem_limit_bytes=60 << 20
    )


def experts_forward(l, capacity, number, normed, mixed, router, hit, seats, weights):
    rows, width = normed.shape
    local_n, hidden = weights[0].shape[1], weights[0].shape[3]
    n_expert = lax.axis_size(EX)
    seats_n = local_n * capacity
    shape = jax.ShapeDtypeStruct
    return pl.pallas_call(
        partial(expert_kernel, l, capacity),
        out_shape=[
            shape((rows, width), f32),
            shape((seats_n, width), bf16),
            shape((seats_n, hidden), f32),
            shape((seats_n, hidden), f32),
            shape((seats_n, 1), f32),
        ],
        in_specs=[VMEM] * 6 + [HBM] * 3,
        out_specs=[VMEM] * 5,
        scratch_shapes=[
            pltpu.VMEM((n_expert, rows, width), bf16),
            pltpu.VMEM((local_n * n_expert, n_expert * rows), f32),
            pltpu.VMEM((seats_n, width), bf16),
        ]
        + expert_scratch(n_expert, rows, local_n, width, hidden)
        + sum_scratch(rows, width),
        compiler_params=settings(number),
        name="experts_forward",
    )(normed, mixed, router, hit, seats, seats.T, *weights)


def experts_backward(l, capacity, number, grads, seats, gate_pre, up_pre, gate_seat, weights):
    rows, width = grads.shape
    local_n, hidden = weights[0].shape[1], weights[0].shape[3]
    n_expert = lax.axis_size(EX)
    seats_n = local_n * capacity
    shape = jax.ShapeDtypeStruct
    return pl.pallas_call(
        partial(expert_back_kernel, l, capacity, local_n * n_expert),
        out_shape=[
            shape((rows, width + 128), f32),
            shape((seats_n, width), bf16),
            shape((seats_n, hidden), bf16),
            shape((seats_n, hidden), bf16),
            shape((seats_n, hidden), bf16),
        ],
        in_specs=[VMEM] * 6 + [HBM] * 3,
        out_specs=[VMEM] * 5,
        scratch_shapes=[
            pltpu.VMEM((n_expert, rows, width), bf16),
            pltpu.VMEM((seats_n, width + 128), bf16),
        ]
        + expert_scratch(n_expert, rows, local_n, width, hidden)
        + sum_scratch(rows, width + 128),
        compiler_params=settings(number),
        name="experts_backward",
    )(grads, seats, seats.T, gate_pre, up_pre, gate_seat, *weights)


class Sums:
    def __init__(self, ins, outs, held, send, recv, keep, z, near, line):
        self.ins, self.outs, self.held = ins, outs, held
        self.send, self.recv, self.keep = send, recv, keep
        self.z, self.near, self.line = z, near, line
        self.all = range(len(ins))

    def split(self, a):
        half = self.outs[a].shape[1] // 2
        return pl.ds(0, half), pl.ds(half, half)

    def move(self, a, j, name):
        part = self.ins[a]
        fromx, fromy, late, later, total, got = self.held[a]
        A, B = self.split(a)
        near = self.near
        kind, src, dst, to = {
            "xd": lambda: (0, part.at[j, near["d"], :, A], fromx.at[j, 0], "x"),
            "xx": lambda: (1, part.at[j, near["x"], :, A], fromx.at[j, 1], "x"),
            "yd": lambda: (2, part.at[j, near["d"], :, B], fromy.at[j, 0], "y"),
            "yy": lambda: (3, part.at[j, near["y"], :, B], fromy.at[j, 1], "y"),
            "ly": lambda: (4, late.at[j, 0], later.at[j, 0], "y"),
            "lx": lambda: (5, late.at[j, 1], later.at[j, 1], "x"),
            "up": lambda: (6, total.at[j], got.at[j], self.z + 1),
            "down": lambda: (7, total.at[j], got.at[j], self.z - 1),
        }[name]()
        if name == "down":
            slot = jnp.where(j == self.z - 1, self.line, j)
            dst = got.at[slot]
        return pltpu.make_async_remote_copy(
            src_ref=src,
            dst_ref=dst,
            send_sem=self.send.at[a, j, kind],
            recv_sem=self.recv.at[a, j, kind],
            device_id={DP: to} if kind >= 6 else {EX: near[to]},
            device_id_type=MESH,
        )

    def own_down(self, a):
        got = self.held[a][5]
        return pltpu.make_async_remote_copy(
            src_ref=got.at[self.line],
            dst_ref=got.at[self.line],
            send_sem=self.send.at[a, self.z, 7],
            recv_sem=self.recv.at[a, self.z, 7],
            device_id={DP: self.z},
            device_id_type=MESH,
        )

    def prepare(self, a, j):
        late, total = self.held[a][2], self.held[a][4]
        A, B = self.split(a)
        near, part = self.near, self.ins[a]
        return [
            pltpu.make_async_copy(src, dst, self.keep.at[a, j, i])
            for i, (src, dst) in enumerate(
                (
                    (part.at[j, near["y"], :, A], late.at[j, 0]),
                    (part.at[j, near["x"], :, B], late.at[j, 1]),
                    (part.at[j, near["own"]], total.at[j]),
                )
            )
        ]

    def at(self, step, act):
        if step == 0:
            act(self.z, 0)
            return

        @pl.when(self.z + step <= self.line - 1)
        def above():
            act(self.z + step, 1)

        @pl.when(self.z - step >= 0)
        def below():
            act(self.z - step, -1)

    def first(self, j, way):
        for a in self.all:
            for name in ("xd", "yd", "xx", "yy"):
                self.move(a, j, name).start()
            for one in self.prepare(a, j):
                one.start()

    def second(self, j, way):
        for a in self.all:
            fromx, fromy, late = self.held[a][:3]
            ready = self.prepare(a, j)
            ready[0].wait()
            self.move(a, j, "xd").wait_recv()
            late[j, 0] = (late[j, 0].astype(f32) + fromx[j, 0].astype(f32)).astype(bf16)
            self.move(a, j, "ly").start()
            ready[1].wait()
            self.move(a, j, "yd").wait_recv()
            late[j, 1] = (late[j, 1].astype(f32) + fromy[j, 0].astype(f32)).astype(bf16)
            self.move(a, j, "lx").start()

    def third(self, j, way):
        for a in self.all:
            fromx, fromy, late, later, total, got = self.held[a]
            for name in ("xx", "yy", "ly", "lx"):
                self.move(a, j, name).wait_recv()
            self.prepare(a, j)[2].wait()
            for side, (columns, here) in enumerate(zip(self.split(a), (fromx, fromy))):
                value = (
                    total[j, :, columns].astype(f32)
                    + here[j, 1].astype(f32)
                    + later[j, side].astype(f32)
                )
                if way == 0:
                    self.outs[a][:, columns] = value
                else:
                    total[j, :, columns] = value.astype(bf16)
            if way == 1:

                @pl.when(self.z > 0)
                def more_up():
                    self.move(a, j, "up").wait_recv()
                    total[j] = (total[j].astype(f32) + got[j].astype(f32)).astype(bf16)

                self.move(a, j, "up").start()
            elif way == -1:

                @pl.when(self.z < self.line - 1)
                def more_down():
                    self.move(a, j, "down").wait_recv()
                    total[j] = (total[j].astype(f32) + got[j].astype(f32)).astype(bf16)

                self.move(a, j, "down").start()
            else:

                @pl.when(self.z > 0)
                def end_up():
                    self.move(a, j, "up").wait_recv()
                    self.outs[a][...] += got[j].astype(f32)

                @pl.when(self.z < self.line - 1)
                def end_down():
                    self.own_down(a).wait_recv()
                    self.outs[a][...] += got[self.line].astype(f32)

    def finish(self, j, way):
        for a in self.all:
            for name in ("xd", "yd", "xx", "yy", "lx", "ly"):
                self.move(a, j, name).wait_send()
            if way == 1:
                self.move(a, j, "up").wait_send()
            elif way == -1:
                self.move(a, j, "down").wait_send()


def sums_scratch(shapes, line):
    scratch = []
    for rows, columns in shapes:
        half = columns // 2
        scratch += [pltpu.VMEM((line, 2, rows, half), bf16) for i in range(4)]
        scratch += [
            pltpu.VMEM((line, rows, columns), bf16),
            pltpu.VMEM((line + 1, rows, columns), bf16),
        ]
    return scratch + [
        pltpu.SemaphoreType.DMA((len(shapes), line, 8)),
        pltpu.SemaphoreType.DMA((len(shapes), line, 8)),
        pltpu.SemaphoreType.DMA((len(shapes), line, 3)),
    ]


def from_behind(value, axis, steps):
    count = lax.axis_size(axis)
    leading, last = (max(0, -steps), min(count, count - steps))
    return lax.ppermute(value, axis, [(source, source + steps) for source in range(leading, last)])


def from_sibling(value):
    count = lax.axis_size(EX)
    return lax.ppermute(value, EX, [(s, s + 1 - 2 * (s % 2)) for s in range(count)])


def rms_norm(stream, gain_row):
    return (
        stream * lax.rsqrt(jnp.mean(stream * stream, axis=-1, keepdims=True) + epsilon) * gain_row
    )


def rotary_tables(token_positions):
    half_dim = HEAD_SIZE // 2
    steps_up = jnp.arange(half_dim).astype(f32)
    frequency = jnp.exp(steps_up * (-2.0 * math.log(rope_base) / HEAD_SIZE))
    angles = token_positions.astype(f32)[:, None] * frequency[None, :]
    return jnp.cos(angles)[:, None, :], jnp.sin(angles)[:, None, :]


def apply_rotary(heads_in, cosine, sine_part):
    half_dim = heads_in.shape[-1] // 2
    first_half = heads_in[..., :half_dim]
    second_half = heads_in[..., half_dim:]
    return jnp.concatenate(
        [
            first_half * cosine - second_half * sine_part,
            second_half * cosine + first_half * sine_part,
        ],
        axis=-1,
    )


def gated_unit(gate_pre, up_pre):
    return jax.nn.silu(gate_pre) * up_pre


def masked_scores(query_rows, gathered_keys, allowed):
    token_rows = query_rows.shape[0]
    grouped_queries = query_rows.reshape(
        token_rows, KEY_VALUE_HEADS, QUERY_HEADS // KEY_VALUE_HEADS, HEAD_SIZE
    )
    score_scale = 1.0 / math.sqrt(HEAD_SIZE)
    scores = (
        jnp.einsum(
            "tkgd,skd->kgts", grouped_queries, gathered_keys, preferred_element_type=f32
        )
        * score_scale
    )
    return (jnp.where(allowed, scores, masked_score), grouped_queries)


def rank_table(routes, pair_order, experts_n):
    layers_n, token_rows, topk_n = routes.shape
    chosen = jnp.swapaxes(routes, 1, 2)
    order = jnp.swapaxes(pair_order.reshape(layers_n, token_rows, topk_n), 1, 2)
    ids = jnp.arange(experts_n, dtype=jnp.int32)[None, :, None]
    none = token_rows * topk_n
    place_of = jnp.full((layers_n, experts_n, token_rows), none, jnp.int32)
    for k in range(topk_n):
        place_of = jnp.where(chosen[:, k][:, None, :] == ids, order[:, k][:, None, :], place_of)
    smaller = (place_of[:, :, :, None] < place_of[:, :, None, :]).astype(jnp.int32)
    return jnp.where(place_of < none, jnp.sum(smaller, axis=2) + 1, 0)


def dense_gates(logits, mask):
    top = jnp.max(jnp.where(mask, logits, masked_score), axis=0, keepdims=True)
    powers = jnp.where(mask, jnp.exp(jnp.where(mask, logits - top, 0.0)), 0.0)
    return powers / jnp.sum(powers, axis=0, keepdims=True)


def local(
    tokens,
    w_qkv,
    w_out,
    w_router,
    norm_gains,
    w_gate,
    w_up,
    w_down,
    out_grad,
    segment_ids,
    routes,
    pair_order,
):
    fast = fast_mesh()
    token_rows = tokens.shape[0]
    layers_n = w_qkv.shape[0]
    topk_n = routes.shape[2]
    n_expert = lax.axis_size(EX)
    n_dp = lax.axis_size(DP)
    expert_here = lax.axis_index(EX)
    dp_here = lax.axis_index(DP)
    device_here = dp_here * n_expert + expert_here
    local_n = w_gate.shape[1]
    experts_n = local_n * n_expert
    capacity = 9 * n_expert * token_rows * topk_n // (8 * experts_n)
    group_rows = n_expert * token_rows
    query_width = QUERY_HEADS * HEAD_SIZE
    key_width = KEY_VALUE_HEADS * HEAD_SIZE
    score_scale = 1.0 / math.sqrt(HEAD_SIZE)
    token_positions = expert_here * token_rows + jnp.arange(token_rows, dtype=jnp.int32)
    cosine, sine_part = rotary_tables(token_positions)
    seg_prev = from_behind(segment_ids, everywhere, 1)
    has_prev = device_here > 0
    row_index = jnp.arange(token_rows)
    own_mask = (segment_ids[None, :] == segment_ids[:, None]) & (
        row_index[None, :] <= row_index[:, None]
    )
    prev_mask = (seg_prev[None, :] == segment_ids[:, None]) & has_prev
    allowed = jnp.concatenate([prev_mask, own_mask], axis=1)

    ranks = rank_table(routes, pair_order, experts_n)
    small = jnp.concatenate(
        [w_router[l] for l in range(layers_n)]
        + [jnp.swapaxes(norm_gains.reshape(2 * layers_n, -1), 0, 1)],
        axis=1,
    )
    small = jnp.pad(small, ((0, 0), (0, 128 - small.shape[1])))
    small_full, ranks_full, qkv_0, out_0 = gather_all(
        [small, ranks.reshape(layers_n * experts_n, token_rows), w_qkv[0], w_out[0]], 1
    )
    qkv_fulls = [qkv_0.reshape(D, -1)]
    out_fulls = [out_0.reshape(query_width, D)]
    for layer_idx in range(1, layers_n):
        qkv_fulls.append(lax.all_gather(w_qkv[layer_idx], everywhere, axis=0, tiled=True))
        out_fulls.append(lax.all_gather(w_out[layer_idx], everywhere, axis=0, tiled=True))
    small_full = small_full.reshape(D, 128)
    gains = jnp.swapaxes(
        small_full[:, layers_n * experts_n : layers_n * (experts_n + 2)], 0, 1
    ).astype(f32)
    routers = [small_full[:, l * experts_n : (l + 1) * experts_n] for l in range(layers_n)]
    routers_turned = [jnp.swapaxes(router, 0, 1) for router in routers]
    ranks_full = ranks_full.reshape(n_dp, n_expert, layers_n, experts_n, token_rows)
    if not fast:
        ranks_full = lax.dynamic_slice_in_dim(ranks_full, dp_here, 1, 0)
    groups = ranks_full.shape[0]
    own_group = dp_here if fast else 0
    hit_all = jnp.transpose(ranks_full > 0, (2, 0, 3, 1, 4)).reshape(
        layers_n, groups, experts_n, group_rows
    )
    mine = lax.dynamic_slice_in_dim(ranks_full, expert_here * local_n, local_n, 3)
    counts = jnp.sum((mine > 0).astype(jnp.int32), axis=-1)
    before = jnp.cumsum(counts, axis=1) - counts
    seats = jnp.where(mine > 0, before[..., None] + mine, 0)
    seats = jnp.transpose(seats, (2, 0, 3, 1, 4)).reshape(layers_n, groups, local_n, group_rows)
    seat_ids = jnp.arange(1, capacity + 1, dtype=jnp.int32)

    def own_of(array):
        return lax.dynamic_index_in_dim(array, own_group, 0, keepdims=False)

    def seat_map(l):
        return (seats[l][:, :, None, :] == seat_ids[:, None]).astype(bf16)

    def gates_of(normed_rows, l, hit):
        logits = jnp.einsum("de,td->et", routers[l], normed_rows, preferred_element_type=f32)
        return dense_gates(logits, hit)

    own_hit = [(ranks[l] > 0) for l in range(layers_n)]

    stream = tokens.astype(f32)
    saved_layers = []
    outputs = []
    for l in range(layers_n):
        qkv_full, out_full = qkv_fulls[l], out_fulls[l]
        normed_a = rms_norm(stream, gains[2 * l]).astype(bf16)
        projected_output = jnp.dot(normed_a, qkv_full, preferred_element_type=f32)
        query_rows = apply_rotary(
            projected_output[:, :query_width].reshape(token_rows, QUERY_HEADS, HEAD_SIZE),
            cosine,
            sine_part,
        ).astype(bf16)
        key_own = apply_rotary(
            projected_output[:, query_width : query_width + key_width].reshape(
                token_rows, KEY_VALUE_HEADS, HEAD_SIZE
            ),
            cosine,
            sine_part,
        ).astype(bf16)
        value_own = (
            projected_output[:, query_width + key_width :]
            .reshape(token_rows, KEY_VALUE_HEADS, HEAD_SIZE)
            .astype(bf16)
        )
        key_prev, value_prev = from_behind((key_own, value_own), everywhere, 1)
        gathered_keys = jnp.concatenate([key_prev, key_own], axis=0)
        gathered_values = jnp.concatenate([value_prev, value_own], axis=0)
        scores, grouped_queries = masked_scores(query_rows, gathered_keys, allowed)
        top_score = jnp.max(scores, axis=-1, keepdims=True)
        exp_scores = jnp.exp(scores - top_score)
        row_total = jnp.sum(exp_scores, axis=-1, keepdims=True)
        prob_low = (exp_scores / row_total).astype(bf16)
        log_total = top_score + jnp.log(row_total)
        attended = (
            jnp.einsum("kgts,skd->tkgd", prob_low, gathered_values, preferred_element_type=f32)
            .reshape(token_rows, query_width)
            .astype(bf16)
        )
        mixed_sum = stream + jnp.dot(attended, out_full, preferred_element_type=f32)
        normed_b = rms_norm(mixed_sum, gains[2 * l + 1]).astype(bf16)

        kept = {}
        if fast:
            if fast:
                normed_all = lax.all_gather(normed_b, everywhere, axis=0, tiled=True)
                kept["normed_all"] = normed_all.reshape(-1, token_rows, D)
            new_stream, *kept["own"] = experts_forward(
                l,
                capacity,
                12 + l,
                normed_b,
                mixed_sum,
                routers_turned[l],
                own_of(hit_all[l]).astype(jnp.int32),
                own_of(seats[l]),
                (w_gate, w_up, w_down),
            )
        else:
            group_normed = lax.all_gather(normed_b, EX, axis=0, tiled=True)
            kept["normed_all"] = group_normed[None]
            seat_own = own_of(seat_map(l))
            gates_own = gates_of(group_normed, l, own_of(hit_all[l]))
            gates_own = lax.dynamic_slice_in_dim(gates_own, expert_here * local_n, local_n, 0)
            gate_seat = jnp.sum(seat_own.astype(f32) * gates_own[:, None, :], axis=-1)
            expert_in = jnp.einsum(
                "est,td->esd", seat_own, group_normed, preferred_element_type=f32
            ).astype(bf16)
            gate_pre = jnp.einsum("esd,edf->esf", expert_in, w_gate[l], preferred_element_type=f32)
            up_pre = jnp.einsum("esd,edf->esf", expert_in, w_up[l], preferred_element_type=f32)
            hidden = gated_unit(gate_pre, up_pre).astype(bf16)
            expert_out = jnp.einsum("esf,efd->esd", hidden, w_down[l], preferred_element_type=f32)
            weighted = (expert_out * gate_seat[..., None]).astype(bf16)
            branch_part = jnp.einsum("est,esd->td", seat_own, weighted, preferred_element_type=f32)
            new_stream = mixed_sum + lax.psum_scatter(
                branch_part, EX, scatter_dimension=0, tiled=True
            )
        saved_layers.append(
            {
                "stream_in": stream,
                "normed_a": normed_a,
                "queries": query_rows,
                "key_all": gathered_keys,
                "value_all": gathered_values,
                "log_total": log_total,
                "attended": attended,
                "mixed_sum": mixed_sum,
                "normed_b": normed_b,
            }
            | kept
        )
        outputs.append(new_stream)
        stream = new_stream

    grad_stream = out_grad.astype(f32)
    weight_parts = [None] * layers_n
    expert_parts = [None] * layers_n
    owns = [None] * layers_n
    for l in reversed(range(layers_n)):
        record = saved_layers[l]
        qkv_full, out_full = qkv_fulls[l], out_fulls[l]
        grad_low = grad_stream.astype(bf16)
        if fast:
            rows_in, gate_pre, up_pre, gate_seat = record["own"]
            summed, rows_grad, hidden_low, dgate_low, dup_low = experts_backward(
                l,
                capacity,
                16 + l,
                grad_low,
                own_of(seats[l]),
                gate_pre,
                up_pre,
                gate_seat,
                (w_gate, w_up, w_down),
            )
        if fast:
            if l == layers_n - 1:
                grads_all = [
                    lax.all_gather(out_grad, everywhere, axis=0, tiled=True).reshape(
                        -1, token_rows, D
                    )
                ]
            owns[l] = (rows_in, rows_grad, hidden_low, dgate_low, dup_low)
            own_shard = grad_low
        else:
            normed_all = record["normed_all"]
            grad_all = lax.all_gather(grad_low, EX, axis=0, tiled=True)[None]
            seat_all = seat_map(l)
            gates_all = jax.vmap(lambda rows, hit: gates_of(rows, l, hit))(normed_all, hit_all[l])
            gates_mine = lax.dynamic_slice_in_dim(gates_all, expert_here * local_n, local_n, 1)
            gate_seat = jnp.sum(seat_all.astype(f32) * gates_mine[:, :, None, :], axis=-1)
            rows_in = jnp.einsum(
                "gest,gtd->egsd", seat_all, normed_all, preferred_element_type=f32
            ).astype(bf16)
            rows_grad = jnp.einsum(
                "gest,gtd->egsd", seat_all, grad_all, preferred_element_type=f32
            ).astype(bf16)
            gate_seat = jnp.swapaxes(gate_seat, 0, 1)[..., None]
            gate_pre = jnp.einsum("egsd,edf->egsf", rows_in, w_gate[l], preferred_element_type=f32)
            up_pre = jnp.einsum("egsd,edf->egsf", rows_in, w_up[l], preferred_element_type=f32)
            dhidden_raw = jnp.einsum(
                "egsd,efd->egsf", rows_grad, w_down[l], preferred_element_type=f32
            )
            hidden, gate_pull = jax.vjp(gated_unit, gate_pre, up_pre)
            hidden_low = hidden.astype(bf16)
            dgate_pre, dup_pre = gate_pull(dhidden_raw * gate_seat)
            dgate_low = dgate_pre.astype(bf16)
            dup_low = dup_pre.astype(bf16)
            dgate_seat = jnp.sum(hidden_low.astype(f32) * dhidden_raw, axis=-1)
            rows_grad = (rows_grad.astype(f32) * gate_seat).astype(bf16)

        def by_expert(array):
            return array.reshape(local_n, -1, array.shape[-1])

        def outer(one, other):
            return jnp.einsum(
                "esa,esb->eab", by_expert(one), by_expert(other), preferred_element_type=f32
            )

        if not fast:
            grad_gate_l = outer(rows_in, dgate_low)
            grad_up_l = outer(rows_in, dup_low)
            grad_down_l = outer(hidden_low, rows_grad)
            grad_gate_l = lax.psum_scatter(
                grad_gate_l.astype(bf16), DP, scatter_dimension=1, tiled=True
            ).astype(f32)
            grad_up_l = lax.psum_scatter(
                grad_up_l.astype(bf16), DP, scatter_dimension=1, tiled=True
            ).astype(f32)
            grad_down_l = lax.psum_scatter(
                grad_down_l.astype(bf16), DP, scatter_dimension=2, tiled=True
            ).astype(f32)
            expert_parts[l] = (grad_gate_l, grad_up_l, grad_down_l)

        if fast:
            dnormed_b = summed[:, :D]
            dgates = summed[:, D : D + experts_n] + summed[:, D + experts_n : D + 2 * experts_n]
        else:
            dexpert_in = (
                jnp.einsum("egsf,edf->egsd", dgate_low, w_gate[l], preferred_element_type=f32)
                + jnp.einsum("egsf,edf->egsd", dup_low, w_up[l], preferred_element_type=f32)
            ).astype(bf16)
            back_part = jnp.einsum(
                "gest,egsd->td", seat_all, dexpert_in, preferred_element_type=f32
            )
            dgates_part = jnp.sum(
                seat_all[0].astype(f32) * dgate_seat[:, 0, :, None], axis=1
            )
            mine = expert_here * local_n + jnp.arange(local_n, dtype=jnp.int32)
            lane = jnp.arange(experts_n, dtype=jnp.int32)
            dgates_part = jnp.sum(
                jnp.where(mine[:, None, None] == lane, dgates_part[..., None], 0.0), axis=0
            )
            dnormed_b, dgates = [
                lax.psum_scatter(part, EX, scatter_dimension=0, tiled=True)
                for part in (back_part, dgates_part)
            ]
        gates_token = gates_of(record["normed_b"], l, own_hit[l]).T
        dlogits = (
            gates_token * (dgates - jnp.sum(gates_token * dgates, axis=1, keepdims=True))
        ).astype(bf16)
        dnormed_b = dnormed_b + jnp.einsum(
            "te,de->td", dlogits, routers[l], preferred_element_type=f32
        )
        unused_norm, norm_pull = jax.vjp(rms_norm, record["mixed_sum"], gains[2 * l + 1])
        dmixed_part, dgain_b = norm_pull(dnormed_b)
        dmixed = grad_stream + dmixed_part
        grad_attn = dmixed.astype(bf16)
        attended_gradient = jnp.einsum(
            "td,qd->tq", grad_attn, out_full, preferred_element_type=f32
        ).astype(bf16)
        gathered_keys = record["key_all"]
        gathered_values = record["value_all"]
        scores, grouped_queries = masked_scores(record["queries"], gathered_keys, allowed)
        prob_float = jnp.exp(scores - record["log_total"])
        prob_low = prob_float.astype(bf16)
        grouped_gradient = attended_gradient.reshape(
            token_rows, KEY_VALUE_HEADS, QUERY_HEADS // KEY_VALUE_HEADS, HEAD_SIZE
        )
        dvalue_all = jnp.einsum(
            "kgts,tkgd->skd", prob_low, grouped_gradient, preferred_element_type=f32
        )
        dprobs = jnp.einsum(
            "tkgd,skd->kgts", grouped_gradient, gathered_values, preferred_element_type=f32
        )
        delta_row = jnp.sum(prob_float * dprobs, axis=-1, keepdims=True)
        dscores = (prob_float * (dprobs - delta_row)).astype(bf16)
        dqueries = (
            jnp.einsum(
                "kgts,skd->tkgd", dscores, gathered_keys, preferred_element_type=f32
            ).reshape(token_rows, QUERY_HEADS, HEAD_SIZE)
            * score_scale
        )
        dkey_all = (
            jnp.einsum("kgts,tkgd->skd", dscores, grouped_queries, preferred_element_type=f32)
            * score_scale
        )
        dkey_next, dvalue_next = from_behind(
            (dkey_all[:token_rows].astype(bf16), dvalue_all[:token_rows].astype(bf16)),
            everywhere,
            -1,
        )
        dkey_own = dkey_all[token_rows:] + dkey_next.astype(f32)
        dvalue_own = dvalue_all[token_rows:] + dvalue_next.astype(f32)
        dq_raw = apply_rotary(dqueries, cosine, -sine_part)
        dk_raw = apply_rotary(dkey_own, cosine, -sine_part)
        dprojected = jnp.concatenate(
            [
                dq_raw.reshape(token_rows, query_width),
                dk_raw.reshape(token_rows, key_width),
                dvalue_own.reshape(token_rows, key_width),
            ],
            axis=1,
        ).astype(bf16)
        dnormed_a = jnp.einsum("tq,dq->td", dprojected, qkv_full, preferred_element_type=f32)
        unused_first, first_pull = jax.vjp(rms_norm, record["stream_in"], gains[2 * l])
        dstream_part, dgain_a = first_pull(dnormed_a)
        grad_stream = dmixed + dstream_part

        small_grad = jnp.concatenate(
            [
                jnp.einsum("td,te->de", record["normed_b"], dlogits, preferred_element_type=f32),
                dgain_a[:, None],
                dgain_b[:, None],
            ],
            axis=1,
        )
        normed_a, attended = record["normed_a"], record["attended"]
        if fast:
            other = from_sibling((normed_a, attended, dprojected, grad_attn))
            normed_a, attended, dprojected, grad_attn = [
                jnp.concatenate([own, sib], axis=0)
                for own, sib in zip((normed_a, attended, dprojected, grad_attn), other)
            ]
            small_grad = small_grad + from_sibling(small_grad)
        grad_qkv_l = jnp.einsum("td,tq->dq", normed_a, dprojected, preferred_element_type=f32)
        grad_out_l = jnp.einsum("tq,td->qd", attended, grad_attn, preferred_element_type=f32)
        weight_parts[l] = (grad_qkv_l, grad_out_l, small_grad)

    small_grads = jnp.concatenate([weight_parts[l][2] for l in range(layers_n)], axis=1)
    if fast:
        shape = (n_dp, n_expert, D // (n_dp * n_expert))
        small_grads = jnp.pad(small_grads, ((0, 0), (0, 128 - small_grads.shape[1])))
        high = small_grads.astype(bf16)
        low = (small_grads - high.astype(f32)).astype(bf16)
        pieces = [jnp.concatenate([high, low], axis=1).reshape(shape + (256,))]
        for l in reversed(range(layers_n)):
            pieces.append(weight_parts[l][0].astype(bf16).reshape(shape + (-1,)))
            pieces.append(weight_parts[l][1].astype(bf16).reshape(shape + (-1,)))
        experts, summed = tail(
            capacity,
            20,
            [record["normed_all"] for record in saved_layers],
            grads_all,
            own_shard,
            jnp.stack(routers_turned),
            hit_all.astype(jnp.int32),
            seats,
            (w_gate, w_up, w_down),
            owns,
            pieces,
        )
        small_sum = summed[0][:, :128] + summed[0][:, 128:]
        grad_qkv = jnp.stack([summed[1 + 2 * (layers_n - 1 - l)] for l in range(layers_n)])
        grad_out = jnp.stack([summed[2 + 2 * (layers_n - 1 - l)] for l in range(layers_n)])
    else:

        def scatter(array):
            return lax.psum_scatter(array, everywhere, scatter_dimension=0, tiled=True)

        small_sum = scatter(small_grads)
        grad_qkv = jnp.stack([scatter(weight_parts[l][0]) for l in range(layers_n)])
        grad_out = jnp.stack([scatter(weight_parts[l][1]) for l in range(layers_n)])
    wide = experts_n + 2
    grad_router = jnp.stack(
        [small_sum[:, l * wide : l * wide + experts_n] for l in range(layers_n)]
    )
    grad_gains = jnp.stack(
        [
            jnp.swapaxes(small_sum[:, l * wide + experts_n : (l + 1) * wide], 0, 1)
            for l in range(layers_n)
        ]
    )
    if fast:
        grad_gate, grad_up, grad_down = experts
    else:
        grad_gate, grad_up, grad_down = [
            jnp.stack([expert_parts[l][member] for l in range(layers_n)]) for member in range(3)
        ]
    layer_outs = jnp.stack(outputs).astype(bf16)
    return (
        layer_outs,
        grad_stream,
        grad_qkv,
        grad_out,
        grad_router,
        grad_gains,
        grad_gate,
        grad_up,
        grad_down,
    )


def solution(mesh):
    return jax.shard_map(
        local,
        mesh=mesh,
        in_specs=(
            P((DP, EX), None),
            P(None, (DP, EX), None),
            P(None, (DP, EX), None),
            P(None, (DP, EX), None),
            P(None, None, (DP, EX)),
            P(None, EX, None, None),
            P(None, EX, None, None),
            P(None, EX, None, None),
            P((DP, EX), None),
            P((DP, EX)),
            P(None, (DP, EX), None),
            P(None, (DP, EX), None),
        ),
        out_specs=(
            P(None, (DP, EX), None),
            P((DP, EX), None),
            P(None, (DP, EX), None),
            P(None, (DP, EX), None),
            P(None, (DP, EX), None),
            P(None, None, (DP, EX)),
            P(None, EX, DP, None),
            P(None, EX, DP, None),
            P(None, EX, None, DP),
        ),
        check_vma=False,
    )
```

time: 2700 us -> 762 us (0.28)
  waiting for transfers between devices: 1450 us -> 11.2 us
  local copies, waits for them, and re-layouts: 589 us -> 61.6 us
  Pallas kernels: 0 us -> 521 us
  blocking collectives: 338 us -> 0 us
  matrix products: 153 us -> 68.6 us
  starting transfers between devices: 55.5 us -> 26.9 us
    reduce_scatter x8 -> x0, waiting for transfers between devices: 940 us -> none  [the longest x2 320 us: local(): lax.psum_scatter(grad_qkv_l, ('dp', 'expert'), scatter_dimension=0, tiled...]
    pallas_call x0 -> x6, Pallas kernels: none -> 521 us  [the longest x1 168 us: tail(): pl.pallas_call(partial(tail_kernel, layers_n, capacity, n_sums), out_shap...]
    unnamed x24 -> x5, waiting for transfers between devices: 381 us -> 0.75 us
    scatter x4 -> x0, local copies, waits for them, and re-layouts: 298 us -> none  [pack_rows(): return buffer.at[chosen, pair_rank].set(row_values)]
    all_gather x5 -> x0, blocking collectives: 256 us -> none  [the longest x2 136 us: fetch_weights(): lax.all_gather(w_router[layer_idx], ('dp', 'expert'), axis=0, tiled=True)]
    gather x26 -> x0, local copies, waits for them, and re-layouts: 114 us -> none  [the longest x4 22.5 us: unpack_rows(): flat_rows[gather_at]]
    dot_general x34 -> x18, matrix products: 143 us -> 58.6 us  [the longest x2 10.4 us: local(): jnp.einsum('tq,dq->td', dprojected, qkv_full, preferred_element_type=f32)]
    all_to_all x2 -> x0, blocking collectives: 82.1 us -> none  [the longest x1 41.1 us: local(): lax.all_to_all(pack_rows(dy_pairs, chosen, pair_rank, experts_n, most_row...]
  transfers between devices with their start and end apart: 33 -> 24, of which waited for: 24 -> 4; matrix products, arithmetic and copies ran while one was open for 20% -> 20% of each run, Pallas kernels for 0% -> 47%
where the time goes in v1:
time: 762 us; the launch traced here: 750 us
  Pallas kernels  521 us (68%)
  matrix products  68.6 us (9%)
  local copies, waits for them, and re-layouts  61.6 us (8%)
  other arithmetic  44.9 us (6%)
  starting transfers between devices  26.9 us (4%)
  between operations  16.3 us (2%)
  waiting for transfers between devices  11.2 us (1%)
    pallas_call x1, Pallas kernels, tail(): pl.pallas_call(partial(tail_kernel, layers_n, capacity, n_sums), out_shap...  168 us
    pallas_call x2, Pallas kernels, experts_backward(): pl.pallas_call(partial(expert_back_kernel, l, capacity, local_n * n_exper...  156 us
    pallas_call x2, Pallas kernels, experts_forward(): pl.pallas_call(partial(expert_kernel, l, capacity), out_shape=[shape((row...  115 us
    pallas_call x1, Pallas kernels, gather_all(): pl.pallas_call(partial(gather_kernel, n_arrays, n_dp), out_shape=[jax.Sha...  81.8 us
    ppermute x9, starting transfers between devices, from_behind(): lax.ppermute(value, axis, [(source, source + steps) for source in range(l...  24 us
    unnamed x290, local copies, waits for them, and re-layouts  21.8 us
  transfers between devices with their start and end apart: 24, of which 4 were waited for; matrix products, arithmetic and copies ran while one was open for 20% of the time, Pallas kernels for 47%

profile of v1, /device:TPU:8, one launch (start us, length us, event | category | flops | bytes accessed | tf_op | source)
XLA Modules:
  0.0 750.2 jit_solution(12883549727576122823)
XLA Ops:
  7.3 1.8 fusion.136
  9.1 1.8 fusion.137
  11.7 1.9 collective-permute-start.1
  18.2 81.8 %gather_all.1 = (bf16[4,8,48,128]{3,2,1,0:T(8,128)(2,1)}, s32[4,8,32,128]{3,2,1,0:T(8,128)}, bf16[4,8,48,2048]{3,2,1,0:T(8,128)(2,1)}, bf16[4,8,48,1536]{3,2,1,0:T(8,128)(2,1)}) custom-call(bf16[48,128]{1,0:T(8,128)(2,1)} %fusion.98.refs_0_, s32[32,128]{1,0:T(8,128)} %bitcast_select_fusion.2.refs_1_, bf16[48,2048]{1,0:T(8,128)(2,1)} %get-tuple-element.146.refs_2_, ...), custom_call_target="tpu_custom_call" | custom-call | tf_op jit(solution)/shard_map/gather_all/pallas_call | solution.py:254
  100.2 1.2 convert_bitcast_fusion
  101.4 1.5 slice_reduce_fusion
  103.6 3.8 fusion.146
  107.5 2.3 collective-permute-start
  111.3 2.2 collective-permute-start.2
  114.7 4.5 collective-permute-done.2
  120.7 3.4 multiply_reduce_fusion.8
  126.6 1.2 convert_reduce_fusion.1
  127.8 1.4 reduce_window_sum.11
  129.3 1.2 fusion.128
  135.0 2.0 copy.471
  137.0 1.9 dynamic-slice_bitcast_fusion.2
  140.3 60.8 %experts_forward.2 = (f32[128,1536]{1,0:T(8,128)}, bf16[576,1536]{1,0:T(8,128)(2,1)}, f32[576,768]{1,0:T(8,128)}, f32[576,768]{1,0:T(8,128)}, f32[576,1]{1,0:T(8,128)}) custom-call(bf16[128,1536]{1,0:T(8,128)(2,1)} %multiply_convert_fusion.2.normed, f32[128,1536]{1,0:T(8,128)} %copy-done.4, bf16[16,1536]{1,0:T(8,128)(2,1)} %bitcast.372, ...), custom_call_target="tpu_custom_call" | custom-call | tf_op jit(solution)/shard_map/experts_forward/pallas_call | solution.py:892
  201.1 1.3 multiply_reduce_fusion.7
  202.4 1.3 multiply_convert_fusion.1
  203.7 4.2 fusion.2
  209.5 1.9 collective-permute-start.3
  214.6 2.5 collective-permute-start.4
  219.1 3.0 collective-permute-done.4
  222.7 1.7 fusion.145
  225.3 2.1 convolution_convert_fusion.5
  227.4 3.6 multiply_reduce_fusion.6
  232.9 1.5 reshape.422.refs_6_
  234.4 1.5 copy.424
  235.9 1.9 reshape.430.refs_5_
  237.8 1.5 squeeze.55
  239.3 1.8 copy.492
  241.1 2.7 copy.472
  243.8 2.1 dynamic-slice_bitcast_fusion
  245.9 1.8 copy.412.seats
  247.7 1.4 convert_bitcast_fusion.3.hit
  249.1 1.5 pad_maximum_fusion.12.refs_4_
  251.1 1.2 fusion.124
  253.0 53.7 %experts_forward.3 = (f32[128,1536]{1,0:T(8,128)}, bf16[576,1536]{1,0:T(8,128)(2,1)}, f32[576,768]{1,0:T(8,128)}, f32[576,768]{1,0:T(8,128)}, f32[576,1]{1,0:T(8,128)}) custom-call(bf16[128,1536]{1,0:T(8,128)(2,1)} %multiply_convert_fusion.normed, f32[128,1536]{1,0:T(8,128)} %copy-done, bf16[16,1536]{1,0:T(8,128)(2,1)} %bitcast.375, ...), custom_call_target="tpu_custom_call" | custom-call | tf_op jit(solution)/shard_map/experts_forward/pallas_call | solution.py:892
  306.7 77.1 %experts_backward.2 = (f32[128,1664]{1,0:T(8,128)}, bf16[576,1536]{1,0:T(8,128)(2,1)}, bf16[576,768]{1,0:T(8,128)(2,1)}, bf16[576,768]{1,0:T(8,128)(2,1)}, bf16[576,768]{1,0:T(8,128)(2,1)}) custom-call(bf16[128,1536]{1,0:T(8,128)(2,1)} %grads, s32[2,1024]{1,0:T(2,128)} %copy.412.seats, s32[1024,2]{1,0:T(8,128)} %get-tuple-element.128.seats_turned, ...), custom_call_target="tpu_custom_call" | custom-call | tf_op jit(solution)/shard_map/experts_backward/pallas_call | solution.py:921
  384.2 1.6 select_reduce_fusion
  390.6 4.9 fusion.11
  395.4 1.9 copy.416
  398.1 1.4 convolution_bitcast_fusion.3
  400.2 3.8 collective-permute-start.6
  404.0 1.3 fusion.17
  407.0 2.3 collective-permute-start.5
  414.4 5.3 multiply_reduce_fusion.1
  420.4 1.6 fusion.132
  422.0 78.9 %experts_backward.3 = (f32[128,1664]{1,0:T(8,128)}, bf16[576,1536]{1,0:T(8,128)(2,1)}, bf16[576,768]{1,0:T(8,128)(2,1)}, bf16[576,768]{1,0:T(8,128)(2,1)}, bf16[576,768]{1,0:T(8,128)(2,1)}) custom-call(bf16[128,1536]{1,0:T(8,128)(2,1)} %get-tuple-element.122.grads.refs_3_, s32[2,1024]{1,0:T(2,128)} %copy.400.seats, ...), custom_call_target="tpu_custom_call" | custom-call | tf_op jit(solution)/shard_map/experts_backward/pallas_call | solution.py:921
  503.2 1.7 multiply_reduce_fusion.2
  506.7 4.0 convolution_convert_fusion.4
  514.1 3.9 collective-permute-start.7
  521.9 3.2 collective-permute-start.8
  525.5 1.8 collective-permute-done.8
  527.4 5.1 fusion.45
  538.9 4.8 convolution_convert_fusion.3
  544.0 4.7 convolution_convert_fusion.2
  548.7 5.5 convolution_convert_fusion.1
  554.2 4.6 convolution_convert_fusion
  558.8 168.5 %tail.1 = (f32[2,2,384,768]{3,2,1,0:T(8,128)}, f32[2,2,384,768]{3,2,1,0:T(8,128)}, f32[2,2,768,384]{3,2,1,0:T(8,128)}, bf16[4,8,128,1536]{3,2,1,0:T(8,128)(2,1)}...) custom-call(bf16[32,128,1536]{2,1,0:T(8,128)(2,1)} %bitcast.325, ...), custom_call_target="tpu_custom_call" | custom-call | tf_op jit(solution)/shard_map/tail/pallas_call | solution.py:824
  728.6 2.1 pad_maximum_fusion.2
  732.7 5.2 copy.510
  737.9 2.4 copy.511
  741.3 2.2 copy.512
  (467 shorter events, 65.5 us)
Async XLA Ops:
  7.2 6.6 copy-start.115
  7.2 6.7 copy-start.129
  7.2 6.8 copy-start.121
  7.2 7.4 copy-start.122
  7.2 196.5 %all-gather.14.cloned.1.call-start = ((), (), s32[]{:S(2)}) async-start(), calls=%async_computation.3 | async-start | bytes 6488064 | tf_op jit(solution)/shard_map/all_gather | solution.py:1240
  9.1 91.0 %copy-start.14 = (bf16[128,1536]{1,0:T(8,128)(2,1)S(1)}, bf16[128,1536]{1,0:T(8,128)(2,1)}, u32[]{:S(2)}) copy-start(bf16[128,1536]{1,0:T(8,128)(2,1)} %param.12) | copy-start | bytes 1179652
  9.1 218.3 %all-gather.16.cloned.1.call-start = ((), (), s32[]{:S(2)}) async-start(), calls=%async_computation.4 | async-start | bytes 4866048 | tf_op jit(solution)/shard_map/all_gather | solution.py:1241
  10.9 547.9 %all-gather.12.cloned.1.call-start = ((), (), s32[]{:S(2)}) async-start(), calls=%async_computation.2 | async-start | bytes 12976128 | tf_op jit(solution)/shard_map/all_gather | solution.py:1392
  11.7 547.2 %all-gather.8.cloned.1.call-start = ((), (), s32[]{:S(2)}) async-start(), calls=%async_computation | async-start | bytes 12976128 | tf_op jit(solution)/shard_map/all_gather | solution.py:1319
  11.7 102.8 %collective-permute-start.1 = (s32[128]{0:T(128)S(1)}, s32[128]{0:T(128)S(1)}, u32[]{:S(2)}, u32[]{:S(2)}) collective-permute-start(s32[128]{0:T(128)S(1)} %copy-done.125), channel_id=1, source_target_pairs={{0,1},{1,2},{2,3},{3,4},{4,5},{5,6},{6,7},{7,8},{8,9},{9,10},{10,1... | collective-permute-start | bytes 1544 | tf_op jit(solution)/shard_map/ppermute | solution.py:1113
  102.9 21.2 %copy-start.93 = (f32[1536]{0:T(1024)}, f32[1536]{0:T(1024)S(1)}, u32[]{:S(2)}) copy-start(f32[1536]{0:T(1024)S(1)} %get-tuple-element.110) | copy-start | bytes 18436
  102.9 99.5 %copy-start.96 = (f32[1536]{0:T(1024)}, f32[1536]{0:T(1024)S(1)}, u32[]{:S(2)}) copy-start(f32[1536]{0:T(1024)S(1)} %get-tuple-element.109) | copy-start | bytes 18436
  102.9 128.5 %copy-start.90 = (f32[1536]{0:T(1024)}, f32[1536]{0:T(1024)S(1)}, u32[]{:S(2)}) copy-start(f32[1536]{0:T(1024)S(1)} %get-tuple-element.108) | copy-start | bytes 18436
  107.5 12.6 %copy-start.80 = (bf16[128,256]{0,1:T(8,128)(2,1)}, bf16[128,256]{0,1:T(8,128)(2,1)S(1)}, u32[]{:S(2)}) copy-start(bf16[128,256]{0,1:T(8,128)(2,1)S(1)} %copy.483) | copy-start | bytes 196612
  107.5 12.5 %collective-permute-start = (bf16[128,2,128]{0,2,1:T(8,128)(2,1)S(1)}, bf16[128,2,128]{0,2,1:T(8,128)(2,1)S(1)}, u32[]{:S(2)}, u32[]{:S(2)}) collective-permute-start(bf16[128,2,128]{0,2,1:T(8,128)(2,1)S(1)} %bitcast.380), channel_id=1, source_target_pairs={{0,1},{1,2},{2,3},{3,4},{4,5},{5,6},{6,7},{7,8},{8,9},{9,10},{10,1... | collective-permute-start | bytes 196616 | tf_op jit(solution)/shard_map/ppermute | solution.py:1113
  111.2 8.0 %copy-start.47 = (bf16[128,2,64]{2,0,1:T(8,128)(2,1)}, bf16[128,2,64]{2,0,1:T(8,128)(2,1)S(1)}, u32[]{:S(2)}) copy-start(bf16[128,2,64]{2,0,1:T(8,128)(2,1)S(1)} %get-tuple-element.147) | copy-start | bytes 98308
  111.2 8.0 %copy-start.49 = (bf16[128,2,64]{2,0,1:T(8,128)(2,1)}, bf16[128,2,64]{2,0,1:T(8,128)(2,1)S(1)}, u32[]{:S(2)}) copy-start(bf16[128,2,64]{2,0,1:T(8,128)(2,1)S(1)} %get-tuple-element.148) | copy-start | bytes 98308
  111.3 7.9 %collective-permute-start.2 = (bf16[128,2,128]{2,0,1:T(8,128)(2,1)S(1)}, bf16[128,2,128]{2,0,1:T(8,128)(2,1)S(1)}, u32[]{:S(2)}, u32[]{:S(2)}) collective-permute-start(bf16[128,2,128]{2,0,1:T(8,128)(2,1)S(1)} %pad_maximum_fusion.13), channel_id=1, source_target_pairs={{0,1},{1,2},{2,3},{3,4},{4,5},{5,6},{6,7},{7,8},{8,9},{9,10},{10,1... | collective-permute-start | bytes 196616 | tf_op jit(solution)/shard_map/ppermute | solution.py:1113
  124.1 6.4 copy-start.4
  125.0 6.1 copy-start.6
  125.1 433.8 %all-gather.10.cloned.1.call-start = ((), (), s32[]{:S(2)}) async-start(), calls=%async_computation.1 | async-start | bytes 12976128 | tf_op jit(solution)/shard_map/all_gather | solution.py:1319
  209.5 15.2 %collective-permute-start.3 = (bf16[128,2,128]{0,2,1:T(8,128)(2,1)}, bf16[128,2,128]{0,2,1:T(8,128)(2,1)}, u32[]{:S(2)}, u32[]{:S(2)}) collective-permute-start(bf16[128,2,128]{0,2,1:T(8,128)(2,1)} %bitcast.126), channel_id=1, source_target_pairs={{0,1},{1,2},{2,3},{3,4},{4,5},{5,6},{6,7},{7,8},{8,9},{9,10},{10,1... | collective-permute-start | bytes 196616 | tf_op jit(solution)/shard_map/ppermute | solution.py:1113
  214.6 7.5 %collective-permute-start.4 = (bf16[128,2,128]{2,0,1:T(8,128)(2,1)S(1)}, bf16[128,2,128]{2,0,1:T(8,128)(2,1)S(1)}, u32[]{:S(2)}, u32[]{:S(2)}) collective-permute-start(bf16[128,2,128]{2,0,1:T(8,128)(2,1)S(1)} %pad_maximum_fusion.14), channel_id=1, source_target_pairs={{0,1},{1,2},{2,3},{3,4},{4,5},{5,6},{6,7},{7,8},{8,9},{9,10},{10,1... | collective-permute-start | bytes 196616 | tf_op jit(solution)/shard_map/ppermute | solution.py:1113
  243.8 6.7 copy-start.108
  250.5 293.2 %collective-permute-start.17 = (bf16[128,1536]{0,1:T(8,128)(2,1)}, bf16[128,1536]{0,1:T(8,128)(2,1)}, u32[]{:S(2)}, u32[]{:S(2)}) collective-permute-start(bf16[128,1536]{0,1:T(8,128)(2,1)} %bitcast.357), channel_id=1, source_target_pairs={{0,1},{1,0},{2,3},{3,2},{4,5},{5,4},{6,7},{7,6},{8,9},{9,8},{10,11... | collective-permute-start | bytes 1179656 | tf_op jit(solution)/shard_map/ppermute | solution.py:1118
  252.4 131.8 %copy-start.31 = (f32[16,128]{0,1:T(8,128)}, f32[16,128]{0,1:T(8,128)S(1)}, u32[]{:S(2)}) copy-start(f32[16,128]{0,1:T(8,128)S(1)} %fusion.124) | copy-start | bytes 24580
  252.4 285.9 %collective-permute-start.13 = (bf16[128,1536]{0,1:T(8,128)(2,1)}, bf16[128,1536]{0,1:T(8,128)(2,1)}, u32[]{:S(2)}, u32[]{:S(2)}) collective-permute-start(bf16[128,1536]{0,1:T(8,128)(2,1)} %bitcast.360), channel_id=1, source_target_pairs={{0,1},{1,0},{2,3},{3,2},{4,5},{5,4},{6,7},{7,6},{8,9},{9,8},{10,11... | collective-permute-start | bytes 1179656 | tf_op jit(solution)/shard_map/ppermute | solution.py:1118
  306.7 77.1 %copy-start.8 = (bf16[128,1536]{1,0:T(8,128)(2,1)S(1)}, bf16[128,1536]{1,0:T(8,128)(2,1)}, u32[]{:S(2)}) copy-start(bf16[128,1536]{1,0:T(8,128)(2,1)} %multiply_convert_fusion.normed) | copy-start | bytes 1179652
  390.5 148.0 %collective-permute-start.14 = (bf16[128,1536]{1,0:T(8,128)(2,1)}, bf16[128,1536]{1,0:T(8,128)(2,1)}, u32[]{:S(2)}, u32[]{:S(2)}) collective-permute-start(bf16[128,1536]{1,0:T(8,128)(2,1)} %fusion.127), channel_id=1, source_target_pairs={{0,1},{1,0},{2,3},{3,2},{4,5},{5,4},{6,7},{7,6},{8,9},{9,8},{10,11... | collective-permute-start | bytes 1179656 | tf_op jit(solution)/shard_map/ppermute | solution.py:1118
  397.3 6.7 copy-start.23
  400.2 13.2 %collective-permute-start.6 = (bf16[128,2,128]{0,2,1:T(8,128)(2,1)}, bf16[128,2,128]{0,2,1:T(8,128)(2,1)}, u32[]{:S(2)}, u32[]{:S(2)}) collective-permute-start(bf16[128,2,128]{0,2,1:T(8,128)(2,1)} %slice.440), channel_id=1, source_target_pairs={{1,0},{2,1},{3,2},{4,3},{5,4},{6,5},{7,6},{8,7},{9,8},{10,9},{11,1... | collective-permute-start | bytes 196616 | tf_op jit(solution)/shard_map/ppermute | solution.py:1113
  407.0 5.5 collective-permute-start.5
  414.3 6.0 copy-start.135
  414.3 6.0 copy-start.2
  414.3 6.0 copy-start.11
  414.4 6.0 copy-start.13
  414.4 6.0 copy-start.92
  414.4 6.0 copy-start.97
  414.4 6.0 copy-start.112
  414.4 6.0 copy-start.119
  414.4 6.0 copy-start.124
  422.0 78.9 %copy-start.33 = (f32[16,128]{0,1:T(8,128)S(1)}, f32[16,128]{0,1:T(8,128)}, u32[]{:S(2)}) copy-start(f32[16,128]{0,1:T(8,128)} %copy-done.31) | copy-start | bytes 24580
  422.0 78.9 %copy-start.114 = (f32[128]{0:T(128)S(1)}, f32[128]{0:T(128)}, u32[]{:S(2)}) copy-start(f32[128]{0:T(128)} %get-tuple-element.120) | copy-start | bytes 1540
  422.0 78.9 %copy-start.120 = (f32[128]{0:T(128)S(1)}, f32[128]{0:T(128)}, u32[]{:S(2)}) copy-start(f32[128]{0:T(128)} %fusion.89) | copy-start | bytes 1540
  422.0 81.2 %copy-start.5 = (f32[128,1536]{1,0:T(8,128)S(1)}, f32[128,1536]{1,0:T(8,128)}, u32[]{:S(2)}) copy-start(f32[128,1536]{1,0:T(8,128)} %copy-done.4) | copy-start | bytes 2359300
  422.0 81.2 %copy-start.94 = (f32[1536]{0:T(1024)S(1)}, f32[1536]{0:T(1024)}, u32[]{:S(2)}) copy-start(f32[1536]{0:T(1024)} %copy-done.93) | copy-start | bytes 18436
  422.0 81.2 %copy-start.117 = (f32[128]{0:T(128)S(1)}, f32[128]{0:T(128)}, u32[]{:S(2)}) copy-start(f32[128]{0:T(128)} %copy-done.116) | copy-start | bytes 1540
  506.7 37.3 %collective-permute-start.18 = (bf16[128,1536]{1,0:T(8,128)(2,1)S(1)}, bf16[128,1536]{1,0:T(8,128)(2,1)}, u32[]{:S(2)}, u32[]{:S(2)}) collective-permute-start(bf16[128,1536]{1,0:T(8,128)(2,1)S(1)} %get-tuple-element.118), channel_id=1, source_target_pairs={{0,1},{1,0},{2,3},{3,2},{4,5},{5,4},{6,7},{7,6},{8,9},{9,8},{10,11... | collective-permute-start | bytes 1179656 | tf_op jit(solution)/shard_map/ppermute | solution.py:1118
  513.6 6.1 copy-start.48
  513.6 6.1 copy-start.50
  513.6 6.1 copy-start.83
  514.1 7.8 %collective-permute-start.7 = (bf16[128,2,128]{2,0,1:T(8,128)(2,1)S(1)}, bf16[128,2,128]{2,0,1:T(8,128)(2,1)S(1)}, u32[]{:S(2)}, u32[]{:S(2)}) collective-permute-start(bf16[128,2,128]{2,0,1:T(8,128)(2,1)S(1)} %slice.439), channel_id=1, source_target_pairs={{1,0},{2,1},{3,2},{4,3},{5,4},{6,5},{7,6},{8,7},{9,8},{10,9},{11,1... | collective-permute-start | bytes 196616 | tf_op jit(solution)/shard_map/ppermute | solution.py:1113
  520.9 6.5 copy-start.15
  520.9 6.5 copy-start.99
  521.9 5.5 collective-permute-start.8
  525.5 7.1 copy-start.86
  527.3 7.7 %collective-permute-start.10 = (f32[1536,18]{0,1:T(8,128)}, f32[1536,18]{0,1:T(8,128)S(1)}, u32[]{:S(2)}, u32[]{:S(2)}) collective-permute-start(f32[1536,18]{0,1:T(8,128)} %pad_maximum_fusion.11), channel_id=1, source_target_pairs={{0,1},{1,0},{2,3},{3,2},{4,5},{5,4},{6,7},{7,6},{8,9},{9,8},{10,11... | collective-permute-start | bytes 331784 | tf_op jit(solution)/shard_map/ppermute | solution.py:1118
  527.4 6.0 copy-start.128
  535.0 1.6 collective-permute-start.9
  536.6 12.1 %collective-permute-start.12 = (bf16[128,2048]{0,1:T(8,128)(2,1)}, bf16[128,2048]{0,1:T(8,128)(2,1)}, u32[]{:S(2)}, u32[]{:S(2)}) collective-permute-start(bf16[128,2048]{0,1:T(8,128)(2,1)} %pad_maximum_fusion.4), channel_id=1, source_target_pairs={{0,1},{1,0},{2,3},{3,2},{4,5},{5,4},{6,7},{7,6},{8,9},{9,8},{10,11... | collective-permute-start | bytes 1572872 | tf_op jit(solution)/shard_map/ppermute | solution.py:1118
  538.3 10.3 %collective-permute-start.11 = (bf16[128,1536]{1,0:T(8,128)(2,1)S(1)}, bf16[128,1536]{1,0:T(8,128)(2,1)S(1)}, u32[]{:S(2)}, u32[]{:S(2)}) collective-permute-start(bf16[128,1536]{1,0:T(8,128)(2,1)S(1)} %copy-done.27), channel_id=1, source_target_pairs={{0,1},{1,0},{2,3},{3,2},{4,5},{5,4},{6,7},{7,6},{8,9},{9,8},{10,11... | collective-permute-start | bytes 1179656 | tf_op jit(solution)/shard_map/ppermute | solution.py:1118
  538.6 15.7 %collective-permute-start.16 = (bf16[128,2048]{0,1:T(8,128)(2,1)S(1)}, bf16[128,2048]{0,1:T(8,128)(2,1)S(1)}, u32[]{:S(2)}, u32[]{:S(2)}) collective-permute-start(bf16[128,2048]{0,1:T(8,128)(2,1)S(1)} %copy-done.72), channel_id=1, source_target_pairs={{0,1},{1,0},{2,3},{3,2},{4,5},{5,4},{6,7},{7,6},{8,9},{9,8},{10,11... | collective-permute-start | bytes 1572872 | tf_op jit(solution)/shard_map/ppermute | solution.py:1118
  543.8 10.5 %collective-permute-start.15 = (bf16[128,1536]{1,0:T(8,128)(2,1)S(1)}, bf16[128,1536]{1,0:T(8,128)(2,1)S(1)}, u32[]{:S(2)}, u32[]{:S(2)}) collective-permute-start(bf16[128,1536]{1,0:T(8,128)(2,1)S(1)} %copy-done.25), channel_id=1, source_target_pairs={{0,1},{1,0},{2,3},{3,2},{4,5},{5,4},{6,7},{7,6},{8,9},{9,8},{10,11... | collective-permute-start | bytes 1179656 | tf_op jit(solution)/shard_map/ppermute | solution.py:1118
  732.7 8.0 %slice-start = ((s8[4718592]{0:T(1024)(128)(4,1)}), s8[4194304]{0:T(1024)(128)(4,1)S(1)}, s32[]{:S(2)}) async-start(s8[4718592]{0:T(1024)(128)(4,1)} %bitcast.329), calls=%async_computation.5 | async-start | bytes 8388608
  (100 other events, 309.6 us)
Sparse Core Ops, SparseCore 0:
  11.5 89.1 all-gather.13
  103.6 68.9 all-gather.15
  175.5 99.9 all-gather.11
  278.2 118.7 all-gather.7
  399.6 118.9 all-gather.9

commit v2 on v1

--- a/solution.py
+++ b/solution.py
@@ -41,34 +41,32 @@
     return z, near
 
 
-def greet(z, near, plane, line):
+def greet(z, near, plane, line, order=None):
     barrier = pltpu.get_barrier_semaphore()
+
+    def tell(**target):
+        pl.semaphore_signal(barrier, inc=1, device_id=target, device_id_type=MESH)
+
     for name in plane:
-        pl.semaphore_signal(
-            barrier, inc=1, device_id={EX: near[name]}, device_id_type=MESH
-        )
+        tell(**{EX: near[name]})
     count = len(plane)
-    if line is None:
-        pl.semaphore_wait(barrier, count)
-        return
-
-    @pl.when(z < line - 1)
-    def up():
-        pl.semaphore_signal(barrier, inc=1, device_id={DP: z + 1}, device_id_type=MESH)
-
-    @pl.when(z > 0)
-    def down():
-        pl.semaphore_signal(barrier, inc=1, device_id={DP: z - 1}, device_id_type=MESH)
-
-    inside = (z > 0) & (z < line - 1)
-
-    @pl.when(inside)
-    def wait_inside():
-        pl.semaphore_wait(barrier, count + 2)
-
-    @pl.when(jnp.logical_not(inside))
-    def wait_end():
-        pl.semaphore_wait(barrier, count + 1)
+    links = []
+    if line is not None:
+        links += [(z < line - 1, {DP: z + 1}), (z > 0, {DP: z - 1})]
+    if order is not None:
+        behind, ahead, has_behind, has_ahead = order
+        links += [
+            (has_behind, {DP: behind[0], EX: behind[1]}),
+            (has_ahead, {DP: ahead[0], EX: ahead[1]}),
+        ]
+    for there, target in links:
+
+        @pl.when(there)
+        def one():
+            tell(**target)
+
+        count = count + jnp.where(there, 1, 0)
+    pl.semaphore_wait(barrier, count)
 
 
 def halves(rows, columns):
@@ -85,6 +83,8 @@
 
 
 KINDS = 10
+QUAD = ("own", "x", "y", "d")
+BESIDE = ("c", "cx", "cy", "cd")
 
 
 class Gather:
@@ -191,6 +191,23 @@
 
         self.first(j)
 
+    def plane_of(self, k):
+        return lax.rem(self.z + k, self.line)
+
+    def spread(self, k, rows, sem):
+        j = self.plane_of(k)
+        self.first(j, [rows.at[j]])
+        self.kept(k, rows, sem).start()
+
+    def kept(self, k, rows, sem):
+        j = self.plane_of(k)
+        return pltpu.make_async_copy(rows.at[j], self.outs[0].at[j, self.near["own"]], sem.at[k])
+
+    def spread_done(self, rows, sem):
+        for k in range(1, self.line):
+            self.finish(self.plane_of(k))
+            self.kept(k, rows, sem).wait()
+
     def line_done(self):
         z = self.z
         for step in range(self.line):
@@ -204,68 +221,6 @@
             def down_done():
                 for a in self.all:
                     self.hop(a, z + step, 9, "own", z - 1).wait_send()
-
-
-def gather_kernel(n_arrays, line, *refs):
-    ins, outs = refs[:n_arrays], refs[n_arrays : 2 * n_arrays]
-    send, recv, keep = refs[2 * n_arrays :]
-    z, near = place()
-    g = Gather(ins, outs, send, recv, z, near, line)
-    greet(z, near, ("x", "y", "c"), line)
-    local = [
-        pltpu.make_async_copy(ins[a], outs[a].at[z, near["own"]], keep.at[a])
-        for a in range(n_arrays)
-    ]
-    g.line_first()
-    g.first(z, ins)
-    for copy_here in local:
-        copy_here.start()
-    g.arrivals(1, g.take)
-    g.second(z)
-    g.arrivals(2, g.take)
-    g.third(z)
-    g.arrivals(1, g.second)
-    g.arrivals(3, g.take)
-    g.arrivals(1, g.third)
-    g.arrivals(2, g.second)
-    g.arrivals(2, g.third)
-    g.arrivals(3, g.second)
-    g.arrivals(3, g.third)
-    g.finish(z)
-    for step in range(1, line):
-        g.arrivals(step, g.finish)
-    for copy_here in local:
-        copy_here.wait()
-    g.line_done()
-
-
-def fast_mesh():
-    return lax.axis_size(DP) == 4 and lax.axis_size(EX) == 8
-
-
-def gather_all(shards, number):
-    n_dp, n_expert = lax.axis_size(DP), lax.axis_size(EX)
-    if not fast_mesh():
-        return [
-            lax.all_gather(shard, everywhere, axis=0).reshape((n_dp, n_expert) + shard.shape)
-            for shard in shards
-        ]
-    n_arrays = len(shards)
-    return pl.pallas_call(
-        partial(gather_kernel, n_arrays, n_dp),
-        out_shape=[
-            jax.ShapeDtypeStruct((n_dp, n_expert) + shard.shape, shard.dtype) for shard in shards
-        ],
-        in_specs=[pl.BlockSpec(memory_space=ANY)] * n_arrays,
-        out_specs=[pl.BlockSpec(memory_space=ANY)] * n_arrays,
-        scratch_shapes=[
-            pltpu.SemaphoreType.DMA((n_arrays, n_dp, KINDS)),
-            pltpu.SemaphoreType.DMA((n_arrays, n_dp, KINDS)),
-            pltpu.SemaphoreType.DMA((n_arrays,)),
-        ],
-        compiler_params=pltpu.CompilerParams(collective_id=number, has_side_effects=True),
-        name="gather_all",
-    )(*shards)
 
 
 def plane_gather(src, dst, send, recv, near):
@@ -399,7 +354,7 @@
 
 def seat_rows(seats, number):
     local_n, tokens_n = seats.shape
-    rows = lax.broadcasted_iota(jnp.int32, (local_n * number, tokens_n), 0)
+    rows = lax.broadcasted_iota(jnp.int32, (local_n * number, tokens_n), 0).astype(f32)
     hot = rows < 0
     for e in range(local_n):
         one = seats[e : e + 1, :]
@@ -409,7 +364,7 @@
 
 def seat_columns(seats, number):
     tokens_n, local_n = seats.shape
-    columns = lax.broadcasted_iota(jnp.int32, (tokens_n, local_n * number), 1)
+    columns = lax.broadcasted_iota(jnp.int32, (tokens_n, local_n * number), 1).astype(f32)
     hot = columns < 0
     for e in range(local_n):
         one = seats[:, e : e + 1]
@@ -423,168 +378,6 @@
     return powers / jnp.sum(powers, axis=0, keepdims=True)
 
 
-def expert_kernel(
-    layer,
-    number,
-    normed,
-    mixed,
-    router,
-    hit,
-    seats,
-    seats_turned,
-    w_gate,
-    w_up,
-    w_down,
-    new_stream,
-    rows_in,
-    gate_pre,
-    up_pre,
-    gate_seat,
-    tokens,
-    gates,
-    weighted,
-    gate_w,
-    up_w,
-    down_w,
-    weight_sem,
-    send,
-    recv,
-    *scratch,
-):
-    z, near = place()
-    local_n = seats.shape[0]
-    rows = normed.shape[0]
-    weights = [
-        pltpu.make_async_copy(src.at[layer], dst, weight_sem.at[i])
-        for i, (src, dst) in enumerate(((w_gate, gate_w), (w_up, up_w), (w_down, down_w)))
-    ]
-    greet(z, near, ("x", "y", "c"), None)
-    first, second, third, finish = plane_gather(normed, tokens, send, recv, near)
-    first()
-    for one in weights:
-        one.start()
-    second()
-    third()
-    finish()
-    everyone = tokens[...].reshape(-1, tokens.shape[2])
-    gates[...] = masked_gates(mul(router[...], everyone, LAST), hit[...] > 0)
-    pick = seat_rows(seats[...], number)
-    for e in range(local_n):
-        here = pl.ds(e * number, number)
-        mine = gates[pl.ds(lax.axis_index(EX) * local_n + e, 1), :]
-        gate_seat[here] = jnp.sum(
-            pick[e * number : (e + 1) * number].astype(f32) * mine, axis=1, keepdims=True
-        )
-    rows_in[...] = mul(pick, everyone).astype(bf16)
-    for one in weights:
-        one.wait()
-
-    def expert(e, carry):
-        here = pl.ds(pl.multiple_of(e * number, 32), number)
-        x = rows_in[here]
-        gate = mul(x, gate_w[e])
-        up = mul(x, up_w[e])
-        gate_pre[here] = gate
-        up_pre[here] = up
-        hidden = (gate * (1.0 / (1.0 + jnp.exp(-gate))) * up).astype(bf16)
-        weighted[here] = (mul(hidden, down_w[e]) * gate_seat[here]).astype(bf16)
-        return carry
-
-    lax.fori_loop(0, local_n, expert, 0)
-
-    def make(name):
-        d = near[name]
-        back = seat_columns(seats_turned[pl.ds(pl.multiple_of(d * rows, rows), rows)], number)
-        scratch[0][d] = mul(back, weighted[...]).astype(bf16)
-
-    plane_sum(make, new_stream, mixed, scratch, near)
-
-
-def expert_back_kernel(
-    layer,
-    number,
-    experts_n,
-    grads,
-    seats,
-    seats_turned,
-    gate_pre,
-    up_pre,
-    gate_seat,
-    w_gate,
-    w_up,
-    w_down,
-    summed,
-    rows_grad,
-    hidden_low,
-    dgate_low,
-    dup_low,
-    tokens,
-    back_rows,
-    gate_w,
-    up_w,
-    down_w,
-    weight_sem,
-    send,
-    recv,
-    *scratch,
-):
-    z, near = place()
-    local_n = seats.shape[0]
-    rows, width = grads.shape
-    weights = [
-        pltpu.make_async_copy(src.at[layer], dst, weight_sem.at[i])
-        for i, (src, dst) in enumerate(((w_gate, gate_w), (w_up, up_w), (w_down, down_w)))
-    ]
-    greet(z, near, ("x", "y", "c"), None)
-    first, second, third, finish = plane_gather(grads, tokens, send, recv, near)
-    first()
-    for one in weights:
-        one.start()
-    second()
-    third()
-    finish()
-    everyone = tokens[...].reshape(-1, tokens.shape[2])
-    picked = mul(seat_rows(seats[...], number), everyone)
-    back_rows[:, pl.ds(0, width)] = picked.astype(bf16)
-    rows_grad[...] = (picked * gate_seat[...]).astype(bf16)
-    for one in weights:
-        one.wait()
-
-    def expert(e, carry):
-        here = pl.ds(pl.multiple_of(e * number, 32), number)
-        gate, up = gate_pre[here], up_pre[here]
-        raw = mul(back_rows[here, pl.ds(0, width)], down_w[e], LAST)
-        sigmoid = 1.0 / (1.0 + jnp.exp(-gate))
-        silu = gate * sigmoid
-        hidden = (silu * up).astype(bf16)
-        hidden_low[here] = hidden
-        dgate_seat = jnp.sum(hidden.astype(f32) * raw, axis=1, keepdims=True)
-        raw = raw * gate_seat[here]
-        dgate = (raw * up * sigmoid * (1.0 + gate * (1.0 - sigmoid))).astype(bf16)
-        dup = (raw * silu).astype(bf16)
-        dgate_low[here] = dgate
-        dup_low[here] = dup
-        back_rows[here, pl.ds(0, width)] = (
-            mul(dgate, gate_w[e], LAST) + mul(dup, up_w[e], LAST)
-        ).astype(bf16)
-        high = dgate_seat.astype(bf16).astype(f32)
-        lane = lax.broadcasted_iota(jnp.int32, (number, 128), 1)
-        mine = lax.axis_index(EX) * local_n + e
-        back_rows[here, pl.ds(width, 128)] = jnp.where(
-            lane == mine, high, jnp.where(lane == experts_n + mine, dgate_seat - high, 0.0)
-        ).astype(bf16)
-        return carry
-
-    lax.fori_loop(0, local_n, expert, 0)
-
-    def make(name):
-        d = near[name]
-        back = seat_columns(seats_turned[pl.ds(pl.multiple_of(d * rows, rows), rows)], number)
-        scratch[0][d] = mul(back, back_rows[...]).astype(bf16)
-
-    plane_sum(make, summed, None, scratch, near)
-
-
 def tail_kernel(layers_n, number, n_sums, *refs):
     refs = list(refs)
 
@@ -595,11 +388,12 @@
 
     tokens_all, grads_all = some(layers_n), some(layers_n - 1)
     (own_shard,) = some(1)
-    routers, hit, seats = some(3)
+    table, hit, seats = some(3)
     w_gate, w_up, w_down = some(3)
     owns = [some(5) for l in range(layers_n)]
     parts = some(n_sums)
     grad_gate, grad_up, grad_down, landing = some(4)
+    beside = some(layers_n)
     sums = some(n_sums)
     (
         tokens,
@@ -623,7 +417,9 @@
         out_sem,
         gather_send,
         gather_recv,
-    ) = some(21)
+        beside_send,
+        beside_recv,
+    ) = some(23)
     held = [some(6) for a in range(n_sums)]
     z, near = place()
     n_dp, local_n = seats.shape[1], seats.shape[2]
@@ -638,19 +434,41 @@
     def layer_of(i):
         return layers_n - 1 - i // per_layer
 
+    def across(l, j):
+        return pltpu.make_async_remote_copy(
+            src_ref=tokens_all[l].at[j],
+            dst_ref=beside[l].at[j],
+            send_sem=beside_send.at[l, j],
+            recv_sem=beside_recv.at[l, j],
+            device_id={EX: near["c"]},
+            device_id_type=MESH,
+        )
+
+    def start(one):
+        one.start()
+
+    def wait(one):
+        one.wait()
+
     def fetch(i, slot, act):
         j = lax.rem(z + 1 + lax.rem(i, per_expert), n_dp)
         for l in range(layers_n):
 
             @pl.when(layer_of(i) == l)
             def of_layer():
-                tokens_from = tokens_all[l].at[pl.ds(j * 8, 8)]
-                if l == 0:
-                    grads_from = landing.at[j]
-                else:
-                    grads_from = grads_all[l - 1].at[pl.ds(j * 8, 8)]
-                act(pltpu.make_async_copy(tokens_from, tokens.at[slot], token_sem.at[slot, 0]))
-                act(pltpu.make_async_copy(grads_from, grads.at[slot], token_sem.at[slot, 1]))
+                if act is start:
+
+                    @pl.when(lax.rem(i, per_layer) < per_expert)
+                    def arrived():
+                        across(l, j).wait_recv()
+
+                for source, names, base in ((tokens_all[l], QUAD, 0), (beside[l], BESIDE, 4)):
+                    for q, name in enumerate(names):
+                        dst = tokens.at[slot, near[name]]
+                        sem = token_sem.at[slot, base + q]
+                        act(pltpu.make_async_copy(source.at[j, q], dst, sem))
+                grads_from = (landing if l == 0 else grads_all[l - 1]).at[j]
+                act(pltpu.make_async_copy(grads_from, grads.at[slot], token_sem.at[slot, 8]))
 
     def weights(l, e):
         return [
@@ -681,12 +499,6 @@
                 for one in make(l, e):
                     act(one)
 
-    def start(one):
-        one.start()
-
-    def wait(one):
-        one.wait()
-
     def results(l, e):
         return [
             pltpu.make_async_copy(stage_wide.at[0], grad_gate.at[l, e], out_sem.at[0]),
@@ -696,6 +508,9 @@
 
     greet(z, near, ("x", "y", "c"), n_dp)
     gather.line_first()
+    for l in reversed(range(layers_n)):
+        for k in range(1, n_dp):
+            across(l, lax.rem(z + k, n_dp)).start()
     total.at(3, total.first)
     total.at(2, total.first)
     of(0, weights, start)
@@ -750,7 +565,9 @@
 
         fetch(i, slot, wait)
         everyone = tokens[slot].reshape(-1, tokens.shape[3])
-        gates[...] = masked_gates(mul(routers[l], everyone, LAST), hit[l, j] > 0)
+        experts_n = hit.shape[2]
+        router = table[pl.ds(pl.multiple_of(l * experts_n, experts_n), experts_n), :].astype(bf16)
+        gates[...] = masked_gates(mul(router, everyone, LAST), hit[l, j] > 0)
         pick = seat_rows(seats[l, j, pl.ds(e, 1)], number)
         rows_in[...] = mul(pick, everyone).astype(bf16)
         rows_grad[...] = mul(pick, grads[slot].reshape(-1, tokens.shape[3])).astype(bf16)
@@ -809,10 +626,15 @@
     for distance in (3, 2, 1, 0):
         total.at(distance, total.finish)
     gather.line_done()
+    for l in range(layers_n):
+        for k in range(1, n_dp):
+            across(l, lax.rem(z + k, n_dp)).wait_send()
     of(steps - 1, results, wait)
 
 
-def tail(capacity, number, tokens_all, grads_all, own_shard, routers, hit, seats, weights, owns, parts):
+def tail(
+    capacity, number, tokens_all, grads_all, own_shard, table, hit, seats, weights, owns, parts
+):
     layers_n, n_dp, local_n, group_rows = seats.shape
     n_expert = lax.axis_size(EX)
     rows, width = own_shard.shape
@@ -829,9 +651,10 @@
             shape((layers_n, local_n, hidden, part), f32),
             shape((n_dp, n_expert, rows, width), bf16),
         ]
+        + [shape(tokens_all[0].shape, bf16)] * layers_n
         + [shape(one.shape[2:], f32) for one in parts],
         in_specs=[HBM] * (2 * layers_n) + [VMEM] * 3 + [HBM] * (3 + len(flat) + n_sums),
-        out_specs=[HBM] * 4 + [VMEM] * n_sums,
+        out_specs=[HBM] * (4 + layers_n) + [VMEM] * n_sums,
         scratch_shapes=[
             pltpu.VMEM((2, n_expert, rows, width), bf16),
             pltpu.VMEM((2, n_expert, rows, width), bf16),
@@ -849,95 +672,716 @@
             pltpu.VMEM((2, part, hidden), f32),
             pltpu.VMEM((hidden, part), f32),
             pltpu.SemaphoreType.DMA((3,)),
-            pltpu.SemaphoreType.DMA((2, 2)),
+            pltpu.SemaphoreType.DMA((2, 9)),
             pltpu.SemaphoreType.DMA((5,)),
             pltpu.SemaphoreType.DMA((3,)),
             pltpu.SemaphoreType.DMA((1, n_dp, KINDS)),
             pltpu.SemaphoreType.DMA((1, n_dp, KINDS)),
+            pltpu.SemaphoreType.DMA((layers_n, n_dp)),
+            pltpu.SemaphoreType.DMA((layers_n, n_dp)),
         ]
         + sums_scratch([one.shape[2:] for one in parts], n_dp),
         compiler_params=settings(number),
         name="tail",
-    )(*tokens_all, *grads_all, own_shard, routers, hit, seats, *weights, *flat, *parts)
-    return results[:3], results[4:]
-
-
-def expert_scratch(n_expert, rows, local_n, width, hidden):
-    return [
+    )(*tokens_all, *grads_all, own_shard, table, hit, seats, *weights, *flat, *parts)
+    return results[:3], results[4 + layers_n :]
+
+
+VMEM = pl.BlockSpec(memory_space=pltpu.VMEM)
+HBM = pl.BlockSpec(memory_space=ANY)
+
+
+def settings(number):
+    return pltpu.CompilerParams(
+        collective_id=number, has_side_effects=True, vmem_limit_bytes=62 << 20
+    )
+
+
+def chain(z, e, line):
+    n_expert = 8
+    behind = (z - jnp.where(e == 0, 1, 0), lax.rem(e + n_expert - 1, n_expert))
+    ahead = (z + jnp.where(e == n_expert - 1, 1, 0), lax.rem(e + 1, n_expert))
+    has_behind = (z > 0) | (e > 0)
+    has_ahead = (z < line - 1) | (e < n_expert - 1)
+    return behind, ahead, has_behind, has_ahead
+
+
+def normalized(value, gain):
+    scale = lax.rsqrt(jnp.mean(value * value, axis=-1, keepdims=True) + epsilon)
+    return value * scale * gain
+
+
+def turn(head, cosine, signed_sine):
+    return head * cosine + pltpu.roll(head, HEAD_SIZE // 2, 1) * signed_sine
+
+
+def head_of(h):
+    return pl.ds(h * HEAD_SIZE, HEAD_SIZE)
+
+
+def allowed_keys(rk, row, z, e, behind, has_behind, seg_column):
+    own = rk[z, e, pl.ds(row, 1), :]
+    first = rk[jnp.where(has_behind, behind[0], z), behind[1], pl.ds(row, 1), :]
+    rows = seg_column.shape[0]
+    query = lax.broadcasted_iota(jnp.int32, (rows, rows), 0)
+    key = lax.broadcasted_iota(jnp.int32, (rows, rows), 1)
+    reach = jnp.where(has_behind, 0, -1)
+    return jnp.concatenate(
+        [(first == seg_column) & (key >= rows * -reach), (own == seg_column) & (key <= query)],
+        axis=1,
+    )
+
+
+def head_probs(query, keys, allowed):
+    scores = mul(query, keys, LAST) * (1.0 / math.sqrt(HEAD_SIZE))
+    scores = jnp.where(allowed, scores, masked_score)
+    powers = jnp.exp(scores - jnp.max(scores, axis=-1, keepdims=True))
+    return powers / jnp.sum(powers, axis=-1, keepdims=True)
+
+
+def forward_kernel(layer, layers_n, number, *refs):
+    first = layer == 0
+    refs = list(refs)
+
+    def some(count):
+        taken = refs[:count]
+        del refs[:count]
+        return taken
+
+    stream, cosine, sine, seg_column = some(4)
+    if first:
+        small, ranks, w_qkv, w_out = some(4)
+    else:
+        table, rk, hit, seats, turned, cross_from, qkv_from, out_from = some(8)
+    w_gate, w_up, w_down = some(3)
+    new_stream, layer_out, normed_a, queries, kv_out, attended, mixed, normed_b = some(8)
+    rows_in, gate_pre, up_pre, gate_seat, quad = some(5)
+    if first:
+        table, rk_out, hit, seats, turned, qkv_out, out_out, qkv_next, out_next = some(9)
+        small_land, rk, seat_all = some(3)
+    else:
+        (cross_to,) = some(1)
+    (
+        qkv,
+        w_o,
+        kv,
+        projected,
+        tokens,
+        gates,
+        weighted,
+        gate_w,
+        up_w,
+        down_w,
+        weight_sem,
+        load_sem,
+        chain_sem,
+        quad_sem,
+        send,
+        recv,
+    ) = some(16)
+    if first:
+        send_0, recv_0, send_1, recv_1, send_2, recv_2, send_3, recv_3, keep = some(9)
+    else:
+        cross_send, cross_recv, cross_keep = some(3)
+    scratch = refs
+    z, near = place()
+    e = near["own"]
+    line = lax.axis_size(DP)
+    local_n = seats.shape[2]
+    rows = stream.shape[0]
+    experts_n = hit.shape[2]
+    behind, ahead, has_behind, has_ahead = chain(z, e, line)
+
+    weights = [
+        pltpu.make_async_copy(src.at[layer], dst, weight_sem.at[i])
+        for i, (src, dst) in enumerate(((w_gate, gate_w), (w_up, up_w), (w_down, down_w)))
+    ]
+    greet(z, near, ("x", "y", "c"), line, (behind, ahead, has_behind, has_ahead))
+    if not first:
+        cross = Gather([cross_from.at[0]], [cross_to], cross_send, cross_recv, z, near, line)
+        cross.spread(1, cross_from, cross_keep)
+    if first:
+        g0 = Gather([small, ranks], [small_land, rk], send_0, recv_0, z, near, line)
+        g1 = Gather([w_qkv.at[0]], [qkv], send_1, recv_1, z, near, line)
+        g2 = Gather([w_out.at[0]], [w_o], send_2, recv_2, z, near, line)
+        g3 = Gather(
+            [w_qkv.at[1], w_out.at[1]], [qkv_next, out_next], send_3, recv_3, z, near, line
+        )
+        local = [
+            pltpu.make_async_copy(one, g.outs[i].at[z, e], keep.at[k])
+            for k, (g, i, one) in enumerate(
+                (g, i, one) for g in (g0, g1, g2, g3) for i, one in enumerate(g.ins)
+            )
+        ]
+        g0.line_first()
+        g0.first(z, g0.ins)
+        g1.line_first()
+        g1.first(z, g1.ins)
+        for one in local:
+            one.start()
+        g0.arrivals(1, g0.take)
+        g0.second(z)
+        g0.arrivals(2, g0.take)
+        g0.third(z)
+        g0.arrivals(1, g0.second)
+        g0.arrivals(3, g0.take)
+        g1.arrivals(1, g1.take)
+        g2.line_first()
+        g2.first(z, g2.ins)
+        g0.arrivals(1, g0.third)
+        g0.arrivals(2, g0.second)
+        g1.second(z)
+        g0.arrivals(2, g0.third)
+        g0.arrivals(3, g0.second)
+        g1.arrivals(2, g1.take)
+        g0.arrivals(3, g0.third)
+        g0.finish(z)
+        for step in range(1, line):
+            g0.arrivals(step, g0.finish)
+        local[0].wait()
+        local[1].wait()
+        table[...] = jnp.transpose(small_land[...].reshape(-1, 128).astype(f32))
+        g1.third(z)
+        g1.arrivals(1, g1.second)
+        for g in range(line):
+            before = jnp.zeros((layers_n * experts_n, 1), f32)
+            for d in range(8):
+                lanes = pl.ds(d * rows, rows)
+                rank = rk[g, d, pl.ds(0, layers_n * experts_n), :].astype(f32)
+                seat_all[g, :, lanes] = jnp.where(rank > 0, rank + before, 0.0)
+                for l in range(layers_n):
+                    hit[l, g, :, lanes] = rank[l * experts_n : (l + 1) * experts_n]
+                here = jnp.where(rank > 0, 1.0, 0.0)
+                before = before + jnp.sum(here, axis=1, keepdims=True)
+            for l in range(layers_n):
+                for k in range(local_n):
+                    row = pl.ds(l * experts_n + e * local_n + k, 1)
+                    seats[l, g, pl.ds(k, 1), :] = seat_all[g, row, :]
+        g1.arrivals(3, g1.take)
+        wide = jnp.zeros((rows - layers_n * local_n, rows), f32)
+        for d in range(8):
+            lanes = pl.ds(d * rows, rows)
+            mine = [seats[l, z, :, lanes] for l in range(layers_n)]
+            turned[lanes, :] = jnp.transpose(jnp.concatenate(mine + [wide], axis=0))
+        rk_out[...] = rk[...]
+        g1.arrivals(1, g1.third)
+        g1.arrivals(2, g1.second)
+        g2.arrivals(1, g2.take)
+        g1.arrivals(2, g1.third)
+        g1.arrivals(3, g1.second)
+        g2.second(z)
+        g2.arrivals(2, g2.take)
+        g1.arrivals(3, g1.third)
+        g2.third(z)
+        g1.finish(z)
+        for step in range(1, line):
+            g1.arrivals(step, g1.finish)
+        local[2].wait()
+        g2.arrivals(1, g2.second)
+        g2.arrivals(3, g2.take)
+    else:
+        loads = [
+            pltpu.make_async_copy(qkv_from, qkv, load_sem.at[0]),
+            pltpu.make_async_copy(out_from, w_o, load_sem.at[1]),
+        ]
+        for one in loads:
+            one.start()
+    for one in weights:
+        one.start()
+    gain = 2 * experts_n + 2 * layer
+    x = stream[...].astype(f32)
+    normed_a[...] = normalized(x, table[pl.ds(gain, 1), :]).astype(bf16)
+    if not first:
+        loads[0].wait()
+    width = queries.shape[1]
+    projected[...] = mul(normed_a[...], qkv[...].reshape(width, -1))
+    keys_n = KEY_VALUE_HEADS * HEAD_SIZE
+    cos, sin = cosine[...], sine[...]
+    for h in range(KEY_VALUE_HEADS):
+        key = turn(projected[:, head_of(QUERY_HEADS + h)], cos, sin)
+        kv[1, :, head_of(h)] = key.astype(bf16)
+    kv[1, :, pl.ds(keys_n, keys_n)] = projected[:, pl.ds(width + keys_n, keys_n)].astype(bf16)
+
+    def pass_on(target):
+        return pltpu.make_async_remote_copy(
+            src_ref=kv.at[1],
+            dst_ref=kv.at[0],
+            send_sem=chain_sem.at[0],
+            recv_sem=chain_sem.at[1],
+            device_id={DP: target[0], EX: target[1]},
+            device_id_type=MESH,
+        )
+
+    @pl.when(has_ahead)
+    def pass_ahead():
+        pass_on(ahead).start()
+
+    if first:
+        g2.arrivals(1, g2.third)
+        g2.arrivals(2, g2.second)
+        g3.line_first()
+        g3.first(z, g3.ins)
+    else:
+        cross.spread(2, cross_from, cross_keep)
+    for h in range(QUERY_HEADS):
+        queries[:, head_of(h)] = turn(projected[:, head_of(h)], cos, sin).astype(bf16)
+    allowed = allowed_keys(rk, layers_n * experts_n, z, e, behind, has_behind, seg_column[...])
+
+    @pl.when(has_behind)
+    def from_behind_here():
+        pass_on(behind).wait_recv()
+
+    @pl.when(jnp.logical_not(has_behind))
+    def nobody_behind():
+        kv[0] = jnp.zeros_like(kv[0])
+
+    for h in range(QUERY_HEADS):
+        group = h // (QUERY_HEADS // KEY_VALUE_HEADS)
+        keys = kv[:, :, head_of(group)].reshape(2 * rows, HEAD_SIZE)
+        values = kv[:, :, head_of(KEY_VALUE_HEADS + group)].reshape(2 * rows, HEAD_SIZE)
+        probs = head_probs(queries[:, head_of(h)], keys, allowed).astype(bf16)
+        attended[:, head_of(h)] = mul(probs, values).astype(bf16)
+        if first and h == 3:
+            g2.arrivals(2, g2.third)
+            g2.arrivals(3, g2.second)
+        if first and h == 7:
+            g2.arrivals(3, g2.third)
+            g3.arrivals(1, g3.take)
+        if not first and h == 3:
+            cross.second(cross.plane_of(1))
+        if not first and h == 9:
+            cross.second(cross.plane_of(2))
+            cross.third(cross.plane_of(1))
+    kv_out[...] = kv[...]
+    if first:
+        g2.finish(z)
+        for step in range(1, line):
+            g2.arrivals(step, g2.finish)
+        local[3].wait()
+    else:
+        loads[1].wait()
+    mixed[...] = x + mul(attended[...], w_o[...].reshape(width, -1))
+    normed_b[...] = normalized(mixed[...], table[pl.ds(gain + 1, 1), :]).astype(bf16)
+
+    one, two, three, four = plane_gather(normed_b, tokens, send, recv, near)
+    one()
+    if first:
+        g3.second(z)
+        g3.arrivals(2, g3.take)
+    two()
+    three()
+    if first:
+        g3.third(z)
+        g3.arrivals(1, g3.second)
+        g3.arrivals(3, g3.take)
+    four()
+    quads = [
+        pltpu.make_async_copy(tokens.at[near[name]], quad.at[i], quad_sem.at[i])
+        for i, name in enumerate(QUAD)
+    ]
+    for copied in quads:
+        copied.start()
+    everyone = tokens[...].reshape(-1, width)
+    router = table[pl.ds(layer * experts_n, experts_n), :].astype(bf16)
+    gates[...] = masked_gates(mul(router, everyone, LAST), hit[layer, z] > 0)
+    pick = seat_rows(seats[layer, z], number)
+    for k in range(local_n):
+        here = pl.ds(k * number, number)
+        mine = gates[pl.ds(e * local_n + k, 1), :]
+        gate_seat[here] = jnp.sum(
+            pick[k * number : (k + 1) * number].astype(f32) * mine, axis=1, keepdims=True
+        )
+    rows_in[...] = mul(pick, everyone).astype(bf16)
+    for copied in weights:
+        copied.wait()
+    if first:
+        g3.arrivals(1, g3.third)
+        g3.arrivals(2, g3.second)
+    else:
+        cross.spread(3, cross_from, cross_keep)
+
+    def expert(k, carry):
+        here = pl.ds(pl.multiple_of(k * number, 32), number)
+        x = rows_in[here]
+        gate = mul(x, gate_w[k])
+        up = mul(x, up_w[k])
+        gate_pre[here] = gate
+        up_pre[here] = up
+        hidden = (gate * (1.0 / (1.0 + jnp.exp(-gate))) * up).astype(bf16)
+        weighted[here] = (mul(hidden, down_w[k]) * gate_seat[here]).astype(bf16)
+        return carry
+
+    lax.fori_loop(0, local_n, expert, 0)
+    if first:
+        g3.arrivals(2, g3.third)
+        g3.arrivals(3, g3.second)
+        out_copies = [
+            pltpu.make_async_copy(qkv, qkv_out, load_sem.at[0]),
+            pltpu.make_async_copy(w_o, out_out, load_sem.at[1]),
+        ]
+        for copied in out_copies:
+            copied.start()
+    else:
+        cross.second(cross.plane_of(3))
+        cross.third(cross.plane_of(2))
+
+    def make(name):
+        d = near[name]
+        lanes = pl.ds(pl.multiple_of(d * rows, rows), rows)
+        mine = turned[lanes, pl.ds(layer * local_n, local_n)]
+        scratch[0][d] = mul(seat_columns(mine, number), weighted[...]).astype(bf16)
+
+    plane_sum(make, new_stream, mixed, scratch, near)
+    layer_out[...] = new_stream[...].astype(bf16)
+
+    for copied in quads:
+        copied.wait()
+
+    @pl.when(has_ahead)
+    def passed_on():
+        pass_on(ahead).wait_send()
+
+    if first:
+        g3.arrivals(3, g3.third)
+        g3.finish(z)
+        for step in range(1, line):
+            g3.arrivals(step, g3.finish)
+        for copied in local[4:] + out_copies:
+            copied.wait()
+        for g in (g0, g1, g2, g3):
+            g.line_done()
+    else:
+        cross.third(cross.plane_of(3))
+        cross.spread_done(cross_from, cross_keep)
+
+
+def layer_forward(layer, number, shapes, stream, tables, given, weights):
+    layers_n, n_dp, n_expert, local_n, capacity = shapes
+    first = layer == 0
+    rows, width = stream.shape
+    hidden = weights[0].shape[3]
+    experts_n = local_n * n_expert
+    seats_n = local_n * capacity
+    keys_n = KEY_VALUE_HEADS * HEAD_SIZE
+    group = n_expert * rows
+    cut_rows = width // (n_dp * n_expert)
+    shape = jax.ShapeDtypeStruct
+    outs = [
+        shape((rows, width), f32),
+        shape((rows, width), bf16),
+        shape((rows, width), bf16),
+        shape((rows, width), bf16),
+        shape((2, rows, 2 * keys_n), bf16),
+        shape((rows, width), bf16),
+        shape((rows, width), f32),
+        shape((rows, width), bf16),
+        shape((seats_n, width), bf16),
+        shape((seats_n, hidden), f32),
+        shape((seats_n, hidden), f32),
+        shape((seats_n, 1), f32),
+        shape((len(QUAD), rows, width), bf16),
+    ]
+    specs = [VMEM] * 12 + [HBM]
+    scratch = []
+    full_qkv = (n_dp, n_expert, cut_rows, width + 2 * keys_n)
+    full_out = (n_dp, n_expert, cut_rows, width)
+    if first:
+        rank_rows = given[1].shape[0]
+        outs += [
+            shape((128, width), f32),
+            shape((n_dp, n_expert, rank_rows, rows), jnp.int32),
+            shape((layers_n, n_dp, experts_n, group), f32),
+            shape((layers_n, n_dp, local_n, group), f32),
+            shape((group, 128), f32),
+        ]
+        outs += [shape(full_qkv, bf16), shape(full_out, bf16)] * 2
+        specs += [VMEM] * 5 + [HBM] * 4
+        scratch += [
+            pltpu.VMEM((n_dp, n_expert, cut_rows, 128), bf16),
+            pltpu.VMEM((n_dp, n_expert, rank_rows, rows), jnp.int32),
+            pltpu.VMEM((n_dp, layers_n * experts_n, group), f32),
+        ]
+    else:
+        outs.append(shape((n_dp, n_expert, rows, width), bf16))
+        specs.append(HBM)
+    scratch += [
+        pltpu.VMEM(full_qkv, bf16),
+        pltpu.VMEM(full_out, bf16),
+        pltpu.VMEM((2, rows, 2 * keys_n), bf16),
+        pltpu.VMEM((rows, width + 2 * keys_n), f32),
+        pltpu.VMEM((n_expert, rows, width), bf16),
+        pltpu.VMEM((experts_n, group), f32),
+        pltpu.VMEM((seats_n, width), bf16),
         pltpu.VMEM((local_n, width, hidden), bf16),
         pltpu.VMEM((local_n, width, hidden), bf16),
         pltpu.VMEM((local_n, hidden, width), bf16),
         pltpu.SemaphoreType.DMA((3,)),
+        pltpu.SemaphoreType.DMA((2,)),
+        pltpu.SemaphoreType.DMA((2,)),
+        pltpu.SemaphoreType.DMA((len(QUAD),)),
         pltpu.SemaphoreType.DMA((8,)),
         pltpu.SemaphoreType.DMA((8,)),
     ]
-
-
-VMEM = pl.BlockSpec(memory_space=pltpu.VMEM)
-HBM = pl.BlockSpec(memory_space=ANY)
-
-
-def settings(number):
-    return pltpu.CompilerParams(
-        collective_id=number, has_side_effects=True, vmem_limit_bytes=60 << 20
-    )
-
-
-def experts_forward(l, capacity, number, normed, mixed, router, hit, seats, weights):
-    rows, width = normed.shape
-    local_n, hidden = weights[0].shape[1], weights[0].shape[3]
-    n_expert = lax.axis_size(EX)
+    if first:
+        for count in (2, 1, 1, 2):
+            scratch += [pltpu.SemaphoreType.DMA((count, n_dp, KINDS)) for i in range(2)]
+        scratch.append(pltpu.SemaphoreType.DMA((6,)))
+    else:
+        scratch += [pltpu.SemaphoreType.DMA((1, n_dp, KINDS)) for i in range(2)]
+        scratch.append(pltpu.SemaphoreType.DMA((n_dp,)))
+    given_specs = [HBM] * 4 if first else [VMEM] * 5 + [HBM] * 3
+    return pl.pallas_call(
+        partial(forward_kernel, layer, layers_n, capacity),
+        out_shape=outs,
+        in_specs=[VMEM] * 4 + given_specs + [HBM] * 3,
+        out_specs=specs,
+        scratch_shapes=scratch + sum_scratch(rows, width),
+        compiler_params=settings(number),
+        name="layer_forward",
+    )(stream, *tables, *given, *weights)
+
+
+def norm_back(value, gain, grad):
+    scale = lax.rsqrt(jnp.mean(value * value, axis=-1, keepdims=True) + epsilon)
+    unit = value * scale
+    inner = grad * gain
+    back = scale * (inner - unit * jnp.mean(inner * unit, axis=-1, keepdims=True))
+    return back, jnp.sum(grad * unit, axis=0, keepdims=True)
+
+
+def backward_kernel(layer, layers_n, number, *refs):
+    refs = list(refs)
+
+    def some(count):
+        taken = refs[:count]
+        del refs[:count]
+        return taken
+
+    grad_stream, stream, cosine, sine, seg_column = some(5)
+    mixed, normed_b, queries, kv, gate_pre, up_pre, gate_seat = some(7)
+    table, rk, hit, seats, turned = some(5)
+    qkv_from, out_from, w_gate, w_up, w_down = some(5)
+    grad_out, grad_low, rows_grad, hidden_low, dgate_low, dup_low = some(6)
+    dprojected, grad_attn, small = some(3)
+    (
+        summed,
+        qkv,
+        w_o,
+        datt,
+        dkv,
+        dkv_send,
+        dkv_got,
+        tokens,
+        back_rows,
+        gate_w,
+        up_w,
+        down_w,
+        weight_sem,
+        load_sem,
+        chain_sem,
+        send,
+        recv,
+    ) = some(17)
+    scratch = refs
+    z, near = place()
+    e = near["own"]
+    line = lax.axis_size(DP)
+    local_n = seats.shape[2]
+    rows, width = stream.shape
+    experts_n = hit.shape[2]
+    behind, ahead, has_behind, has_ahead = chain(z, e, line)
+    weights = [
+        pltpu.make_async_copy(src.at[layer], dst, weight_sem.at[i])
+        for i, (src, dst) in enumerate(((w_gate, gate_w), (w_up, up_w), (w_down, down_w)))
+    ]
+    loads = [
+        pltpu.make_async_copy(qkv_from, qkv, load_sem.at[0]),
+        pltpu.make_async_copy(out_from, w_o, load_sem.at[1]),
+    ]
+    grad_low[...] = grad_stream[...].astype(bf16)
+    greet(z, near, ("x", "y", "c"), None, (behind, ahead, has_behind, has_ahead))
+
+    first, second, third, finish = plane_gather(grad_low, tokens, send, recv, near)
+    first()
+    for one in weights + loads:
+        one.start()
+    second()
+    third()
+    finish()
+    everyone = tokens[...].reshape(-1, width)
+    picked = mul(seat_rows(seats[layer, z], number), everyone)
+    back_rows[:, pl.ds(0, width)] = picked.astype(bf16)
+    rows_grad[...] = (picked * gate_seat[...]).astype(bf16)
+    for one in weights:
+        one.wait()
+
+    def expert(k, carry):
+        here = pl.ds(pl.multiple_of(k * number, 32), number)
+        gate, up = gate_pre[here], up_pre[here]
+        raw = mul(back_rows[here, pl.ds(0, width)], down_w[k], LAST)
+        sigmoid = 1.0 / (1.0 + jnp.exp(-gate))
+        silu = gate * sigmoid
+        hidden = (silu * up).astype(bf16)
+        hidden_low[here] = hidden
+        dgate_seat = jnp.sum(hidden.astype(f32) * raw, axis=1, keepdims=True)
+        raw = raw * gate_seat[here]
+        dgate = (raw * up * sigmoid * (1.0 + gate * (1.0 - sigmoid))).astype(bf16)
+        dup = (raw * silu).astype(bf16)
+        dgate_low[here] = dgate
+        dup_low[here] = dup
+        back_rows[here, pl.ds(0, width)] = (
+            mul(dgate, gate_w[k], LAST) + mul(dup, up_w[k], LAST)
+        ).astype(bf16)
+        high = dgate_seat.astype(bf16).astype(f32)
+        lane = lax.broadcasted_iota(jnp.int32, (number, 128), 1)
+        mine = e * local_n + k
+        back_rows[here, pl.ds(width, 128)] = jnp.where(
+            lane == mine, high, jnp.where(lane == experts_n + mine, dgate_seat - high, 0.0)
+        ).astype(bf16)
+        return carry
+
+    lax.fori_loop(0, local_n, expert, 0)
+
+    def make(name):
+        d = near[name]
+        lanes = pl.ds(pl.multiple_of(d * rows, rows), rows)
+        mine = turned[lanes, pl.ds(layer * local_n, local_n)]
+        scratch[0][d] = mul(seat_columns(mine, number), back_rows[...]).astype(bf16)
+
+    plane_sum(make, summed, None, scratch, near)
+
+    over = ((0,), (0,))
+    gain = 2 * experts_n + 2 * layer
+    router = table[pl.ds(layer * experts_n, experts_n), :].astype(bf16)
+    own_lanes = pl.ds(pl.multiple_of(e * rows, rows), rows)
+    gates = masked_gates(mul(router, normed_b[...], LAST), hit[layer, z, :, own_lanes] > 0)
+    turned_sum = jnp.transpose(summed[:, pl.ds(width, 128)])
+    dgates = turned_sum[:experts_n] + turned_sum[experts_n : 2 * experts_n]
+    inner = jnp.sum(gates * dgates, axis=0, keepdims=True)
+    dlogits = (gates * (dgates - inner)).astype(bf16)
+    small[pl.ds(0, experts_n)] = mul(dlogits, normed_b[...])
+    dnormed = summed[:, pl.ds(0, width)] + mul(dlogits, router, over)
+    back, dgain = norm_back(mixed[...], table[pl.ds(gain + 1, 1), :], dnormed)
+    small[pl.ds(experts_n + 1, 1)] = dgain
+    dmixed = grad_stream[...].astype(f32) + back
+    grad_out[...] = dmixed
+    grad_attn[...] = dmixed.astype(bf16)
+
+    loads[1].wait()
+    datt[...] = mul(grad_attn[...], w_o[...].reshape(width, -1), LAST).astype(bf16)
+    allowed = allowed_keys(rk, layers_n * experts_n, z, e, behind, has_behind, seg_column[...])
+    cos, sin = cosine[...], sine[...]
+    per_group = QUERY_HEADS // KEY_VALUE_HEADS
+    scale = 1.0 / math.sqrt(HEAD_SIZE)
+    for group in range(KEY_VALUE_HEADS):
+        keys = kv[:, :, head_of(group)].reshape(2 * rows, HEAD_SIZE)
+        values = kv[:, :, head_of(KEY_VALUE_HEADS + group)].reshape(2 * rows, HEAD_SIZE)
+        dkeys = jnp.zeros((2 * rows, HEAD_SIZE), f32)
+        dvalues = jnp.zeros((2 * rows, HEAD_SIZE), f32)
+        for h in range(group * per_group, (group + 1) * per_group):
+            query = queries[:, head_of(h)]
+            probs = head_probs(query, keys, allowed)
+            given = datt[:, head_of(h)]
+            dprobs = mul(given, values, LAST)
+            delta = jnp.sum(probs * dprobs, axis=-1, keepdims=True)
+            dscores = (probs * (dprobs - delta)).astype(bf16)
+            dquery = mul(dscores, keys) * scale
+            dprojected[:, head_of(h)] = turn(dquery, cos, -sin).astype(bf16)
+            dkeys = dkeys + mul(dscores, query, over)
+            dvalues = dvalues + mul(probs.astype(bf16), given, over)
+        dkv[:, head_of(group)] = dkeys * scale
+        dkv[:, head_of(KEY_VALUE_HEADS + group)] = dvalues
+    dkv_send[...] = dkv[pl.ds(0, rows)].astype(bf16)
+
+    def pass_on(target):
+        return pltpu.make_async_remote_copy(
+            src_ref=dkv_send,
+            dst_ref=dkv_got,
+            send_sem=chain_sem.at[0],
+            recv_sem=chain_sem.at[1],
+            device_id={DP: target[0], EX: target[1]},
+            device_id_type=MESH,
+        )
+
+    @pl.when(has_behind)
+    def pass_back():
+        pass_on(behind).start()
+
+    loads[0].wait()
+    query_part = pl.ds(0, width)
+    key_part = pl.ds(width, dkv.shape[1])
+    weights_q = qkv[:, :, :, query_part].reshape(-1, width)
+    dnormed = mul(dprojected[:, query_part], weights_q, LAST)
+
+    @pl.when(has_ahead)
+    def from_ahead_here():
+        pass_on(ahead).wait_recv()
+        dkv[pl.ds(rows, rows)] += dkv_got[...].astype(f32)
+
+    for h in range(KEY_VALUE_HEADS):
+        dkey = turn(dkv[pl.ds(rows, rows), head_of(h)], cos, -sin)
+        dprojected[:, head_of(QUERY_HEADS + h)] = dkey.astype(bf16)
+        dvalue = dkv[pl.ds(rows, rows), head_of(KEY_VALUE_HEADS + h)]
+        dprojected[:, head_of(QUERY_HEADS + KEY_VALUE_HEADS + h)] = dvalue.astype(bf16)
+    weights_kv = qkv[:, :, :, key_part].reshape(-1, dkv.shape[1])
+    dnormed = dnormed + mul(dprojected[:, key_part], weights_kv, LAST)
+    back, dgain = norm_back(stream[...].astype(f32), table[pl.ds(gain, 1), :], dnormed)
+    small[pl.ds(experts_n, 1)] = dgain
+    grad_out[...] += back
+
+    @pl.when(has_behind)
+    def passed_back():
+        pass_on(behind).wait_send()
+
+
+def layer_backward(layer, number, shapes, grads, stream, tables, saved, plan, weights):
+    layers_n, n_dp, n_expert, local_n, capacity = shapes
+    rows, width = stream.shape
+    hidden = weights[-1].shape[2]
+    experts_n = local_n * n_expert
     seats_n = local_n * capacity
+    keys_n = KEY_VALUE_HEADS * HEAD_SIZE
+    cut_rows = width // (n_dp * n_expert)
     shape = jax.ShapeDtypeStruct
+    outs = [
+        shape((rows, width), f32),
+        shape((rows, width), bf16),
+        shape((seats_n, width), bf16),
+        shape((seats_n, hidden), bf16),
+        shape((seats_n, hidden), bf16),
+        shape((seats_n, hidden), bf16),
+        shape((rows, width + 2 * keys_n), bf16),
+        shape((rows, width), bf16),
+        shape((experts_n + 2, width), f32),
+    ]
+    scratch = [
+        pltpu.VMEM((rows, width + 128), f32),
+        pltpu.VMEM((n_dp, n_expert, cut_rows, width + 2 * keys_n), bf16),
+        pltpu.VMEM((n_dp, n_expert, cut_rows, width), bf16),
+        pltpu.VMEM((rows, width), bf16),
+        pltpu.VMEM((2 * rows, 2 * keys_n), f32),
+        pltpu.VMEM((rows, 2 * keys_n), bf16),
+        pltpu.VMEM((rows, 2 * keys_n), bf16),
+        pltpu.VMEM((n_expert, rows, width), bf16),
+        pltpu.VMEM((seats_n, width + 128), bf16),
+        pltpu.VMEM((local_n, width, hidden), bf16),
+        pltpu.VMEM((local_n, width, hidden), bf16),
+        pltpu.VMEM((local_n, hidden, width), bf16),
+        pltpu.SemaphoreType.DMA((3,)),
+        pltpu.SemaphoreType.DMA((2,)),
+        pltpu.SemaphoreType.DMA((2,)),
+        pltpu.SemaphoreType.DMA((8,)),
+        pltpu.SemaphoreType.DMA((8,)),
+    ]
     return pl.pallas_call(
-        partial(expert_kernel, l, capacity),
-        out_shape=[
-            shape((rows, width), f32),
-            shape((seats_n, width), bf16),
-            shape((seats_n, hidden), f32),
-            shape((seats_n, hidden), f32),
-            shape((seats_n, 1), f32),
-        ],
-        in_specs=[VMEM] * 6 + [HBM] * 3,
-        out_specs=[VMEM] * 5,
-        scratch_shapes=[
-            pltpu.VMEM((n_expert, rows, width), bf16),
-            pltpu.VMEM((local_n * n_expert, n_expert * rows), f32),
-            pltpu.VMEM((seats_n, width), bf16),
-        ]
-        + expert_scratch(n_expert, rows, local_n, width, hidden)
-        + sum_scratch(rows, width),
+        partial(backward_kernel, layer, layers_n, capacity),
+        out_shape=outs,
+        in_specs=[VMEM] * 17 + [HBM] * 5,
+        out_specs=[VMEM] * 9,
+        scratch_shapes=scratch + sum_scratch(rows, width + 128),
         compiler_params=settings(number),
-        name="experts_forward",
-    )(normed, mixed, router, hit, seats, seats.T, *weights)
-
-
-def experts_backward(l, capacity, number, grads, seats, gate_pre, up_pre, gate_seat, weights):
-    rows, width = grads.shape
-    local_n, hidden = weights[0].shape[1], weights[0].shape[3]
-    n_expert = lax.axis_size(EX)
-    seats_n = local_n * capacity
-    shape = jax.ShapeDtypeStruct
-    return pl.pallas_call(
-        partial(expert_back_kernel, l, capacity, local_n * n_expert),
-        out_shape=[
-            shape((rows, width + 128), f32),
-            shape((seats_n, width), bf16),
-            shape((seats_n, hidden), bf16),
-            shape((seats_n, hidden), bf16),
-            shape((seats_n, hidden), bf16),
-        ],
-        in_specs=[VMEM] * 6 + [HBM] * 3,
-        out_specs=[VMEM] * 5,
-        scratch_shapes=[
-            pltpu.VMEM((n_expert, rows, width), bf16),
-            pltpu.VMEM((seats_n, width + 128), bf16),
-        ]
-        + expert_scratch(n_expert, rows, local_n, width, hidden)
-        + sum_scratch(rows, width + 128),
-        compiler_params=settings(number),
-        name="experts_backward",
-    )(grads, seats, seats.T, gate_pre, up_pre, gate_seat, *weights)
+        name="layer_backward",
+    )(grads, stream, *tables, *saved, *plan, *weights)
 
 
 class Sums:
@@ -1183,6 +1627,127 @@
     return powers / jnp.sum(powers, axis=0, keepdims=True)
 
 
+def local_chips(
+    tokens,
+    w_qkv,
+    w_out,
+    w_router,
+    norm_gains,
+    w_gate,
+    w_up,
+    w_down,
+    out_grad,
+    segment_ids,
+    routes,
+    pair_order,
+):
+    token_rows = tokens.shape[0]
+    layers_n = w_qkv.shape[0]
+    topk_n = routes.shape[2]
+    n_expert = lax.axis_size(EX)
+    n_dp = lax.axis_size(DP)
+    local_n = w_gate.shape[1]
+    experts_n = local_n * n_expert
+    capacity = 9 * n_expert * token_rows * topk_n // (8 * experts_n)
+    shapes = (layers_n, n_dp, n_expert, local_n, capacity)
+    positions = lax.axis_index(EX) * token_rows + jnp.arange(token_rows, dtype=jnp.int32)
+    cosine, sine = rotary_tables(positions)
+    tables = (
+        jnp.concatenate([cosine, cosine], axis=-1)[:, 0],
+        jnp.concatenate([-sine, sine], axis=-1)[:, 0],
+        segment_ids[:, None],
+    )
+    ranks = rank_table(routes, pair_order, experts_n).reshape(layers_n * experts_n, token_rows)
+    ranks = jnp.concatenate([ranks, segment_ids[None], jnp.zeros((7, token_rows), jnp.int32)])
+    small = jnp.concatenate(
+        [w_router[l] for l in range(layers_n)]
+        + [jnp.swapaxes(norm_gains.reshape(2 * layers_n, -1), 0, 1)],
+        axis=1,
+    )
+    small = jnp.pad(small, ((0, 0), (0, 128 - small.shape[1])))
+    experts = (w_gate, w_up, w_down)
+
+    def along_line(rows):
+        return lax.all_gather(rows, DP, axis=0)
+
+    saved, outputs, normed_all, streams = [], [], [], [tokens]
+    for l in range(layers_n):
+        given = (small, ranks, w_qkv, w_out) if l == 0 else (*plan, along_line(out_grad), *full[l])
+        results = layer_forward(l, 1 + l, shapes, streams[l], tables, given, experts)
+        if l == 0:
+            plan = results[13:18]
+            full = [results[18:20], results[20:22]]
+        else:
+            grads_all = [results[13]]
+        streams.append(results[0])
+        outputs.append(results[1])
+        saved.append(results[2:12])
+        normed_all.append(along_line(results[12]))
+
+    grads = out_grad
+    owns, parts, smalls = [None] * layers_n, [None] * layers_n, [None] * layers_n
+    for l in reversed(range(layers_n)):
+        normed_a, queries, kv, attended, mixed, normed_b, rows_in = saved[l][:7]
+        kept = (mixed, normed_b, queries, kv, *saved[l][7:])
+        sources = (*full[l], *experts)
+        results = layer_backward(
+            l, 4 + l, shapes, grads, streams[l], tables, kept, plan, sources
+        )
+        grads, own_shard = results[:2]
+        owns[l] = (rows_in, *results[2:6])
+        dprojected, grad_attn, small_grad = results[6:9]
+        other = from_sibling((normed_a, attended, dprojected, grad_attn))
+        pairs = [
+            jnp.concatenate([own, sib], axis=0)
+            for own, sib in zip((normed_a, attended, dprojected, grad_attn), other)
+        ]
+        parts[l] = [
+            lax.dot_general(
+                one, another, (((0,), (0,)), ((), ())), preferred_element_type=f32
+            ).astype(bf16)
+            for one, another in ((pairs[0], pairs[2]), (pairs[1], pairs[3]))
+        ]
+        smalls[l] = small_grad + from_sibling(small_grad)
+    cut_shape = (n_dp, n_expert, D // (n_dp * n_expert))
+    wide = experts_n + 2
+    small_grads = jnp.pad(jnp.concatenate(smalls), ((0, 128 - layers_n * wide), (0, 0))).T
+    high = small_grads.astype(bf16)
+    low = (small_grads - high.astype(f32)).astype(bf16)
+    pieces = [jnp.concatenate([high, low], axis=1).reshape(cut_shape + (256,))]
+    for l in reversed(range(layers_n)):
+        pieces += [part.reshape(cut_shape + (-1,)) for part in parts[l]]
+    table, rk, hit, seats, turned = plan
+    grad_experts, summed = tail(
+        capacity,
+        8,
+        normed_all,
+        grads_all,
+        own_shard,
+        table,
+        hit,
+        seats,
+        experts,
+        owns,
+        pieces,
+    )
+    small_sum = summed[0][:, :128] + summed[0][:, 128:]
+    grad_qkv = jnp.stack([summed[1 + 2 * (layers_n - 1 - l)] for l in range(layers_n)])
+    grad_out = jnp.stack([summed[2 + 2 * (layers_n - 1 - l)] for l in range(layers_n)])
+    small_sum = small_sum[:, : layers_n * wide].reshape(-1, layers_n, wide)
+    small_sum = jnp.swapaxes(small_sum, 0, 1)
+    grad_router = small_sum[:, :, :experts_n]
+    grad_gains = jnp.swapaxes(small_sum[:, :, experts_n:], 1, 2)
+    return (
+        jnp.stack(outputs),
+        grads,
+        grad_qkv,
+        grad_out,
+        grad_router,
+        grad_gains,
+        *grad_experts,
+    )
+
+
 def local(
     tokens,
     w_qkv,
@@ -1197,7 +1762,6 @@
     routes,
     pair_order,
 ):
-    fast = fast_mesh()
     token_rows = tokens.shape[0]
     layers_n = w_qkv.shape[0]
     topk_n = routes.shape[2]
@@ -1231,9 +1795,10 @@
         axis=1,
     )
     small = jnp.pad(small, ((0, 0), (0, 128 - small.shape[1])))
-    small_full, ranks_full, qkv_0, out_0 = gather_all(
-        [small, ranks.reshape(layers_n * experts_n, token_rows), w_qkv[0], w_out[0]], 1
-    )
+    small_full, ranks_full, qkv_0, out_0 = [
+        lax.all_gather(one, everywhere, axis=0)
+        for one in (small, ranks.reshape(layers_n * experts_n, token_rows), w_qkv[0], w_out[0])
+    ]
     qkv_fulls = [qkv_0.reshape(D, -1)]
     out_fulls = [out_0.reshape(query_width, D)]
     for layer_idx in range(1, layers_n):
@@ -1246,10 +1811,8 @@
     routers = [small_full[:, l * experts_n : (l + 1) * experts_n] for l in range(layers_n)]
     routers_turned = [jnp.swapaxes(router, 0, 1) for router in routers]
     ranks_full = ranks_full.reshape(n_dp, n_expert, layers_n, experts_n, token_rows)
-    if not fast:
-        ranks_full = lax.dynamic_slice_in_dim(ranks_full, dp_here, 1, 0)
+    ranks_full = lax.dynamic_slice_in_dim(ranks_full, dp_here, 1, 0)
     groups = ranks_full.shape[0]
-    own_group = dp_here if fast else 0
     hit_all = jnp.transpose(ranks_full > 0, (2, 0, 3, 1, 4)).reshape(
         layers_n, groups, experts_n, group_rows
     )
@@ -1261,7 +1824,7 @@
     seat_ids = jnp.arange(1, capacity + 1, dtype=jnp.int32)
 
     def own_of(array):
-        return lax.dynamic_index_in_dim(array, own_group, 0, keepdims=False)
+        return lax.dynamic_index_in_dim(array, 0, 0, keepdims=False)
 
     def seat_map(l):
         return (seats[l][:, :, None, :] == seat_ids[:, None]).astype(bf16)
@@ -1313,23 +1876,8 @@
         mixed_sum = stream + jnp.dot(attended, out_full, preferred_element_type=f32)
         normed_b = rms_norm(mixed_sum, gains[2 * l + 1]).astype(bf16)
 
-        kept = {}
-        if fast:
-            if fast:
-                normed_all = lax.all_gather(normed_b, everywhere, axis=0, tiled=True)
-                kept["normed_all"] = normed_all.reshape(-1, token_rows, D)
-            new_stream, *kept["own"] = experts_forward(
-                l,
-                capacity,
-                12 + l,
-                normed_b,
-                mixed_sum,
-                routers_turned[l],
-                own_of(hit_all[l]).astype(jnp.int32),
-                own_of(seats[l]),
-                (w_gate, w_up, w_down),
-            )
-        else:
+        if True:
+            kept = {}
             group_normed = lax.all_gather(normed_b, EX, axis=0, tiled=True)
             kept["normed_all"] = group_normed[None]
             seat_own = own_of(seat_map(l))
@@ -1373,29 +1921,7 @@
         record = saved_layers[l]
         qkv_full, out_full = qkv_fulls[l], out_fulls[l]
         grad_low = grad_stream.astype(bf16)
-        if fast:
-            rows_in, gate_pre, up_pre, gate_seat = record["own"]
-            summed, rows_grad, hidden_low, dgate_low, dup_low = experts_backward(
-                l,
-                capacity,
-                16 + l,
-                grad_low,
-                own_of(seats[l]),
-                gate_pre,
-                up_pre,
-                gate_seat,
-                (w_gate, w_up, w_down),
-            )
-        if fast:
-            if l == layers_n - 1:
-                grads_all = [
-                    lax.all_gather(out_grad, everywhere, axis=0, tiled=True).reshape(
-                        -1, token_rows, D
-                    )
-                ]
-            owns[l] = (rows_in, rows_grad, hidden_low, dgate_low, dup_low)
-            own_shard = grad_low
-        else:
+        if True:
             normed_all = record["normed_all"]
             grad_all = lax.all_gather(grad_low, EX, axis=0, tiled=True)[None]
             seat_all = seat_map(l)
@@ -1430,7 +1956,7 @@
                 "esa,esb->eab", by_expert(one), by_expert(other), preferred_element_type=f32
             )
 
-        if not fast:
+        if True:
             grad_gate_l = outer(rows_in, dgate_low)
             grad_up_l = outer(rows_in, dup_low)
             grad_down_l = outer(hidden_low, rows_grad)
@@ -1445,10 +1971,7 @@
             ).astype(f32)
             expert_parts[l] = (grad_gate_l, grad_up_l, grad_down_l)
 
-        if fast:
-            dnormed_b = summed[:, :D]
-            dgates = summed[:, D : D + experts_n] + summed[:, D + experts_n : D + 2 * experts_n]
-        else:
+        if True:
             dexpert_in = (
                 jnp.einsum("egsf,edf->egsd", dgate_low, w_gate[l], preferred_element_type=f32)
                 + jnp.einsum("egsf,edf->egsd", dup_low, w_up[l], preferred_element_type=f32)
@@ -1539,44 +2062,12 @@
             axis=1,
         )
         normed_a, attended = record["normed_a"], record["attended"]
-        if fast:
-            other = from_sibling((normed_a, attended, dprojected, grad_attn))
-            normed_a, attended, dprojected, grad_attn = [
-                jnp.concatenate([own, sib], axis=0)
-                for own, sib in zip((normed_a, attended, dprojected, grad_attn), other)
-            ]
-            small_grad = small_grad + from_sibling(small_grad)
         grad_qkv_l = jnp.einsum("td,tq->dq", normed_a, dprojected, preferred_element_type=f32)
         grad_out_l = jnp.einsum("tq,td->qd", attended, grad_attn, preferred_element_type=f32)
         weight_parts[l] = (grad_qkv_l, grad_out_l, small_grad)
 
     small_grads = jnp.concatenate([weight_parts[l][2] for l in range(layers_n)], axis=1)
-    if fast:
-        shape = (n_dp, n_expert, D // (n_dp * n_expert))
-        small_grads = jnp.pad(small_grads, ((0, 0), (0, 128 - small_grads.shape[1])))
-        high = small_grads.astype(bf16)
-        low = (small_grads - high.astype(f32)).astype(bf16)
-        pieces = [jnp.concatenate([high, low], axis=1).reshape(shape + (256,))]
-        for l in reversed(range(layers_n)):
-            pieces.append(weight_parts[l][0].astype(bf16).reshape(shape + (-1,)))
-            pieces.append(weight_parts[l][1].astype(bf16).reshape(shape + (-1,)))
-        experts, summed = tail(
-            capacity,
-            20,
-            [record["normed_all"] for record in saved_layers],
-            grads_all,
-            own_shard,
-            jnp.stack(routers_turned),
-            hit_all.astype(jnp.int32),
-            seats,
-            (w_gate, w_up, w_down),
-            owns,
-            pieces,
-        )
-        small_sum = summed[0][:, :128] + summed[0][:, 128:]
-        grad_qkv = jnp.stack([summed[1 + 2 * (layers_n - 1 - l)] for l in range(layers_n)])
-        grad_out = jnp.stack([summed[2 + 2 * (layers_n - 1 - l)] for l in range(layers_n)])
-    else:
+    if True:
 
         def scatter(array):
             return lax.psum_scatter(array, everywhere, scatter_dimension=0, tiled=True)
@@ -1594,9 +2085,7 @@
             for l in range(layers_n)
         ]
     )
-    if fast:
-        grad_gate, grad_up, grad_down = experts
-    else:
+    if True:
         grad_gate, grad_up, grad_down = [
             jnp.stack([expert_parts[l][member] for l in range(layers_n)]) for member in range(3)
         ]
@@ -1615,8 +2104,9 @@
 
 
 def solution(mesh):
+    sizes = (mesh.shape[DP], mesh.shape[EX])
     return jax.shard_map(
-        local,
+        local_chips if sizes == (4, 8) else local,
         mesh=mesh,
         in_specs=(
             P((DP, EX), None),

time: 762 us -> 648 us (0.85)
  matrix products: 68.6 us -> 18.6 us
  Pallas kernels: 521 us -> 567 us
  local copies, waits for them, and re-layouts: 61.6 us -> 19.6 us
  other arithmetic: 44.9 us -> 9.54 us
  starting transfers between devices: 26.9 us -> 5.61 us
  waiting for transfers between devices: 11.2 us -> 0.76 us
    dot_general x30 -> x4, matrix products: 68.6 us -> 18.6 us  [local_chips(): lax.dot_general(one, another, (((0,), (0,)), ((), ())), preferred_element...]
    pallas_call x5 -> x4, Pallas kernels: 352 us -> 397 us  [the longest x2 254 us: layer_forward(): pl.pallas_call(partial(forward_kernel, layer, layers_n, capacity), out_sh...]
    ppermute x9 -> x0, starting transfers between devices: 24 us -> none  [from_behind(): lax.ppermute(value, axis, [(source, source + steps) for source in range(l...]
    convert_element_type x17 -> x2, other arithmetic: 14.1 us -> 0.08 us  [the longest x1 0.04 us: local_chips(): low = (small_grads - high.astype(f32)).astype(bf16)]
    unnamed x290 -> x36, local copies, waits for them, and re-layouts: 21.8 us -> 11.9 us
    ppermute x9 -> x0, waiting for transfers between devices: 9.4 us -> none  [from_behind(): lax.ppermute(value, axis, [(source, source + steps) for source in range(l...]
    squeeze x6 -> x0, local copies, waits for them, and re-layouts: 8.9 us -> none  [the longest x2 4.69 us: local(): seats[l]]
    slice x21 -> x4, local copies, waits for them, and re-layouts: 10.2 us -> 2.26 us  [the longest x1 0.86 us: local_chips(): small_sum = summed[0][:, :128] + summed[0][:, 128:]]
  transfers between devices with their start and end apart: 24 -> 13, of which waited for: 4 -> 0; matrix products, arithmetic and copies ran while one was open for 20% -> 5% of each run, Pallas kernels for 47% -> 62%
where the time goes in v2:
time: 648 us; the launch traced here: 636 us
  Pallas kernels  567 us (88%)
  local copies, waits for them, and re-layouts  19.6 us (3%)
  matrix products  18.6 us (3%)
  between operations  14.5 us (2%)
  other arithmetic  9.54 us (1%)
    pallas_call x2, Pallas kernels, layer_forward(): pl.pallas_call(partial(forward_kernel, layer, layers_n, capacity), out_sh...  254 us
    pallas_call x1, Pallas kernels, tail(): pl.pallas_call(partial(tail_kernel, layers_n, capacity, n_sums), out_shap...  170 us
    pallas_call x2, Pallas kernels, layer_backward(): pl.pallas_call(partial(backward_kernel, layer, layers_n, capacity), out_s...  143 us
    dot_general x4, matrix products, local_chips(): lax.dot_general(one, another, (((0,), (0,)), ((), ())), preferred_element...  18.6 us
  transfers between devices with their start and end apart: 13, of which 0 were waited for; matrix products, arithmetic and copies ran while one was open for 5% of the time, Pallas kernels for 62%

profile of v2, /device:TPU:8, one launch (start us, length us, event | category | flops | bytes accessed | tf_op | source)
XLA Modules:
  0.0 635.9 jit_solution(8780341848460710139)
XLA Ops:
  7.2 0.0 all-gather.7.cloned.1.call-start
  7.2 0.7 all-gather.7.cloned.1.call-update
  7.9 0.0 all-gather.9.cloned.1.call-start
  8.0 0.1 pad.38.clone
  8.0 0.1 eq.140
  8.1 0.7 reduce
  8.8 0.7 fusion.41
  9.5 0.1 copy.57
  9.6 0.1 copy.58
  9.7 0.8 copy.50
  10.5 1.4 copy.51.refs_3_.refs_4_
  11.9 0.1 reshape.223
  12.1 0.4 slice_reduce_fusion.3
  12.4 0.8 fusion.42
  13.3 0.7 convert_reduce_fusion
  14.0 0.1 bitcast_select_fusion
  14.1 0.7 fusion.35.refs_4_
  14.8 0.3 fusion.29
  15.1 0.8 maximum_bitcast_fusion
  15.9 1.3 add_add_fusion.refs_5_
  17.2 156.1 %layer_forward.2 = (f32[128,1536]{1,0:T(8,128)}, bf16[128,1536]{1,0:T(8,128)(2,1)}, bf16[128,1536]{1,0:T(8,128)(2,1)}, bf16[128,1536]{1,0:T(8,128)(2,1)}, bf16[2...) custom-call(bf16[128,1536]{1,0:T(8,128)(2,1)} %refs_1_.1, ...), custom_call_target="tpu_custom_call" | custom-call | tf_op jit(solution)/shard_map/layer_forward/pallas_call | solution.py:1133
  173.3 0.0 all-gather.9.cloned.1.call-update
  173.4 0.0 all-gather.11.cloned.1.call-start
  173.4 0.0 all-gather.7.cloned.1.call-done
  173.4 97.7 %layer_forward.3 = (f32[128,1536]{1,0:T(8,128)}, bf16[128,1536]{1,0:T(8,128)(2,1)}, bf16[128,1536]{1,0:T(8,128)(2,1)}, bf16[128,1536]{1,0:T(8,128)(2,1)}, bf16[2...) custom-call(f32[128,1536]{1,0:T(8,128)} %get-tuple-element.70.refs_0, ...), custom_call_target="tpu_custom_call" | custom-call | tf_op jit(solution)/shard_map/layer_forward/pallas_call | solution.py:1133
  271.1 0.0 all-gather.11.cloned.1.call-update
  271.2 0.5 collective-permute-start.8
  271.6 74.8 %layer_backward.2 = (f32[128,1536]{1,0:T(8,128)}, bf16[128,1536]{1,0:T(8,128)(2,1)}, bf16[576,1536]{1,0:T(8,128)(2,1)}, bf16[576,768]{1,0:T(8,128)(2,1)}, bf16[5...) custom-call(bf16[128,1536]{1,0:T(8,128)(2,1)} %refs_0_.3, ...), custom_call_target="tpu_custom_call" | custom-call | tf_op jit(solution)/shard_map/layer_backward/pallas_call | solution.py:1376
  346.5 68.5 %layer_backward.3 = (f32[128,1536]{1,0:T(8,128)}, bf16[128,1536]{1,0:T(8,128)(2,1)}, bf16[576,1536]{1,0:T(8,128)(2,1)}, bf16[576,768]{1,0:T(8,128)(2,1)}, bf16[5...) custom-call(f32[128,1536]{1,0:T(8,128)} %get-tuple-element.86.refs_0, ...), custom_call_target="tpu_custom_call" | custom-call | tf_op jit(solution)/shard_map/layer_backward/pallas_call | solution.py:1376
  415.0 2.9 collective-permute-start
  417.9 0.1 collective-permute-start.1
  418.0 0.9 pad_maximum_fusion
  419.0 0.4 collective-permute-start.9
  419.4 0.1 collective-permute-start.5
  419.5 0.4 collective-permute-start.4
  419.9 0.9 add.38
  420.9 0.0 collective-permute-done.1
  420.9 0.2 collective-permute-start.3
  421.2 0.1 pad_maximum_fusion.1
  421.2 1.2 copy.55
  422.4 0.0 collective-permute-done.5
  422.4 0.4 collective-permute-start.2
  422.8 0.2 collective-permute-start.7
  423.0 5.0 convolution_convert_fusion.3
  428.0 0.3 collective-permute-start.6
  428.4 0.0 collective-permute-done.9
  428.4 4.7 convolution_convert_fusion.2
  433.1 0.0 collective-permute-done.2
  433.1 0.0 collective-permute-done.3
  433.1 4.5 convolution_convert_fusion.1
  437.6 4.4 convolution_convert_fusion
  442.0 170.1 %tail.1 = (f32[2,2,384,768]{3,2,1,0:T(8,128)}, f32[2,2,384,768]{3,2,1,0:T(8,128)}, f32[2,2,768,384]{3,2,1,0:T(8,128)}, bf16[4,8,128,1536]{3,2,1,0:T(8,128)(2,1)}...) custom-call(bf16[4,4,128,1536]{3,2,1,0:T(8,128)(2,1)} %bitcast.91, ...), custom_call_target="tpu_custom_call" | custom-call | tf_op jit(solution)/shard_map/tail/pallas_call | solution.py:646
  612.1 0.9 fusion.40
  613.0 0.1 copy.56
  613.1 0.6 slice_bitcast_fusion
  613.7 0.6 slice.70
  614.3 2.0 pad_maximum_fusion.2
  616.3 0.9 pad_maximum_fusion.3
  617.2 0.9 copy.63
  618.1 5.2 copy.64
  623.3 2.4 copy.65
  625.7 0.4 slice-done
  626.1 0.6 slice-done.1
  626.6 2.2 copy.66
  (47 shorter events, 0.2 us)
Async XLA Ops:
  7.2 166.2 %all-gather.7.cloned.1.call-start = ((), (), s32[]{:S(2)}) async-start(), calls=%async_computation | async-start | bytes 1966080 | tf_op jit(solution)/shard_map/all_gather | solution.py:1671
  7.9 434.1 %all-gather.9.cloned.1.call-start = ((), (), s32[]{:S(2)}) async-start(), calls=%async_computation.1 | async-start | bytes 7864320 | tf_op jit(solution)/shard_map/all_gather | solution.py:1671
  173.4 268.6 %all-gather.11.cloned.1.call-start = ((), (), s32[]{:S(2)}) async-start(), calls=%async_computation.2 | async-start | bytes 7864320 | tf_op jit(solution)/shard_map/all_gather | solution.py:1671
  173.4 97.7 %copy-start.11 = (bf16[128,1536]{1,0:T(8,128)(2,1)S(1)}, bf16[128,1536]{1,0:T(8,128)(2,1)}, u32[]{:S(2)}) copy-start(bf16[128,1536]{1,0:T(8,128)(2,1)} %get-tuple-element.119) | copy-start | bytes 1179652
  271.2 156.8 %collective-permute-start.8 = (bf16[128,1536]{1,0:T(8,128)(2,1)S(1)}, bf16[128,1536]{1,0:T(8,128)(2,1)}, u32[]{:S(2)}, u32[]{:S(2)}) collective-permute-start(bf16[128,1536]{1,0:T(8,128)(2,1)S(1)} %copy-done.11), channel_id=1, source_target_pairs={{0,1},{1,0},{2,3},{3,2},{4,5},{5,4},{6,7},{7,6},{8,9},{9,8},{10,11... | collective-permute-start | bytes 1179656 | tf_op jit(solution)/shard_map/ppermute | solution.py:1562
  346.4 71.5 %copy-start.10 = (f32[18,1536]{1,0:T(8,128)S(1)}, f32[18,1536]{1,0:T(8,128)}, u32[]{:S(2)}) copy-start(f32[18,1536]{1,0:T(8,128)} %get-tuple-element.112) | copy-start | bytes 331780
  346.4 71.6 %copy-start.6 = (bf16[128,1536]{1,0:T(8,128)(2,1)S(1)}, bf16[128,1536]{1,0:T(8,128)(2,1)}, u32[]{:S(2)}) copy-start(bf16[128,1536]{1,0:T(8,128)(2,1)} %get-tuple-element.69) | copy-start | bytes 1179652
  346.4 71.6 %copy-start.7 = (bf16[128,1536]{1,0:T(8,128)(2,1)S(1)}, bf16[128,1536]{1,0:T(8,128)(2,1)}, u32[]{:S(2)}) copy-start(bf16[128,1536]{1,0:T(8,128)(2,1)} %get-tuple-element.78) | copy-start | bytes 1179652
  346.5 74.4 %copy-start.2 = (bf16[128,2048]{1,0:T(8,128)(2,1)S(1)}, bf16[128,2048]{1,0:T(8,128)(2,1)}, u32[]{:S(2)}) copy-start(bf16[128,2048]{1,0:T(8,128)(2,1)} %get-tuple-element.114) | copy-start | bytes 1572868
  415.0 4.5 collective-permute-start
  417.9 2.9 collective-permute-start.1
  419.0 9.4 %collective-permute-start.9 = (bf16[128,1536]{1,0:T(8,128)(2,1)}, bf16[128,1536]{1,0:T(8,128)(2,1)}, u32[]{:S(2)}, u32[]{:S(2)}) collective-permute-start(bf16[128,1536]{1,0:T(8,128)(2,1)} %get-tuple-element.120), channel_id=1, source_target_pairs={{0,1},{1,0},{2,3},{3,2},{4,5},{5,4},{6,7},{7,6},{8,9},{9,8},{10,11... | collective-permute-start | bytes 1179656 | tf_op jit(solution)/shard_map/ppermute | solution.py:1562
  419.4 3.0 collective-permute-start.5
  419.5 3.3 collective-permute-start.4
  420.9 12.2 %collective-permute-start.3 = (bf16[128,2048]{1,0:T(8,128)(2,1)S(1)}, bf16[128,2048]{1,0:T(8,128)(2,1)S(1)}, u32[]{:S(2)}, u32[]{:S(2)}) collective-permute-start(bf16[128,2048]{1,0:T(8,128)(2,1)S(1)} %copy-done.2), channel_id=1, source_target_pairs={{0,1},{1,0},{2,3},{3,2},{4,5},{5,4},{6,7},{7,6},{8,9},{9,8},{10,11... | collective-permute-start | bytes 1572872 | tf_op jit(solution)/shard_map/ppermute | solution.py:1562
  421.0 1.3 copy-start.5
  421.1 1.8 copy-start.3
  422.4 10.7 %collective-permute-start.2 = (bf16[128,1536]{1,0:T(8,128)(2,1)S(1)}, bf16[128,1536]{1,0:T(8,128)(2,1)S(1)}, u32[]{:S(2)}, u32[]{:S(2)}) collective-permute-start(bf16[128,1536]{1,0:T(8,128)(2,1)S(1)} %copy-done.5), channel_id=1, source_target_pairs={{0,1},{1,0},{2,3},{3,2},{4,5},{5,4},{6,7},{7,6},{8,9},{9,8},{10,11... | collective-permute-start | bytes 1179656 | tf_op jit(solution)/shard_map/ppermute | solution.py:1562
  422.8 5.2 copy-start.4
  422.8 5.6 copy-start.12
  422.8 14.7 %collective-permute-start.7 = (bf16[128,2048]{1,0:T(8,128)(2,1)S(1)}, bf16[128,2048]{1,0:T(8,128)(2,1)S(1)}, u32[]{:S(2)}, u32[]{:S(2)}) collective-permute-start(bf16[128,2048]{1,0:T(8,128)(2,1)S(1)} %copy-done.3), channel_id=1, source_target_pairs={{0,1},{1,0},{2,3},{3,2},{4,5},{5,4},{6,7},{7,6},{8,9},{9,8},{10,11... | collective-permute-start | bytes 1572872 | tf_op jit(solution)/shard_map/ppermute | solution.py:1562
  428.0 9.5 %collective-permute-start.6 = (bf16[128,1536]{1,0:T(8,128)(2,1)S(1)}, bf16[128,1536]{1,0:T(8,128)(2,1)S(1)}, u32[]{:S(2)}, u32[]{:S(2)}) collective-permute-start(bf16[128,1536]{1,0:T(8,128)(2,1)S(1)} %copy-done.4), channel_id=1, source_target_pairs={{0,1},{1,0},{2,3},{3,2},{4,5},{5,4},{6,7},{7,6},{8,9},{9,8},{10,11... | collective-permute-start | bytes 1179656 | tf_op jit(solution)/shard_map/ppermute | solution.py:1562
  612.1 4.2 copy-start.8
  612.1 4.2 copy-start.9
  612.1 5.1 copy-start.1
  618.1 5.2 copy-start
  618.1 8.0 %slice-start = ((s8[4718592]{0:T(1024)(128)(4,1)}), s8[4194304]{0:T(1024)(128)(4,1)S(1)}, s32[]{:S(2)}) async-start(s8[4718592]{0:T(1024)(128)(4,1)} %bitcast.95), calls=%async_computation.3 | async-start | bytes 8388608
  623.3 3.4 slice-start.1
Sparse Core Ops, SparseCore 0:
  9.6 45.5 all-gather.6
  173.5 117.0 all-gather.8
  292.1 114.3 all-gather.10

commit v3 on v2

--- a/solution.py
+++ b/solution.py
@@ -83,19 +83,21 @@
 
 
 KINDS = 10
+SMALL = 24
+BLOCK = 512
 QUAD = ("own", "x", "y", "d")
 BESIDE = ("c", "cx", "cy", "cd")
 
 
 class Gather:
-    def __init__(self, ins, outs, send, recv, z, near, line):
+    def __init__(self, ins, outs, send, recv, z, near, line, flat=False):
         self.ins, self.outs, self.send, self.recv = ins, outs, send, recv
-        self.z, self.near, self.line = z, near, line
+        self.z, self.near, self.line, self.flat = z, near, line, flat
         self.parts = [halves(*ref.shape) for ref in ins]
         self.all = range(len(ins))
 
     def hop(self, a, j, kind, whose, to, part=None, src=None):
-        dst = self.outs[a].at[j, self.near[whose]]
+        dst = self.outs[a].at[j] if self.flat else self.outs[a].at[j, self.near[whose]]
         src = dst if src is None else src
         if part is not None:
             src, dst = cut(src, part), cut(dst, part)
@@ -190,6 +192,17 @@
                     self.hop(a, j, 9, "own", z - 1).start()
 
         self.first(j)
+
+    def carry(self, j, kind):
+        z = self.z
+        for a in self.all:
+            self.landed(a, j, kind, "own")
+        more, target = (z < self.line - 1, z + 1) if kind == 8 else (z > 0, z - 1)
+
+        @pl.when(more)
+        def on():
+            for a in self.all:
+                self.hop(a, j, kind, "own", target).start()
 
     def plane_of(self, k):
         return lax.rem(self.z + k, self.line)
@@ -378,7 +391,7 @@
     return powers / jnp.sum(powers, axis=0, keepdims=True)
 
 
-def tail_kernel(layers_n, number, n_sums, *refs):
+def tail_kernel(layers_n, number, *refs):
     refs = list(refs)
 
     def some(count):
@@ -391,10 +404,12 @@
     table, hit, seats = some(3)
     w_gate, w_up, w_down = some(3)
     owns = [some(5) for l in range(layers_n)]
-    parts = some(n_sums)
+    row_sources = [some(2) for l in range(layers_n)]
+    column_sources = [some(2) for l in range(layers_n)]
+    smalls = some(layers_n)
     grad_gate, grad_up, grad_down, landing = some(4)
     beside = some(layers_n)
-    sums = some(n_sums)
+    small_sum, grad_qkv, grad_out = some(3)
     (
         tokens,
         grads,
@@ -419,14 +434,35 @@
         gather_recv,
         beside_send,
         beside_recv,
-    ) = some(23)
-    held = [some(6) for a in range(n_sums)]
+        small_own,
+        small_got,
+        small_part,
+        small_sem,
+        columns,
+        row_block,
+        block_sum,
+        block_got,
+        final,
+        final_got,
+        column_send,
+        column_recv,
+        column_keep,
+        row_sem,
+        block_send,
+        block_recv,
+        final_send,
+        final_recv,
+    ) = some(41)
+    held = [some(6)]
     z, near = place()
     n_dp, local_n = seats.shape[1], seats.shape[2]
     width = cols_in.shape[1]
     ours = pl.ds(pl.multiple_of(z * width, 128), width)
     gather = Gather([own_shard], [landing], gather_send, gather_recv, z, near, n_dp)
-    total = Sums(parts, sums, held, *refs, z, near, n_dp)
+    total = Sums([small_part], [small_sum], held, *refs, z, near, n_dp)
+    own_e = near["own"]
+    plane_n = columns.shape[1]
+    over = ((0,), (0,))
     per_expert = n_dp - 1
     per_layer = local_n * per_expert
     steps = layers_n * per_layer
@@ -506,46 +542,251 @@
             pltpu.make_async_copy(stage_tall, grad_down.at[l, e], out_sem.at[2]),
         ]
 
-    greet(z, near, ("x", "y", "c"), n_dp)
+    def column_pieces(l, owner):
+        first, second = column_sources[l]
+        extra = second.shape[1] // 128 - plane_n
+        return [
+            (first.at[:, pl.ds(pl.multiple_of(owner * 256, 256), 256)], 0, 256),
+            (second.at[:, pl.ds(pl.multiple_of(owner * 128, 128), 128)], 256, 128),
+            (
+                second.at[
+                    :, pl.ds(pl.multiple_of((plane_n + owner // 2 % extra) * 128, 128), 128)
+                ],
+                384,
+                128,
+            ),
+        ]
+
+    def column_copy(l, owner, source, piece):
+        src, at, size = column_pieces(l, owner)[piece]
+        return pltpu.make_async_remote_copy(
+            src_ref=src,
+            dst_ref=columns.at[l, source, :, pl.ds(at, size)],
+            send_sem=column_send.at[l, owner, piece],
+            recv_sem=column_recv.at[l, source, piece],
+            device_id={EX: owner},
+            device_id_type=MESH,
+        )
+
+    def column_own(l, piece):
+        src, at, size = column_pieces(l, own_e)[piece]
+        dst = columns.at[l, own_e, :, pl.ds(at, size)]
+        return pltpu.make_async_copy(src, dst, column_keep.at[l, piece])
+
+    def column_each(l, act_send, act_recv, act_own):
+        for d in range(1, plane_n):
+            owner = lax.rem(own_e + d, plane_n)
+            source = lax.rem(own_e + plane_n - d, plane_n)
+            for piece in range(3):
+                if piece < 2:
+                    if act_send is not None:
+                        act_send(column_copy(l, owner, own_e, piece))
+                    if act_recv is not None:
+                        act_recv(column_copy(l, owner, source, piece))
+                    continue
+                if act_send is not None:
+
+                    @pl.when(lax.rem(owner, 2) == 0)
+                    def extra_out():
+                        act_send(column_copy(l, owner, own_e, piece))
+
+                if act_recv is not None:
+
+                    @pl.when(lax.rem(own_e, 2) == 0)
+                    def extra_in():
+                        act_recv(column_copy(l, owner, source, piece))
+
+        if act_own is not None:
+            act_own(column_own(l, 0))
+            act_own(column_own(l, 1))
+
+            @pl.when(lax.rem(own_e, 2) == 0)
+            def extra_own():
+                act_own(column_own(l, 2))
+
+    def row_loads(l):
+        return [
+            pltpu.make_async_copy(src.at[0], row_block.at[i], row_sem.at[i])
+            for i, src in enumerate(row_sources[l])
+        ]
+
+    def blocks(l):
+        column_each(l, None, lambda one: one.wait_recv(), wait)
+        for one in row_loads(l):
+            one.wait()
+        height = block_sum.shape[2]
+        for i in range(2):
+            here = pl.ds(i * 256, 256)
+            given = columns[l, :, :, here].reshape(-1, 256)
+            for j in range(n_dp):
+                rows = row_block[i, :, :, pl.ds(j * height, height)].reshape(-1, height)
+                block_sum[l, j, :, here] = mul(rows, given, over).astype(bf16)
+        if l > 0:
+            for one in row_loads(l - 1):
+                one.start()
+
+    def block_move(l, j, way):
+        slot = jnp.where(j == z + way, n_dp, j) if way < 0 else j
+        return pltpu.make_async_remote_copy(
+            src_ref=block_sum.at[l, j],
+            dst_ref=block_got.at[l, slot],
+            send_sem=block_send.at[l, j],
+            recv_sem=block_recv.at[l, slot],
+            device_id={DP: z + way},
+            device_id_type=MESH,
+        )
+
+    def block_landed(l, slot):
+        pltpu.make_async_remote_copy(
+            src_ref=block_got.at[l, slot],
+            dst_ref=block_got.at[l, slot],
+            send_sem=block_send.at[l, 0],
+            recv_sem=block_recv.at[l, slot],
+            device_id={DP: z},
+            device_id_type=MESH,
+        ).wait_recv()
+
+    def block_step(l):
+        def act(j, way):
+            if way == 0:
+                return
+            more = (z > 0) if way > 0 else (z < n_dp - 1)
+
+            @pl.when(more)
+            def add():
+                block_landed(l, j)
+                block_sum[l, j] = (
+                    block_sum[l, j].astype(f32) + block_got[l, j].astype(f32)
+                ).astype(bf16)
+
+            block_move(l, j, way).start()
+
+        return act
+
+    def final_copy(l, owner, source):
+        return pltpu.make_async_remote_copy(
+            src_ref=final.at[l, owner],
+            dst_ref=final_got.at[l, source],
+            send_sem=final_send.at[l, owner],
+            recv_sem=final_recv.at[l, source],
+            device_id={EX: owner},
+            device_id_type=MESH,
+        )
+
+    def block_end(l):
+        final[l] = block_sum[l, z].reshape(final.shape[1:])
+
+        @pl.when(z > 0)
+        def below():
+            block_landed(l, z)
+            got = block_got[l, z].reshape(final.shape[1:])
+            final[l] = (final[l].astype(f32) + got.astype(f32)).astype(bf16)
+
+        @pl.when(z < n_dp - 1)
+        def above():
+            block_landed(l, n_dp)
+            got = block_got[l, n_dp].reshape(final.shape[1:])
+            final[l] = (final[l].astype(f32) + got.astype(f32)).astype(bf16)
+
+        for d in range(1, plane_n):
+            final_copy(l, lax.rem(own_e + d, plane_n), own_e).start()
+        final_got[l, own_e] = final[l, own_e]
+
+    def block_out(l):
+        for d in range(1, plane_n):
+            final_copy(l, own_e, lax.rem(own_e + d, plane_n)).wait_recv()
+        for source in range(plane_n):
+            got = final_got[l, source].astype(f32)
+            grad_qkv[l, :, pl.ds(source * 256, 256)] = got[:, :256]
+            grad_out[l, :, pl.ds(source * 128, 128)] = got[:, 256:384]
+            if source % 2 == 0:
+                grad_out[l, :, pl.ds((plane_n + source // 2) * 128, 128)] = got[:, 384:]
+
+    def small_exchange():
+        return pltpu.make_async_remote_copy(
+            src_ref=small_own,
+            dst_ref=small_got,
+            send_sem=small_sem.at[0],
+            recv_sem=small_sem.at[1],
+            device_id={EX: near["c"]},
+            device_id_type=MESH,
+        )
+
+    def small_parts():
+        small_exchange().wait_recv()
+        both = small_own[...] + small_got[...]
+        rest = jnp.zeros((128 - both.shape[0], both.shape[1]), f32)
+        turned = jnp.transpose(jnp.concatenate([both, rest], axis=0))
+        high = turned.astype(bf16)
+        low = (turned - high.astype(f32)).astype(bf16)
+        shape = small_part.shape[:3] + (128,)
+        small_part[:, :, :, pl.ds(0, 128)] = high.reshape(shape)
+        small_part[:, :, :, pl.ds(128, 128)] = low.reshape(shape)
+        for distance in (3, 2, 1, 0):
+            total.at(distance, total.first)
+
+    for l in range(layers_n):
+        small_own[pl.ds(l * SMALL, SMALL)] = smalls[l][...]
+
+    @pl.when(lax.rem(own_e, 2) == 1)
+    def no_extra():
+        columns[:, :, :, pl.ds(384, 128)] = jnp.zeros(columns.shape[:3] + (128,), bf16)
+
+    greet(z, near, ("x", "y", "d", "c", "cx", "cy", "cd"), n_dp)
     gather.line_first()
+    small_exchange().start()
     for l in reversed(range(layers_n)):
         for k in range(1, n_dp):
             across(l, lax.rem(z + k, n_dp)).start()
-    total.at(3, total.first)
-    total.at(2, total.first)
+    for l in reversed(range(layers_n)):
+        column_each(l, start, None, start)
+    for one in row_loads(layers_n - 1):
+        one.start()
     of(0, weights, start)
     fetch(0, 0, start)
 
+    def block_at(l, distance):
+        return lambda: total.at(distance, block_step(l))
+
     services = {
-        0: [lambda: gather.arrivals(1, gather.take)],
-        1: [lambda: gather.arrivals(2, gather.take)],
+        0: [lambda: gather.arrivals(1, gather.take), small_parts],
+        1: [lambda: gather.arrivals(2, gather.take), lambda: blocks(1)],
         2: [
             lambda: gather.arrivals(1, gather.second),
             lambda: gather.arrivals(3, gather.take),
+            block_at(1, 3),
         ],
         3: [
             lambda: gather.arrivals(1, gather.third),
             lambda: gather.arrivals(2, gather.second),
-            lambda: total.at(3, total.second),
-            lambda: total.at(2, total.second),
+            block_at(1, 2),
+            lambda: blocks(0),
         ],
         4: [
             lambda: gather.arrivals(2, gather.third),
             lambda: gather.arrivals(3, gather.second),
-            lambda: total.at(1, total.first),
-            lambda: total.at(0, total.first),
+            block_at(0, 3),
+            block_at(1, 1),
         ],
         5: [
             lambda: gather.arrivals(3, gather.third),
             lambda: gather.arrivals(1, gather.finish),
             lambda: gather.arrivals(2, gather.finish),
             lambda: gather.arrivals(3, gather.finish),
+            block_at(0, 2),
         ],
-        7: [lambda: total.at(3, total.third)],
-        8: [lambda: total.at(2, total.third)],
-        9: [lambda: total.at(1, total.second)],
-        10: [lambda: total.at(0, total.second)],
-        11: [lambda: total.at(1, total.third)],
+        6: [
+            lambda: total.at(3, total.second),
+            lambda: total.at(2, total.second),
+            lambda: total.at(1, total.second),
+            lambda: total.at(0, total.second),
+            block_at(0, 1),
+        ],
+        7: [lambda: block_end(1)],
+        8: [lambda: total.at(3, total.third), lambda: total.at(2, total.third)],
+        9: [lambda: total.at(1, total.third)],
+        10: [lambda: block_end(0)],
+        11: [lambda: total.at(0, total.third), lambda: block_out(1)],
     }
 
     def step(i, carry):
@@ -566,13 +807,18 @@
         fetch(i, slot, wait)
         everyone = tokens[slot].reshape(-1, tokens.shape[3])
         experts_n = hit.shape[2]
-        router = table[pl.ds(pl.multiple_of(l * experts_n, experts_n), experts_n), :].astype(bf16)
-        gates[...] = masked_gates(mul(router, everyone, LAST), hit[l, j] > 0)
+
+        @pl.when(e == 0)
+        def gates_here():
+            here = pl.ds(pl.multiple_of(l * experts_n, experts_n), experts_n)
+            router = table[here, :].astype(bf16)
+            gates[k] = masked_gates(mul(router, everyone, LAST), hit[l, j] > 0)
+
         pick = seat_rows(seats[l, j, pl.ds(e, 1)], number)
         rows_in[...] = mul(pick, everyone).astype(bf16)
         rows_grad[...] = mul(pick, grads[slot].reshape(-1, tokens.shape[3])).astype(bf16)
         place_of = pl.ds(pl.multiple_of((k + 1) * number, 32), number)
-        mine = gates[pl.ds(lax.axis_index(EX) * local_n + e, 1), :]
+        mine = gates[k, pl.ds(own_e * local_n + e, 1), :]
         gate_seat = jnp.sum(pick.astype(f32) * mine, axis=1, keepdims=True)
 
         @pl.when(k == 0)
@@ -602,7 +848,6 @@
             def staged():
                 of(i - per_expert, results, wait)
 
-            over = ((0,), (0,))
             stage_wide[0] = mul(cols_in[...], dgate_low[...], over)
             stage_wide[1] = mul(cols_in[...], dup_low[...], over)
             stage_tall[...] = mul(hidden_low[...], cols_grad[...], over)
@@ -622,9 +867,16 @@
         return carry
 
     lax.fori_loop(0, steps, step, 0)
-    total.at(0, total.third)
+    block_out(0)
     for distance in (3, 2, 1, 0):
         total.at(distance, total.finish)
+    small_exchange().wait_send()
+    for l in range(layers_n):
+        column_each(l, lambda one: one.wait_send(), None, None)
+        for d in range(1, plane_n):
+            final_copy(l, lax.rem(own_e + d, plane_n), own_e).wait_send()
+        for distance in (3, 2, 1):
+            total.at(distance, lambda j, way: block_move(l, j, way).wait_send())
     gather.line_done()
     for l in range(layers_n):
         for k in range(1, n_dp):
@@ -633,18 +885,30 @@
 
 
 def tail(
-    capacity, number, tokens_all, grads_all, own_shard, table, hit, seats, weights, owns, parts
+    capacity,
+    number,
+    tokens_all,
+    grads_all,
+    own_shard,
+    plan,
+    weights,
+    owns,
+    row_sources,
+    column_sources,
+    smalls,
 ):
+    table, hit, seats = plan
     layers_n, n_dp, local_n, group_rows = seats.shape
     n_expert = lax.axis_size(EX)
     rows, width = own_shard.shape
     hidden = weights[0].shape[3]
     part = width // n_dp
+    cut_rows = part // n_expert
+    wide = column_sources[0][0].shape[1]
     shape = jax.ShapeDtypeStruct
-    n_sums = len(parts)
-    flat = [one for own in owns for one in own]
+    several = [one for group in (owns, row_sources, column_sources) for l in group for one in l]
     results = pl.pallas_call(
-        partial(tail_kernel, layers_n, capacity, n_sums),
+        partial(tail_kernel, layers_n, capacity),
         out_shape=[
             shape((layers_n, local_n, part, hidden), f32),
             shape((layers_n, local_n, part, hidden), f32),
@@ -652,13 +916,17 @@
             shape((n_dp, n_expert, rows, width), bf16),
         ]
         + [shape(tokens_all[0].shape, bf16)] * layers_n
-        + [shape(one.shape[2:], f32) for one in parts],
-        in_specs=[HBM] * (2 * layers_n) + [VMEM] * 3 + [HBM] * (3 + len(flat) + n_sums),
-        out_specs=[HBM] * (4 + layers_n) + [VMEM] * n_sums,
+        + [
+            shape((cut_rows, 256), f32),
+            shape((layers_n, cut_rows, wide), f32),
+            shape((layers_n, cut_rows, width), f32),
+        ],
+        in_specs=[HBM] * (2 * layers_n) + [VMEM] * 3 + [HBM] * (3 + len(several)) + [VMEM] * layers_n,
+        out_specs=[HBM] * (4 + layers_n) + [VMEM] * 3,
         scratch_shapes=[
             pltpu.VMEM((2, n_expert, rows, width), bf16),
             pltpu.VMEM((2, n_expert, rows, width), bf16),
-            pltpu.VMEM(hit.shape[2:], f32),
+            pltpu.VMEM((n_dp - 1,) + hit.shape[2:], f32),
             pltpu.VMEM((capacity, width), bf16),
             pltpu.VMEM((capacity, width), bf16),
             pltpu.VMEM((n_dp * capacity, part), bf16),
@@ -679,11 +947,37 @@
             pltpu.SemaphoreType.DMA((1, n_dp, KINDS)),
             pltpu.SemaphoreType.DMA((layers_n, n_dp)),
             pltpu.SemaphoreType.DMA((layers_n, n_dp)),
+            pltpu.VMEM((layers_n * SMALL, width), f32),
+            pltpu.VMEM((layers_n * SMALL, width), f32),
+            pltpu.VMEM((n_dp, n_expert, cut_rows, 256), bf16),
+            pltpu.SemaphoreType.DMA((2,)),
+            pltpu.VMEM((layers_n, n_expert, rows, BLOCK), bf16),
+            pltpu.VMEM((2, n_expert, rows, width), bf16),
+            pltpu.VMEM((layers_n, n_dp, part, BLOCK), bf16),
+            pltpu.VMEM((layers_n, n_dp + 1, part, BLOCK), bf16),
+            pltpu.VMEM((layers_n, n_expert, cut_rows, BLOCK), bf16),
+            pltpu.VMEM((layers_n, n_expert, cut_rows, BLOCK), bf16),
+            pltpu.SemaphoreType.DMA((layers_n, n_expert, 3)),
+            pltpu.SemaphoreType.DMA((layers_n, n_expert, 3)),
+            pltpu.SemaphoreType.DMA((layers_n, 3)),
+            pltpu.SemaphoreType.DMA((2,)),
+            pltpu.SemaphoreType.DMA((layers_n, n_dp)),
+            pltpu.SemaphoreType.DMA((layers_n, n_dp + 1)),
+            pltpu.SemaphoreType.DMA((layers_n, n_expert)),
+            pltpu.SemaphoreType.DMA((layers_n, n_expert)),
         ]
-        + sums_scratch([one.shape[2:] for one in parts], n_dp),
+        + sums_scratch([(cut_rows, 256)], n_dp),
         compiler_params=settings(number),
         name="tail",
-    )(*tokens_all, *grads_all, own_shard, table, hit, seats, *weights, *flat, *parts)
+    )(
+        *tokens_all,
+        *grads_all,
+        own_shard,
+        *plan,
+        *weights,
+        *several,
+        *smalls,
+    )
     return results[:3], results[4 + layers_n :]
 
 
@@ -693,17 +987,15 @@
 
 def settings(number):
     return pltpu.CompilerParams(
-        collective_id=number, has_side_effects=True, vmem_limit_bytes=62 << 20
+        collective_id=number, has_side_effects=True, vmem_limit_bytes=63 << 20
     )
 
 
-def chain(z, e, line):
+def chain(z, e):
     n_expert = 8
-    behind = (z - jnp.where(e == 0, 1, 0), lax.rem(e + n_expert - 1, n_expert))
-    ahead = (z + jnp.where(e == n_expert - 1, 1, 0), lax.rem(e + 1, n_expert))
-    has_behind = (z > 0) | (e > 0)
-    has_ahead = (z < line - 1) | (e < n_expert - 1)
-    return behind, ahead, has_behind, has_ahead
+    behind = (z, lax.rem(e + n_expert - 1, n_expert))
+    ahead = (z, lax.rem(e + 1, n_expert))
+    return behind, ahead, e > 0, e < n_expert - 1
 
 
 def normalized(value, gain):
@@ -721,7 +1013,7 @@
 
 def allowed_keys(rk, row, z, e, behind, has_behind, seg_column):
     own = rk[z, e, pl.ds(row, 1), :]
-    first = rk[jnp.where(has_behind, behind[0], z), behind[1], pl.ds(row, 1), :]
+    first = rk[z, behind[1], pl.ds(row, 1), :]
     rows = seg_column.shape[0]
     query = lax.broadcasted_iota(jnp.int32, (rows, rows), 0)
     key = lax.broadcasted_iota(jnp.int32, (rows, rows), 1)
@@ -750,7 +1042,7 @@
 
     stream, cosine, sine, seg_column = some(4)
     if first:
-        small, ranks, w_qkv, w_out = some(4)
+        small, ranks, w_qkv, w_out, out_grad = some(5)
     else:
         table, rk, hit, seats, turned, cross_from, qkv_from, out_from = some(8)
     w_gate, w_up, w_down = some(3)
@@ -758,6 +1050,7 @@
     rows_in, gate_pre, up_pre, gate_seat, quad = some(5)
     if first:
         table, rk_out, hit, seats, turned, qkv_out, out_out, qkv_next, out_next = some(9)
+        (line_grads,) = some(1)
         small_land, rk, seat_all = some(3)
     else:
         (cross_to,) = some(1)
@@ -780,7 +1073,8 @@
         recv,
     ) = some(16)
     if first:
-        send_0, recv_0, send_1, recv_1, send_2, recv_2, send_3, recv_3, keep = some(9)
+        send_0, recv_0, send_1, recv_1, send_2, recv_2, send_3, recv_3 = some(8)
+        send_4, recv_4, keep = some(3)
     else:
         cross_send, cross_recv, cross_keep = some(3)
     scratch = refs
@@ -790,7 +1084,7 @@
     local_n = seats.shape[2]
     rows = stream.shape[0]
     experts_n = hit.shape[2]
-    behind, ahead, has_behind, has_ahead = chain(z, e, line)
+    behind, ahead, has_behind, has_ahead = chain(z, e)
 
     weights = [
         pltpu.make_async_copy(src.at[layer], dst, weight_sem.at[i])
@@ -807,6 +1101,7 @@
         g3 = Gather(
             [w_qkv.at[1], w_out.at[1]], [qkv_next, out_next], send_3, recv_3, z, near, line
         )
+        g4 = Gather([out_grad], [line_grads], send_4, recv_4, z, near, line, flat=True)
         local = [
             pltpu.make_async_copy(one, g.outs[i].at[z, e], keep.at[k])
             for k, (g, i, one) in enumerate(
@@ -947,11 +1242,9 @@
         if first and h == 7:
             g2.arrivals(3, g2.third)
             g3.arrivals(1, g3.take)
-        if not first and h == 3:
+            g4.line_first()
+        if not first and h == 8:
             cross.second(cross.plane_of(1))
-        if not first and h == 9:
-            cross.second(cross.plane_of(2))
-            cross.third(cross.plane_of(1))
     kv_out[...] = kv[...]
     if first:
         g2.finish(z)
@@ -997,7 +1290,9 @@
     if first:
         g3.arrivals(1, g3.third)
         g3.arrivals(2, g3.second)
+        g4.arrivals(1, g4.carry)
     else:
+        cross.second(cross.plane_of(2))
         cross.spread(3, cross_from, cross_keep)
 
     def expert(k, carry):
@@ -1015,6 +1310,7 @@
     if first:
         g3.arrivals(2, g3.third)
         g3.arrivals(3, g3.second)
+        g4.arrivals(2, g4.carry)
         out_copies = [
             pltpu.make_async_copy(qkv, qkv_out, load_sem.at[0]),
             pltpu.make_async_copy(w_o, out_out, load_sem.at[1]),
@@ -1022,8 +1318,8 @@
         for copied in out_copies:
             copied.start()
     else:
+        cross.third(cross.plane_of(1))
         cross.second(cross.plane_of(3))
-        cross.third(cross.plane_of(2))
 
     def make(name):
         d = near[name]
@@ -1043,14 +1339,16 @@
 
     if first:
         g3.arrivals(3, g3.third)
+        g4.arrivals(3, g4.carry)
         g3.finish(z)
         for step in range(1, line):
             g3.arrivals(step, g3.finish)
         for copied in local[4:] + out_copies:
             copied.wait()
-        for g in (g0, g1, g2, g3):
+        for g in (g0, g1, g2, g3, g4):
             g.line_done()
     else:
+        cross.third(cross.plane_of(2))
         cross.third(cross.plane_of(3))
         cross.spread_done(cross_from, cross_keep)
 
@@ -1095,7 +1393,8 @@
             shape((group, 128), f32),
         ]
         outs += [shape(full_qkv, bf16), shape(full_out, bf16)] * 2
-        specs += [VMEM] * 5 + [HBM] * 4
+        outs.append(shape((n_dp, rows, width), bf16))
+        specs += [VMEM] * 5 + [HBM] * 5
         scratch += [
             pltpu.VMEM((n_dp, n_expert, cut_rows, 128), bf16),
             pltpu.VMEM((n_dp, n_expert, rank_rows, rows), jnp.int32),
@@ -1123,13 +1422,13 @@
         pltpu.SemaphoreType.DMA((8,)),
     ]
     if first:
-        for count in (2, 1, 1, 2):
+        for count in (2, 1, 1, 2, 1):
             scratch += [pltpu.SemaphoreType.DMA((count, n_dp, KINDS)) for i in range(2)]
         scratch.append(pltpu.SemaphoreType.DMA((6,)))
     else:
         scratch += [pltpu.SemaphoreType.DMA((1, n_dp, KINDS)) for i in range(2)]
         scratch.append(pltpu.SemaphoreType.DMA((n_dp,)))
-    given_specs = [HBM] * 4 if first else [VMEM] * 5 + [HBM] * 3
+    given_specs = [HBM] * 5 if first else [VMEM] * 5 + [HBM] * 3
     return pl.pallas_call(
         partial(forward_kernel, layer, layers_n, capacity),
         out_shape=outs,
@@ -1160,9 +1459,11 @@
     grad_stream, stream, cosine, sine, seg_column = some(5)
     mixed, normed_b, queries, kv, gate_pre, up_pre, gate_seat = some(7)
     table, rk, hit, seats, turned = some(5)
+    row_sources = some(2)
     qkv_from, out_from, w_gate, w_up, w_down = some(5)
     grad_out, grad_low, rows_grad, hidden_low, dgate_low, dup_low = some(6)
     dprojected, grad_attn, small = some(3)
+    row_lands = some(2)
     (
         summed,
         qkv,
@@ -1171,6 +1472,7 @@
         dkv,
         dkv_send,
         dkv_got,
+        all_probs,
         tokens,
         back_rows,
         gate_w,
@@ -1181,7 +1483,10 @@
         chain_sem,
         send,
         recv,
-    ) = some(17)
+        row_send,
+        row_recv,
+        row_keep,
+    ) = some(21)
     scratch = refs
     z, near = place()
     e = near["own"]
@@ -1189,7 +1494,7 @@
     local_n = seats.shape[2]
     rows, width = stream.shape
     experts_n = hit.shape[2]
-    behind, ahead, has_behind, has_ahead = chain(z, e, line)
+    behind, ahead, has_behind, has_ahead = chain(z, e)
     weights = [
         pltpu.make_async_copy(src.at[layer], dst, weight_sem.at[i])
         for i, (src, dst) in enumerate(((w_gate, gate_w), (w_up, up_w), (w_down, down_w)))
@@ -1201,13 +1506,38 @@
     grad_low[...] = grad_stream[...].astype(bf16)
     greet(z, near, ("x", "y", "c"), None, (behind, ahead, has_behind, has_ahead))
 
+    spreads = [
+        Gather([src], [dst], row_send.at[i], row_recv.at[i], 0, near, None)
+        for i, (src, dst) in enumerate(zip(row_sources, row_lands))
+    ]
+    kept = [
+        pltpu.make_async_copy(src, dst.at[0, e], row_keep.at[i])
+        for i, (src, dst) in enumerate(zip(row_sources, row_lands))
+    ]
+
     first, second, third, finish = plane_gather(grad_low, tokens, send, recv, near)
     first()
     for one in weights + loads:
         one.start()
+    allowed = allowed_keys(rk, layers_n * experts_n, z, e, behind, has_behind, seg_column[...])
+    per_group = QUERY_HEADS // KEY_VALUE_HEADS
+
+    def keys_of(group):
+        return kv[:, :, head_of(group)].reshape(2 * rows, HEAD_SIZE)
+
+    def prepare(heads):
+        for h in heads:
+            all_probs[h] = head_probs(queries[:, head_of(h)], keys_of(h // per_group), allowed)
+
+    prepare(range(0, 5))
     second()
+    prepare(range(5, 9))
     third()
+    prepare(range(9, QUERY_HEADS))
     finish()
+    spreads[0].first(0, spreads[0].ins)
+    for one in kept:
+        one.start()
     everyone = tokens[...].reshape(-1, width)
     picked = mul(seat_rows(seats[layer, z], number), everyone)
     back_rows[:, pl.ds(0, width)] = picked.astype(bf16)
@@ -1248,7 +1578,10 @@
         mine = turned[lanes, pl.ds(layer * local_n, local_n)]
         scratch[0][d] = mul(seat_columns(mine, number), back_rows[...]).astype(bf16)
 
+    spreads[0].second(0)
     plane_sum(make, summed, None, scratch, near)
+    spreads[0].third(0)
+    spreads[1].first(0, spreads[1].ins)
 
     over = ((0,), (0,))
     gain = 2 * experts_n + 2 * layer
@@ -1259,6 +1592,7 @@
     dgates = turned_sum[:experts_n] + turned_sum[experts_n : 2 * experts_n]
     inner = jnp.sum(gates * dgates, axis=0, keepdims=True)
     dlogits = (gates * (dgates - inner)).astype(bf16)
+    small[...] = jnp.zeros_like(small)
     small[pl.ds(0, experts_n)] = mul(dlogits, normed_b[...])
     dnormed = summed[:, pl.ds(0, width)] + mul(dlogits, router, over)
     back, dgain = norm_back(mixed[...], table[pl.ds(gain + 1, 1), :], dnormed)
@@ -1269,18 +1603,16 @@
 
     loads[1].wait()
     datt[...] = mul(grad_attn[...], w_o[...].reshape(width, -1), LAST).astype(bf16)
-    allowed = allowed_keys(rk, layers_n * experts_n, z, e, behind, has_behind, seg_column[...])
     cos, sin = cosine[...], sine[...]
-    per_group = QUERY_HEADS // KEY_VALUE_HEADS
     scale = 1.0 / math.sqrt(HEAD_SIZE)
     for group in range(KEY_VALUE_HEADS):
-        keys = kv[:, :, head_of(group)].reshape(2 * rows, HEAD_SIZE)
-        values = kv[:, :, head_of(KEY_VALUE_HEADS + group)].reshape(2 * rows, HEAD_SIZE)
+        keys = keys_of(group)
+        values = keys_of(KEY_VALUE_HEADS + group)
         dkeys = jnp.zeros((2 * rows, HEAD_SIZE), f32)
         dvalues = jnp.zeros((2 * rows, HEAD_SIZE), f32)
         for h in range(group * per_group, (group + 1) * per_group):
             query = queries[:, head_of(h)]
-            probs = head_probs(query, keys, allowed)
+            probs = all_probs[h]
             given = datt[:, head_of(h)]
             dprobs = mul(given, values, LAST)
             delta = jnp.sum(probs * dprobs, axis=-1, keepdims=True)
@@ -1289,6 +1621,8 @@
             dprojected[:, head_of(h)] = turn(dquery, cos, -sin).astype(bf16)
             dkeys = dkeys + mul(dscores, query, over)
             dvalues = dvalues + mul(probs.astype(bf16), given, over)
+        if group == 0:
+            spreads[1].second(0)
         dkv[:, head_of(group)] = dkeys * scale
         dkv[:, head_of(KEY_VALUE_HEADS + group)] = dvalues
     dkv_send[...] = dkv[pl.ds(0, rows)].astype(bf16)
@@ -1332,6 +1666,11 @@
     @pl.when(has_behind)
     def passed_back():
         pass_on(behind).wait_send()
+
+    spreads[1].third(0)
+    for i in range(2):
+        spreads[i].finish(0)
+        kept[i].wait()
 
 
 def layer_backward(layer, number, shapes, grads, stream, tables, saved, plan, weights):
@@ -1352,7 +1691,9 @@
         shape((seats_n, hidden), bf16),
         shape((rows, width + 2 * keys_n), bf16),
         shape((rows, width), bf16),
-        shape((experts_n + 2, width), f32),
+        shape((SMALL, width), f32),
+        shape((1, n_expert, rows, width), bf16),
+        shape((1, n_expert, rows, width), bf16),
     ]
     scratch = [
         pltpu.VMEM((rows, width + 128), f32),
@@ -1362,6 +1703,7 @@
         pltpu.VMEM((2 * rows, 2 * keys_n), f32),
         pltpu.VMEM((rows, 2 * keys_n), bf16),
         pltpu.VMEM((rows, 2 * keys_n), bf16),
+        pltpu.VMEM((QUERY_HEADS, rows, 2 * rows), f32),
         pltpu.VMEM((n_expert, rows, width), bf16),
         pltpu.VMEM((seats_n, width + 128), bf16),
         pltpu.VMEM((local_n, width, hidden), bf16),
@@ -1372,12 +1714,15 @@
         pltpu.SemaphoreType.DMA((2,)),
         pltpu.SemaphoreType.DMA((8,)),
         pltpu.SemaphoreType.DMA((8,)),
+        pltpu.SemaphoreType.DMA((2, 1, 1, KINDS)),
+        pltpu.SemaphoreType.DMA((2, 1, 1, KINDS)),
+        pltpu.SemaphoreType.DMA((2,)),
     ]
     return pl.pallas_call(
         partial(backward_kernel, layer, layers_n, capacity),
         out_shape=outs,
-        in_specs=[VMEM] * 17 + [HBM] * 5,
-        out_specs=[VMEM] * 9,
+        in_specs=[VMEM] * 17 + [HBM] * 7,
+        out_specs=[VMEM] * 9 + [HBM] * 2,
         scratch_shapes=scratch + sum_scratch(rows, width + 128),
         compiler_params=settings(number),
         name="layer_backward",
@@ -1672,11 +2017,14 @@
 
     saved, outputs, normed_all, streams = [], [], [], [tokens]
     for l in range(layers_n):
-        given = (small, ranks, w_qkv, w_out) if l == 0 else (*plan, along_line(out_grad), *full[l])
+        given = (small, ranks, w_qkv, w_out, out_grad)
+        if l > 0:
+            given = (*plan, line_grads, *full[l])
         results = layer_forward(l, 1 + l, shapes, streams[l], tables, given, experts)
         if l == 0:
             plan = results[13:18]
             full = [results[18:20], results[20:22]]
+            line_grads = results[22]
         else:
             grads_all = [results[13]]
         streams.append(results[0])
@@ -1685,58 +2033,36 @@
         normed_all.append(along_line(results[12]))
 
     grads = out_grad
-    owns, parts, smalls = [None] * layers_n, [None] * layers_n, [None] * layers_n
+    owns, smalls = [None] * layers_n, [None] * layers_n
+    row_sources, column_sources = [None] * layers_n, [None] * layers_n
     for l in reversed(range(layers_n)):
         normed_a, queries, kv, attended, mixed, normed_b, rows_in = saved[l][:7]
         kept = (mixed, normed_b, queries, kv, *saved[l][7:])
-        sources = (*full[l], *experts)
-        results = layer_backward(
-            l, 4 + l, shapes, grads, streams[l], tables, kept, plan, sources
-        )
+        sources = (normed_a, attended, *full[l], *experts)
+        results = layer_backward(l, 4 + l, shapes, grads, streams[l], tables, kept, plan, sources)
         grads, own_shard = results[:2]
         owns[l] = (rows_in, *results[2:6])
-        dprojected, grad_attn, small_grad = results[6:9]
-        other = from_sibling((normed_a, attended, dprojected, grad_attn))
-        pairs = [
-            jnp.concatenate([own, sib], axis=0)
-            for own, sib in zip((normed_a, attended, dprojected, grad_attn), other)
-        ]
-        parts[l] = [
-            lax.dot_general(
-                one, another, (((0,), (0,)), ((), ())), preferred_element_type=f32
-            ).astype(bf16)
-            for one, another in ((pairs[0], pairs[2]), (pairs[1], pairs[3]))
-        ]
-        smalls[l] = small_grad + from_sibling(small_grad)
-    cut_shape = (n_dp, n_expert, D // (n_dp * n_expert))
-    wide = experts_n + 2
-    small_grads = jnp.pad(jnp.concatenate(smalls), ((0, 128 - layers_n * wide), (0, 0))).T
-    high = small_grads.astype(bf16)
-    low = (small_grads - high.astype(f32)).astype(bf16)
-    pieces = [jnp.concatenate([high, low], axis=1).reshape(cut_shape + (256,))]
-    for l in reversed(range(layers_n)):
-        pieces += [part.reshape(cut_shape + (-1,)) for part in parts[l]]
-    table, rk, hit, seats, turned = plan
-    grad_experts, summed = tail(
+        column_sources[l] = results[6:8]
+        smalls[l] = results[8]
+        row_sources[l] = results[9:11]
+    grad_experts, (small_sum, grad_qkv, grad_out) = tail(
         capacity,
         8,
         normed_all,
         grads_all,
         own_shard,
-        table,
-        hit,
-        seats,
+        (plan[0], plan[2], plan[3]),
         experts,
         owns,
-        pieces,
+        row_sources,
+        column_sources,
+        smalls,
     )
-    small_sum = summed[0][:, :128] + summed[0][:, 128:]
-    grad_qkv = jnp.stack([summed[1 + 2 * (layers_n - 1 - l)] for l in range(layers_n)])
-    grad_out = jnp.stack([summed[2 + 2 * (layers_n - 1 - l)] for l in range(layers_n)])
-    small_sum = small_sum[:, : layers_n * wide].reshape(-1, layers_n, wide)
+    small_sum = small_sum[:, :128] + small_sum[:, 128:]
+    small_sum = small_sum[:, : layers_n * SMALL].reshape(-1, layers_n, SMALL)
     small_sum = jnp.swapaxes(small_sum, 0, 1)
     grad_router = small_sum[:, :, :experts_n]
-    grad_gains = jnp.swapaxes(small_sum[:, :, experts_n:], 1, 2)
+    grad_gains = jnp.swapaxes(small_sum[:, :, experts_n : experts_n + 2], 1, 2)
     return (
         jnp.stack(outputs),
         grads,

time: 648 us -> 582 us (0.90)
  Pallas kernels: 567 us -> 531 us
  matrix products: 18.6 us -> 0 us
    pallas_call x1, Pallas kernels: 170 us -> 134 us  [tail(): pl.pallas_call(partial(tail_kernel, layers_n, capacity), out_shape=[shape...]
    dot_general x4 -> x0, matrix products: 18.6 us -> none  [local_chips(): lax.dot_general(one, another, (((0,), (0,)), ((), ())), preferred_element...]
    pallas_call x2, Pallas kernels: 143 us -> 158 us  [layer_backward(): pl.pallas_call(partial(backward_kernel, layer, layers_n, capacity), out_s...]
    pallas_call x2, Pallas kernels: 254 us -> 240 us  [layer_forward(): pl.pallas_call(partial(forward_kernel, layer, layers_n, capacity), out_sh...]
    unnamed x36 -> x20, local copies, waits for them, and re-layouts: 11.9 us -> 15.8 us
  transfers between devices with their start and end apart: 13 -> 2, of which waited for: 0 -> 0; matrix products, arithmetic and copies ran while one was open for 5% -> 0% of each run, Pallas kernels for 62% -> 43%
where the time goes in v3:
time: 582 us; the launch traced here: 574 us
  Pallas kernels  531 us (91%)
  local copies, waits for them, and re-layouts  22.2 us (4%)
  between operations  14.6 us (3%)
    pallas_call x2, Pallas kernels, layer_forward(): pl.pallas_call(partial(forward_kernel, layer, layers_n, capacity), out_sh...  240 us
    pallas_call x2, Pallas kernels, layer_backward(): pl.pallas_call(partial(backward_kernel, layer, layers_n, capacity), out_s...  158 us
    pallas_call x1, Pallas kernels, tail(): pl.pallas_call(partial(tail_kernel, layers_n, capacity), out_shape=[shape...  134 us
    unnamed x20, local copies, waits for them, and re-layouts  15.8 us
  transfers between devices with their start and end apart: 2, of which 0 were waited for; matrix products, arithmetic and copies ran while one was open for 0% of the time, Pallas kernels for 43%

profile of v3, /device:TPU:8, one launch (start us, length us, event | category | flops | bytes accessed | tf_op | source)
XLA Modules:
  0.0 573.9 jit_solution(8491189366454323437)
XLA Ops:
  7.2 0.0 all-gather.5.cloned.1.call-start
  7.2 1.4 copy.48.refs_3_.refs_4_
  8.6 0.8 copy.47
  9.4 0.7 fusion.11
  10.1 0.1 copy.54
  10.2 0.1 copy.53
  10.3 0.7 reduce
  11.0 0.1 reshape.208
  11.2 0.4 slice_reduce_fusion.3
  11.5 0.8 fusion.12
  12.4 0.7 convert_reduce_fusion
  13.1 0.1 eq.140
  13.2 0.1 pad.9.clone
  13.3 0.3 fusion.3
  13.6 0.1 bitcast_select_fusion
  13.7 0.8 maximum_bitcast_fusion
  14.4 0.7 fusion.9.refs_4_
  15.1 1.3 add_add_fusion.refs_5_
  16.5 150.7 %layer_forward.2 = (f32[128,1536]{1,0:T(8,128)}, bf16[128,1536]{1,0:T(8,128)(2,1)}, bf16[128,1536]{1,0:T(8,128)(2,1)}, bf16[128,1536]{1,0:T(8,128)(2,1)}, bf16[2...) custom-call(bf16[128,1536]{1,0:T(8,128)(2,1)} %refs_1_.1, ...), custom_call_target="tpu_custom_call" | custom-call | tf_op jit(solution)/shard_map/layer_forward/pallas_call | solution.py:1432
  167.1 0.0 all-gather.5.cloned.1.call-update
  167.2 0.0 all-gather.7.cloned.1.call-start
  167.2 88.9 %layer_forward.3 = (f32[128,1536]{1,0:T(8,128)}, bf16[128,1536]{1,0:T(8,128)(2,1)}, bf16[128,1536]{1,0:T(8,128)(2,1)}, bf16[128,1536]{1,0:T(8,128)(2,1)}, bf16[2...) custom-call(f32[128,1536]{1,0:T(8,128)} %get-tuple-element.73.refs_0, ...), custom_call_target="tpu_custom_call" | custom-call | tf_op jit(solution)/shard_map/layer_forward/pallas_call | solution.py:1432
  256.1 0.0 all-gather.7.cloned.1.call-update
  256.1 80.0 %layer_backward.2 = (f32[128,1536]{1,0:T(8,128)}, bf16[128,1536]{1,0:T(8,128)(2,1)}, bf16[576,1536]{1,0:T(8,128)(2,1)}, bf16[576,768]{1,0:T(8,128)(2,1)}, bf16[5...) custom-call(bf16[128,1536]{1,0:T(8,128)(2,1)} %refs_0_.3, ...), custom_call_target="tpu_custom_call" | custom-call | tf_op jit(solution)/shard_map/layer_backward/pallas_call | solution.py:1721
  336.1 0.0 copy-start.2
  336.1 0.0 copy-start.3
  336.1 77.8 %layer_backward.3 = (f32[128,1536]{1,0:T(8,128)}, bf16[128,1536]{1,0:T(8,128)(2,1)}, bf16[576,1536]{1,0:T(8,128)(2,1)}, bf16[576,768]{1,0:T(8,128)(2,1)}, bf16[5...) custom-call(f32[128,1536]{1,0:T(8,128)} %get-tuple-element.92.refs_0, ...), custom_call_target="tpu_custom_call" | custom-call | tf_op jit(solution)/shard_map/layer_backward/pallas_call | solution.py:1721
  413.9 0.0 copy-done.2
  413.9 0.0 copy-done.3
  413.9 0.9 pad_maximum_fusion
  414.9 0.0 all-gather.5.cloned.1.call-done
  414.9 0.0 all-gather.7.cloned.1.call-done
  414.9 0.0 copy-start.1
  414.9 134.1 %tail.1 = (f32[2,2,384,768]{3,2,1,0:T(8,128)}, f32[2,2,384,768]{3,2,1,0:T(8,128)}, f32[2,2,768,384]{3,2,1,0:T(8,128)}, bf16[4,8,128,1536]{3,2,1,0:T(8,128)(2,1)}...) custom-call(bf16[4,4,128,1536]{3,2,1,0:T(8,128)(2,1)} %bitcast.71, ...), custom_call_target="tpu_custom_call" | custom-call | tf_op jit(solution)/shard_map/tail/pallas_call | solution.py:910
  549.0 0.8 fusion.10
  549.8 0.1 copy.52
  549.9 0.6 slice.70
  550.5 0.6 slice_bitcast_fusion
  551.1 0.0 copy-done.1
  551.1 0.9 copy.61
  551.9 2.1 copy.62
  554.0 1.9 copy.63
  555.9 0.0 copy-start
  555.9 0.0 slice-start
  555.9 5.2 copy.64
  561.1 0.0 copy-done
  561.1 0.0 slice-start.1
  561.1 2.4 copy.65
  563.5 0.4 slice-done
  564.0 0.6 slice-done.1
  564.5 2.2 copy.66
  (8 shorter events, 0.0 us)
Async XLA Ops:
  7.2 407.7 %all-gather.5.cloned.1.call-start = ((), (), s32[]{:S(2)}) async-start(), calls=%async_computation | async-start | bytes 7864320 | tf_op jit(solution)/shard_map/all_gather | solution.py:2016
  167.2 247.7 %all-gather.7.cloned.1.call-start = ((), (), s32[]{:S(2)}) async-start(), calls=%async_computation.1 | async-start | bytes 7864320 | tf_op jit(solution)/shard_map/all_gather | solution.py:2016
  336.1 77.8 %copy-start.2 = (bf16[128,1536]{1,0:T(8,128)(2,1)S(1)}, bf16[128,1536]{1,0:T(8,128)(2,1)}, u32[]{:S(2)}) copy-start(bf16[128,1536]{1,0:T(8,128)(2,1)} %get-tuple-element.72) | copy-start | bytes 1179652
  336.1 77.8 %copy-start.3 = (bf16[128,1536]{1,0:T(8,128)(2,1)S(1)}, bf16[128,1536]{1,0:T(8,128)(2,1)}, u32[]{:S(2)}) copy-start(bf16[128,1536]{1,0:T(8,128)(2,1)} %get-tuple-element.82) | copy-start | bytes 1179652
  414.9 136.2 %copy-start.1 = (f32[128,1536]{1,0:T(8,128)S(1)}, f32[128,1536]{1,0:T(8,128)}, u32[]{:S(2)}) copy-start(f32[128,1536]{1,0:T(8,128)} %get-tuple-element.162) | copy-start | bytes 2359300
  555.9 5.2 copy-start
  555.9 8.0 %slice-start = ((s8[4718592]{0:T(1024)(128)(4,1)}), s8[4194304]{0:T(1024)(128)(4,1)S(1)}, s32[]{:S(2)}) async-start(s8[4718592]{0:T(1024)(128)(4,1)} %bitcast.73), calls=%async_computation.2 | async-start | bytes 8388608
  561.1 3.4 slice-start.1
Sparse Core Ops, SparseCore 0:
  167.3 112.7 all-gather.4
  281.7 113.5 all-gather.6

commit v4 on v3

--- a/solution.py
+++ b/solution.py
@@ -1047,7 +1047,7 @@
         table, rk, hit, seats, turned, cross_from, qkv_from, out_from = some(8)
     w_gate, w_up, w_down = some(3)
     new_stream, layer_out, normed_a, queries, kv_out, attended, mixed, normed_b = some(8)
-    rows_in, gate_pre, up_pre, gate_seat, quad = some(5)
+    rows_out, gate_out, up_out, gate_seat, quad = some(5)
     if first:
         table, rk_out, hit, seats, turned, qkv_out, out_out, qkv_next, out_next = some(9)
         (line_grads,) = some(1)
@@ -1071,7 +1071,11 @@
         quad_sem,
         send,
         recv,
-    ) = some(16)
+        rows_in,
+        gate_pre,
+        up_pre,
+        leave_sem,
+    ) = some(20)
     if first:
         send_0, recv_0, send_1, recv_1, send_2, recv_2, send_3, recv_3 = some(8)
         send_4, recv_4, keep = some(3)
@@ -1090,7 +1094,8 @@
         pltpu.make_async_copy(src.at[layer], dst, weight_sem.at[i])
         for i, (src, dst) in enumerate(((w_gate, gate_w), (w_up, up_w), (w_down, down_w)))
     ]
-    greet(z, near, ("x", "y", "c"), line, (behind, ahead, has_behind, has_ahead))
+    order = (behind, ahead, has_behind, has_ahead)
+    greet(z, near, ("x", "y", "c"), line if first else None, order)
     if not first:
         cross = Gather([cross_from.at[0]], [cross_to], cross_send, cross_recv, z, near, line)
         cross.spread(1, cross_from, cross_keep)
@@ -1263,6 +1268,10 @@
         g3.arrivals(2, g3.take)
     two()
     three()
+    if not first:
+        cross.second(cross.plane_of(2))
+        cross.spread(3, cross_from, cross_keep)
+        cross.third(cross.plane_of(1))
     if first:
         g3.third(z)
         g3.arrivals(1, g3.second)
@@ -1291,10 +1300,6 @@
         g3.arrivals(1, g3.third)
         g3.arrivals(2, g3.second)
         g4.arrivals(1, g4.carry)
-    else:
-        cross.second(cross.plane_of(2))
-        cross.spread(3, cross_from, cross_keep)
-
     def expert(k, carry):
         here = pl.ds(pl.multiple_of(k * number, 32), number)
         x = rows_in[here]
@@ -1307,6 +1312,12 @@
         return carry
 
     lax.fori_loop(0, local_n, expert, 0)
+    leaving = [
+        pltpu.make_async_copy(src, dst, leave_sem.at[i])
+        for i, (src, dst) in enumerate(((rows_in, rows_out), (gate_pre, gate_out), (up_pre, up_out)))
+    ]
+    for copied in leaving:
+        copied.start()
     if first:
         g3.arrivals(2, g3.third)
         g3.arrivals(3, g3.second)
@@ -1318,7 +1329,7 @@
         for copied in out_copies:
             copied.start()
     else:
-        cross.third(cross.plane_of(1))
+        cross.third(cross.plane_of(2))
         cross.second(cross.plane_of(3))
 
     def make(name):
@@ -1330,7 +1341,7 @@
     plane_sum(make, new_stream, mixed, scratch, near)
     layer_out[...] = new_stream[...].astype(bf16)
 
-    for copied in quads:
+    for copied in quads + leaving:
         copied.wait()
 
     @pl.when(has_ahead)
@@ -1348,7 +1359,6 @@
         for g in (g0, g1, g2, g3, g4):
             g.line_done()
     else:
-        cross.third(cross.plane_of(2))
         cross.third(cross.plane_of(3))
         cross.spread_done(cross_from, cross_keep)
 
@@ -1379,7 +1389,7 @@
         shape((seats_n, 1), f32),
         shape((len(QUAD), rows, width), bf16),
     ]
-    specs = [VMEM] * 12 + [HBM]
+    specs = [VMEM] * 8 + [HBM] * 3 + [VMEM, HBM]
     scratch = []
     full_qkv = (n_dp, n_expert, cut_rows, width + 2 * keys_n)
     full_out = (n_dp, n_expert, cut_rows, width)
@@ -1420,6 +1430,10 @@
         pltpu.SemaphoreType.DMA((len(QUAD),)),
         pltpu.SemaphoreType.DMA((8,)),
         pltpu.SemaphoreType.DMA((8,)),
+        pltpu.VMEM((seats_n, width), bf16),
+        pltpu.VMEM((seats_n, hidden), f32),
+        pltpu.VMEM((seats_n, hidden), f32),
+        pltpu.SemaphoreType.DMA((3,)),
     ]
     if first:
         for count in (2, 1, 1, 2, 1):
@@ -1457,11 +1471,12 @@
         return taken
 
     grad_stream, stream, cosine, sine, seg_column = some(5)
-    mixed, normed_b, queries, kv, gate_pre, up_pre, gate_seat = some(7)
+    mixed, normed_b, queries, kv, gate_seat = some(5)
     table, rk, hit, seats, turned = some(5)
     row_sources = some(2)
     qkv_from, out_from, w_gate, w_up, w_down = some(5)
-    grad_out, grad_low, rows_grad, hidden_low, dgate_low, dup_low = some(6)
+    gate_from, up_from = some(2)
+    grad_out, grad_low, *leaving_to = some(6)
     dprojected, grad_attn, small = some(3)
     row_lands = some(2)
     (
@@ -1486,7 +1501,14 @@
         row_send,
         row_recv,
         row_keep,
-    ) = some(21)
+        gate_pre,
+        up_pre,
+        rows_grad,
+        hidden_low,
+        dgate_low,
+        dup_low,
+        leave_sem,
+    ) = some(28)
     scratch = refs
     z, near = place()
     e = near["own"]
@@ -1503,6 +1525,10 @@
         pltpu.make_async_copy(qkv_from, qkv, load_sem.at[0]),
         pltpu.make_async_copy(out_from, w_o, load_sem.at[1]),
     ]
+    weights += [
+        pltpu.make_async_copy(gate_from, gate_pre, leave_sem.at[4]),
+        pltpu.make_async_copy(up_from, up_pre, leave_sem.at[5]),
+    ]
     grad_low[...] = grad_stream[...].astype(bf16)
     greet(z, near, ("x", "y", "c"), None, (behind, ahead, has_behind, has_ahead))
 
@@ -1533,11 +1559,12 @@
     second()
     prepare(range(5, 9))
     third()
+    spreads[0].first(0, spreads[0].ins)
+    spreads[1].first(0, spreads[1].ins)
+    for one in kept:
+        one.start()
     prepare(range(9, QUERY_HEADS))
     finish()
-    spreads[0].first(0, spreads[0].ins)
-    for one in kept:
-        one.start()
     everyone = tokens[...].reshape(-1, width)
     picked = mul(seat_rows(seats[layer, z], number), everyone)
     back_rows[:, pl.ds(0, width)] = picked.astype(bf16)
@@ -1571,6 +1598,12 @@
         return carry
 
     lax.fori_loop(0, local_n, expert, 0)
+    leaving = [
+        pltpu.make_async_copy(src, dst, leave_sem.at[i])
+        for i, (src, dst) in enumerate(zip((rows_grad, hidden_low, dgate_low, dup_low), leaving_to))
+    ]
+    for one in leaving:
+        one.start()
 
     def make(name):
         d = near[name]
@@ -1581,7 +1614,7 @@
     spreads[0].second(0)
     plane_sum(make, summed, None, scratch, near)
     spreads[0].third(0)
-    spreads[1].first(0, spreads[1].ins)
+    spreads[1].second(0)
 
     over = ((0,), (0,))
     gain = 2 * experts_n + 2 * layer
@@ -1622,7 +1655,7 @@
             dkeys = dkeys + mul(dscores, query, over)
             dvalues = dvalues + mul(probs.astype(bf16), given, over)
         if group == 0:
-            spreads[1].second(0)
+            spreads[1].third(0)
         dkv[:, head_of(group)] = dkeys * scale
         dkv[:, head_of(KEY_VALUE_HEADS + group)] = dvalues
     dkv_send[...] = dkv[pl.ds(0, rows)].astype(bf16)
@@ -1667,7 +1700,9 @@
     def passed_back():
         pass_on(behind).wait_send()
 
-    spreads[1].third(0)
+    for one in leaving:
+        one.wait()
+
     for i in range(2):
         spreads[i].finish(0)
         kept[i].wait()
@@ -1676,7 +1711,7 @@
 def layer_backward(layer, number, shapes, grads, stream, tables, saved, plan, weights):
     layers_n, n_dp, n_expert, local_n, capacity = shapes
     rows, width = stream.shape
-    hidden = weights[-1].shape[2]
+    hidden = weights[-1].shape[1]
     experts_n = local_n * n_expert
     seats_n = local_n * capacity
     keys_n = KEY_VALUE_HEADS * HEAD_SIZE
@@ -1717,12 +1752,19 @@
         pltpu.SemaphoreType.DMA((2, 1, 1, KINDS)),
         pltpu.SemaphoreType.DMA((2, 1, 1, KINDS)),
         pltpu.SemaphoreType.DMA((2,)),
+        pltpu.VMEM((seats_n, hidden), f32),
+        pltpu.VMEM((seats_n, hidden), f32),
+        pltpu.VMEM((seats_n, width), bf16),
+        pltpu.VMEM((seats_n, hidden), bf16),
+        pltpu.VMEM((seats_n, hidden), bf16),
+        pltpu.VMEM((seats_n, hidden), bf16),
+        pltpu.SemaphoreType.DMA((6,)),
     ]
     return pl.pallas_call(
         partial(backward_kernel, layer, layers_n, capacity),
         out_shape=outs,
-        in_specs=[VMEM] * 17 + [HBM] * 7,
-        out_specs=[VMEM] * 9 + [HBM] * 2,
+        in_specs=[VMEM] * 15 + [HBM] * 9,
+        out_specs=[VMEM] * 2 + [HBM] * 4 + [VMEM] * 3 + [HBM] * 2,
         scratch_shapes=scratch + sum_scratch(rows, width + 128),
         compiler_params=settings(number),
         name="layer_backward",
@@ -2037,8 +2079,9 @@
     row_sources, column_sources = [None] * layers_n, [None] * layers_n
     for l in reversed(range(layers_n)):
         normed_a, queries, kv, attended, mixed, normed_b, rows_in = saved[l][:7]
-        kept = (mixed, normed_b, queries, kv, *saved[l][7:])
-        sources = (normed_a, attended, *full[l], *experts)
+        gate_pre, up_pre, gate_seat = saved[l][7:]
+        kept = (mixed, normed_b, queries, kv, gate_seat)
+        sources = (normed_a, attended, *full[l], *experts, gate_pre, up_pre)
         results = layer_backward(l, 4 + l, shapes, grads, streams[l], tables, kept, plan, sources)
         grads, own_shard = results[:2]
         owns[l] = (rows_in, *results[2:6])

time: 582 us -> 565 us (0.971)
  Pallas kernels: 531 us -> 514 us
    pallas_call x2, Pallas kernels: 158 us -> 142 us  [layer_backward(): pl.pallas_call(partial(backward_kernel, layer, layers_n, capacity), out_s...]
  transfers between devices with their start and end apart: 2 -> 2, of which waited for: 0 -> 0; matrix products, arithmetic and copies ran while one was open for 0% -> 0% of each run, Pallas kernels for 43% -> 41%
where the time goes in v4:
time: 565 us; the launch traced here: 556 us
  Pallas kernels  514 us (91%)
  local copies, waits for them, and re-layouts  22.2 us (4%)
  between operations  14.6 us (3%)
    pallas_call x2, Pallas kernels, layer_forward(): pl.pallas_call(partial(forward_kernel, layer, layers_n, capacity), out_sh...  235 us
    pallas_call x2, Pallas kernels, layer_backward(): pl.pallas_call(partial(backward_kernel, layer, layers_n, capacity), out_s...  142 us
    pallas_call x1, Pallas kernels, tail(): pl.pallas_call(partial(tail_kernel, layers_n, capacity), out_shape=[shape...  137 us
    unnamed x20, local copies, waits for them, and re-layouts  15.8 us
  transfers between devices with their start and end apart: 2, of which 0 were waited for; matrix products, arithmetic and copies ran while one was open for 0% of the time, Pallas kernels for 41%

profile of v4, /device:TPU:8, one launch (start us, length us, event | category | flops | bytes accessed | tf_op | source)
XLA Modules:
  0.0 556.5 jit_solution(6042261846937336718)
XLA Ops:
  7.2 0.0 all-gather.5.cloned.1.call-start
  7.2 1.4 copy.48.refs_3_.refs_4_
  8.6 0.8 copy.47
  9.4 0.7 fusion.11
  10.1 0.1 copy.54
  10.2 0.1 copy.53
  10.3 0.7 reduce
  11.0 0.1 reshape.208
  11.2 0.4 slice_reduce_fusion.3
  11.5 0.8 fusion.12
  12.4 0.7 convert_reduce_fusion
  13.1 0.1 eq.140
  13.2 0.1 pad.9.clone
  13.3 0.3 fusion.3
  13.6 0.1 bitcast_select_fusion
  13.7 0.8 maximum_bitcast_fusion
  14.4 0.7 fusion.9.refs_4_
  15.1 1.3 add_add_fusion.refs_5_
  16.5 149.1 %layer_forward.2 = (f32[128,1536]{1,0:T(8,128)}, bf16[128,1536]{1,0:T(8,128)(2,1)}, bf16[128,1536]{1,0:T(8,128)(2,1)}, bf16[128,1536]{1,0:T(8,128)(2,1)}, bf16[2...) custom-call(bf16[128,1536]{1,0:T(8,128)(2,1)} %refs_1_.1, ...), custom_call_target="tpu_custom_call" | custom-call | tf_op jit(solution)/shard_map/layer_forward/pallas_call | solution.py:1446
  165.6 0.0 all-gather.5.cloned.1.call-update
  165.6 0.0 all-gather.7.cloned.1.call-start
  165.7 85.7 %layer_forward.3 = (f32[128,1536]{1,0:T(8,128)}, bf16[128,1536]{1,0:T(8,128)(2,1)}, bf16[128,1536]{1,0:T(8,128)(2,1)}, bf16[128,1536]{1,0:T(8,128)(2,1)}, bf16[2...) custom-call(f32[128,1536]{1,0:T(8,128)} %get-tuple-element.73.refs_0, ...), custom_call_target="tpu_custom_call" | custom-call | tf_op jit(solution)/shard_map/layer_forward/pallas_call | solution.py:1446
  251.4 0.0 all-gather.7.cloned.1.call-update
  251.4 68.3 %layer_backward.2 = (f32[128,1536]{1,0:T(8,128)}, bf16[128,1536]{1,0:T(8,128)(2,1)}, bf16[576,1536]{1,0:T(8,128)(2,1)}, bf16[576,768]{1,0:T(8,128)(2,1)}, bf16[5...) custom-call(bf16[128,1536]{1,0:T(8,128)(2,1)} %refs_0_.3, ...), custom_call_target="tpu_custom_call" | custom-call | tf_op jit(solution)/shard_map/layer_backward/pallas_call | solution.py:1763
  319.7 0.0 copy-start.2
  319.7 0.0 copy-start.3
  319.7 74.1 %layer_backward.3 = (f32[128,1536]{1,0:T(8,128)}, bf16[128,1536]{1,0:T(8,128)(2,1)}, bf16[576,1536]{1,0:T(8,128)(2,1)}, bf16[576,768]{1,0:T(8,128)(2,1)}, bf16[5...) custom-call(f32[128,1536]{1,0:T(8,128)} %get-tuple-element.92.refs_0, ...), custom_call_target="tpu_custom_call" | custom-call | tf_op jit(solution)/shard_map/layer_backward/pallas_call | solution.py:1763
  393.8 0.0 copy-done.2
  393.9 0.0 copy-done.3
  393.9 0.9 pad_maximum_fusion
  394.8 0.0 all-gather.5.cloned.1.call-done
  394.8 0.0 all-gather.7.cloned.1.call-done
  394.8 0.0 copy-start.1
  394.8 136.7 %tail.1 = (f32[2,2,384,768]{3,2,1,0:T(8,128)}, f32[2,2,384,768]{3,2,1,0:T(8,128)}, f32[2,2,768,384]{3,2,1,0:T(8,128)}, bf16[4,8,128,1536]{3,2,1,0:T(8,128)(2,1)}...) custom-call(bf16[4,4,128,1536]{3,2,1,0:T(8,128)(2,1)} %bitcast.71, ...), custom_call_target="tpu_custom_call" | custom-call | tf_op jit(solution)/shard_map/tail/pallas_call | solution.py:910
  531.6 0.8 fusion.10
  532.3 0.1 copy.52
  532.4 0.6 slice.70
  533.0 0.6 slice_bitcast_fusion
  533.6 0.0 copy-done.1
  533.6 0.9 copy.61
  534.5 2.1 copy.62
  536.6 1.9 copy.63
  538.5 0.0 copy-start
  538.5 0.0 slice-start
  538.5 5.2 copy.64
  543.7 0.0 copy-done
  543.7 0.0 slice-start.1
  543.7 2.4 copy.65
  546.1 0.4 slice-done
  546.5 0.6 slice-done.1
  547.1 2.2 copy.66
  (8 shorter events, 0.0 us)
Async XLA Ops:
  7.2 387.6 %all-gather.5.cloned.1.call-start = ((), (), s32[]{:S(2)}) async-start(), calls=%async_computation | async-start | bytes 7864320 | tf_op jit(solution)/shard_map/all_gather | solution.py:2058
  165.6 229.2 %all-gather.7.cloned.1.call-start = ((), (), s32[]{:S(2)}) async-start(), calls=%async_computation.1 | async-start | bytes 7864320 | tf_op jit(solution)/shard_map/all_gather | solution.py:2058
  319.7 74.1 %copy-start.2 = (bf16[128,1536]{1,0:T(8,128)(2,1)S(1)}, bf16[128,1536]{1,0:T(8,128)(2,1)}, u32[]{:S(2)}) copy-start(bf16[128,1536]{1,0:T(8,128)(2,1)} %get-tuple-element.72) | copy-start | bytes 1179652
  319.7 74.1 %copy-start.3 = (bf16[128,1536]{1,0:T(8,128)(2,1)S(1)}, bf16[128,1536]{1,0:T(8,128)(2,1)}, u32[]{:S(2)}) copy-start(bf16[128,1536]{1,0:T(8,128)(2,1)} %get-tuple-element.82) | copy-start | bytes 1179652
  394.8 138.8 %copy-start.1 = (f32[128,1536]{1,0:T(8,128)S(1)}, f32[128,1536]{1,0:T(8,128)}, u32[]{:S(2)}) copy-start(f32[128,1536]{1,0:T(8,128)} %get-tuple-element.162) | copy-start | bytes 2359300
  538.5 5.2 copy-start
  538.5 8.0 %slice-start = ((s8[4718592]{0:T(1024)(128)(4,1)}), s8[4194304]{0:T(1024)(128)(4,1)S(1)}, s32[]{:S(2)}) async-start(s8[4718592]{0:T(1024)(128)(4,1)} %bitcast.73), calls=%async_computation.2 | async-start | bytes 8388608
  543.7 3.4 slice-start.1
Sparse Core Ops, SparseCore 0:
  165.7 112.7 all-gather.4
  280.1 113.5 all-gather.6

commit v5 on v4

--- a/solution.py
+++ b/solution.py
@@ -1128,6 +1128,7 @@
         g1.arrivals(1, g1.take)
         g2.line_first()
         g2.first(z, g2.ins)
+        g3.line_first()
         g0.arrivals(1, g0.third)
         g0.arrivals(2, g0.second)
         g1.second(z)
@@ -1219,7 +1220,6 @@
     if first:
         g2.arrivals(1, g2.third)
         g2.arrivals(2, g2.second)
-        g3.line_first()
         g3.first(z, g3.ins)
     else:
         cross.spread(2, cross_from, cross_keep)

time: 565 us -> 565 us (level)
  no operation moved by 1% of the time
where the time goes in v5:
time: 565 us; the launch traced here: 557 us
  Pallas kernels  515 us (91%)
  local copies, waits for them, and re-layouts  22.2 us (4%)
  between operations  14.6 us (3%)
    pallas_call x2, Pallas kernels, layer_forward(): pl.pallas_call(partial(forward_kernel, layer, layers_n, capacity), out_sh...  235 us
    pallas_call x2, Pallas kernels, layer_backward(): pl.pallas_call(partial(backward_kernel, layer, layers_n, capacity), out_s...  142 us
    pallas_call x1, Pallas kernels, tail(): pl.pallas_call(partial(tail_kernel, layers_n, capacity), out_shape=[shape...  138 us
    unnamed x20, local copies, waits for them, and re-layouts  15.8 us
  transfers between devices with their start and end apart: 2, of which 0 were waited for; matrix products, arithmetic and copies ran while one was open for 0% of the time, Pallas kernels for 41%

profile of v5, /device:TPU:8, one launch (start us, length us, event | category | flops | bytes accessed | tf_op | source)
XLA Modules:
  0.0 557.3 jit_solution(7752983742180319071)
XLA Ops:
  7.2 0.0 all-gather.5.cloned.1.call-start
  7.2 1.4 copy.48.refs_3_.refs_4_
  8.6 0.8 copy.47
  9.4 0.7 fusion.11
  10.1 0.1 copy.54
  10.2 0.1 copy.53
  10.3 0.7 reduce
  11.0 0.1 reshape.208
  11.2 0.4 slice_reduce_fusion.3
  11.5 0.8 fusion.12
  12.4 0.7 convert_reduce_fusion
  13.1 0.1 eq.140
  13.2 0.1 pad.9.clone
  13.3 0.3 fusion.3
  13.6 0.1 bitcast_select_fusion
  13.7 0.8 maximum_bitcast_fusion
  14.4 0.7 fusion.9.refs_4_
  15.1 1.3 add_add_fusion.refs_5_
  16.5 149.1 %layer_forward.2 = (f32[128,1536]{1,0:T(8,128)}, bf16[128,1536]{1,0:T(8,128)(2,1)}, bf16[128,1536]{1,0:T(8,128)(2,1)}, bf16[128,1536]{1,0:T(8,128)(2,1)}, bf16[2...) custom-call(bf16[128,1536]{1,0:T(8,128)(2,1)} %refs_1_.1, ...), custom_call_target="tpu_custom_call" | custom-call | tf_op jit(solution)/shard_map/layer_forward/pallas_call | solution.py:1446
  165.6 0.0 all-gather.5.cloned.1.call-update
  165.6 0.0 all-gather.7.cloned.1.call-start
  165.7 85.7 %layer_forward.3 = (f32[128,1536]{1,0:T(8,128)}, bf16[128,1536]{1,0:T(8,128)(2,1)}, bf16[128,1536]{1,0:T(8,128)(2,1)}, bf16[128,1536]{1,0:T(8,128)(2,1)}, bf16[2...) custom-call(f32[128,1536]{1,0:T(8,128)} %get-tuple-element.73.refs_0, ...), custom_call_target="tpu_custom_call" | custom-call | tf_op jit(solution)/shard_map/layer_forward/pallas_call | solution.py:1446
  251.3 0.0 all-gather.7.cloned.1.call-update
  251.4 68.3 %layer_backward.2 = (f32[128,1536]{1,0:T(8,128)}, bf16[128,1536]{1,0:T(8,128)(2,1)}, bf16[576,1536]{1,0:T(8,128)(2,1)}, bf16[576,768]{1,0:T(8,128)(2,1)}, bf16[5...) custom-call(bf16[128,1536]{1,0:T(8,128)(2,1)} %refs_0_.3, ...), custom_call_target="tpu_custom_call" | custom-call | tf_op jit(solution)/shard_map/layer_backward/pallas_call | solution.py:1763
  319.7 0.0 copy-start.2
  319.7 0.0 copy-start.3
  319.7 74.1 %layer_backward.3 = (f32[128,1536]{1,0:T(8,128)}, bf16[128,1536]{1,0:T(8,128)(2,1)}, bf16[576,1536]{1,0:T(8,128)(2,1)}, bf16[576,768]{1,0:T(8,128)(2,1)}, bf16[5...) custom-call(f32[128,1536]{1,0:T(8,128)} %get-tuple-element.92.refs_0, ...), custom_call_target="tpu_custom_call" | custom-call | tf_op jit(solution)/shard_map/layer_backward/pallas_call | solution.py:1763
  393.8 0.0 copy-done.2
  393.8 0.0 copy-done.3
  393.8 0.9 pad_maximum_fusion
  394.8 0.0 all-gather.5.cloned.1.call-done
  394.8 0.0 all-gather.7.cloned.1.call-done
  394.8 0.0 copy-start.1
  394.8 137.6 %tail.1 = (f32[2,2,384,768]{3,2,1,0:T(8,128)}, f32[2,2,384,768]{3,2,1,0:T(8,128)}, f32[2,2,768,384]{3,2,1,0:T(8,128)}, bf16[4,8,128,1536]{3,2,1,0:T(8,128)(2,1)}...) custom-call(bf16[4,4,128,1536]{3,2,1,0:T(8,128)(2,1)} %bitcast.71, ...), custom_call_target="tpu_custom_call" | custom-call | tf_op jit(solution)/shard_map/tail/pallas_call | solution.py:910
  532.4 0.8 fusion.10
  533.2 0.1 copy.52
  533.3 0.6 slice.70
  533.9 0.6 slice_bitcast_fusion
  534.5 0.0 copy-done.1
  534.5 0.9 copy.61
  535.4 2.1 copy.62
  537.4 1.9 copy.63
  539.3 0.0 copy-start
  539.3 0.0 slice-start
  539.3 5.2 copy.64
  544.5 0.0 copy-done
  544.5 0.0 slice-start.1
  544.5 2.4 copy.65
  546.9 0.4 slice-done
  547.4 0.6 slice-done.1
  547.9 2.2 copy.66
  (8 shorter events, 0.0 us)
Async XLA Ops:
  7.2 387.6 %all-gather.5.cloned.1.call-start = ((), (), s32[]{:S(2)}) async-start(), calls=%async_computation | async-start | bytes 7864320 | tf_op jit(solution)/shard_map/all_gather | solution.py:2058
  165.6 229.2 %all-gather.7.cloned.1.call-start = ((), (), s32[]{:S(2)}) async-start(), calls=%async_computation.1 | async-start | bytes 7864320 | tf_op jit(solution)/shard_map/all_gather | solution.py:2058
  319.7 74.1 %copy-start.2 = (bf16[128,1536]{1,0:T(8,128)(2,1)S(1)}, bf16[128,1536]{1,0:T(8,128)(2,1)}, u32[]{:S(2)}) copy-start(bf16[128,1536]{1,0:T(8,128)(2,1)} %get-tuple-element.72) | copy-start | bytes 1179652
  319.7 74.1 %copy-start.3 = (bf16[128,1536]{1,0:T(8,128)(2,1)S(1)}, bf16[128,1536]{1,0:T(8,128)(2,1)}, u32[]{:S(2)}) copy-start(bf16[128,1536]{1,0:T(8,128)(2,1)} %get-tuple-element.82) | copy-start | bytes 1179652
  394.8 139.7 %copy-start.1 = (f32[128,1536]{1,0:T(8,128)S(1)}, f32[128,1536]{1,0:T(8,128)}, u32[]{:S(2)}) copy-start(f32[128,1536]{1,0:T(8,128)} %get-tuple-element.162) | copy-start | bytes 2359300
  539.3 5.2 copy-start
  539.3 8.0 %slice-start = ((s8[4718592]{0:T(1024)(128)(4,1)}), s8[4194304]{0:T(1024)(128)(4,1)S(1)}, s32[]{:S(2)}) async-start(s8[4718592]{0:T(1024)(128)(4,1)} %bitcast.73), calls=%async_computation.2 | async-start | bytes 8388608
  544.5 3.4 slice-start.1
Sparse Core Ops, SparseCore 0:
  165.7 112.7 all-gather.4
  280.1 113.5 all-gather.6

commit v6 on v4

--- a/solution.py
+++ b/solution.py
@@ -1263,9 +1263,6 @@
 
     one, two, three, four = plane_gather(normed_b, tokens, send, recv, near)
     one()
-    if first:
-        g3.second(z)
-        g3.arrivals(2, g3.take)
     two()
     three()
     if not first:
@@ -1273,9 +1270,9 @@
         cross.spread(3, cross_from, cross_keep)
         cross.third(cross.plane_of(1))
     if first:
-        g3.third(z)
+        g3.second(z)
         g3.arrivals(1, g3.second)
-        g3.arrivals(3, g3.take)
+        g3.arrivals(2, g3.take)
     four()
     quads = [
         pltpu.make_async_copy(tokens.at[near[name]], quad.at[i], quad_sem.at[i])
@@ -1297,6 +1294,8 @@
     for copied in weights:
         copied.wait()
     if first:
+        g3.third(z)
+        g3.arrivals(3, g3.take)
         g3.arrivals(1, g3.third)
         g3.arrivals(2, g3.second)
         g4.arrivals(1, g4.carry)

time: 565 us -> 565 us (level)
  transfers between devices with their start and end apart: 2 -> 2, of which waited for: 0 -> 1; matrix products, arithmetic and copies ran while one was open for 0% -> 0% of each run, Pallas kernels for 41% -> 41%
where the time goes in v6:
time: 565 us; the launch traced here: 557 us
  Pallas kernels  513 us (91%)
  local copies, waits for them, and re-layouts  22.2 us (4%)
  between operations  14.6 us (3%)
    pallas_call x2, Pallas kernels, layer_forward(): pl.pallas_call(partial(forward_kernel, layer, layers_n, capacity), out_sh...  233 us
    pallas_call x2, Pallas kernels, layer_backward(): pl.pallas_call(partial(backward_kernel, layer, layers_n, capacity), out_s...  143 us
    pallas_call x1, Pallas kernels, tail(): pl.pallas_call(partial(tail_kernel, layers_n, capacity), out_shape=[shape...  137 us
    unnamed x20, local copies, waits for them, and re-layouts  15.8 us
  transfers between devices with their start and end apart: 2, of which 1 were waited for; matrix products, arithmetic and copies ran while one was open for 0% of the time, Pallas kernels for 41%

profile of v6, /device:TPU:8, one launch (start us, length us, event | category | flops | bytes accessed | tf_op | source)
XLA Modules:
  0.0 556.7 jit_solution(4602558935800813356)
XLA Ops:
  7.2 0.0 all-gather.5.cloned.1.call-start
  7.2 1.4 copy.48.refs_3_.refs_4_
  8.6 0.8 copy.47
  9.4 0.7 fusion.11
  10.1 0.1 copy.54
  10.2 0.1 copy.53
  10.3 0.7 reduce
  11.0 0.1 reshape.208
  11.2 0.4 slice_reduce_fusion.3
  11.5 0.8 fusion.12
  12.4 0.7 convert_reduce_fusion
  13.1 0.1 eq.140
  13.2 0.1 pad.9.clone
  13.3 0.3 fusion.3
  13.6 0.1 bitcast_select_fusion
  13.7 0.8 maximum_bitcast_fusion
  14.4 0.7 fusion.9.refs_4_
  15.1 1.3 add_add_fusion.refs_5_
  16.5 147.2 %layer_forward.2 = (f32[128,1536]{1,0:T(8,128)}, bf16[128,1536]{1,0:T(8,128)(2,1)}, bf16[128,1536]{1,0:T(8,128)(2,1)}, bf16[128,1536]{1,0:T(8,128)(2,1)}, bf16[2...) custom-call(bf16[128,1536]{1,0:T(8,128)(2,1)} %refs_1_.1, ...), custom_call_target="tpu_custom_call" | custom-call | tf_op jit(solution)/shard_map/layer_forward/pallas_call | solution.py:1445
  163.7 0.0 all-gather.5.cloned.1.call-update
  163.7 0.0 all-gather.7.cloned.1.call-start
  163.8 85.8 %layer_forward.3 = (f32[128,1536]{1,0:T(8,128)}, bf16[128,1536]{1,0:T(8,128)(2,1)}, bf16[128,1536]{1,0:T(8,128)(2,1)}, bf16[128,1536]{1,0:T(8,128)(2,1)}, bf16[2...) custom-call(f32[128,1536]{1,0:T(8,128)} %get-tuple-element.73.refs_0, ...), custom_call_target="tpu_custom_call" | custom-call | tf_op jit(solution)/shard_map/layer_forward/pallas_call | solution.py:1445
  249.6 0.0 all-gather.7.cloned.1.call-update
  249.6 69.0 %layer_backward.2 = (f32[128,1536]{1,0:T(8,128)}, bf16[128,1536]{1,0:T(8,128)(2,1)}, bf16[576,1536]{1,0:T(8,128)(2,1)}, bf16[576,768]{1,0:T(8,128)(2,1)}, bf16[5...) custom-call(bf16[128,1536]{1,0:T(8,128)(2,1)} %refs_0_.3, ...), custom_call_target="tpu_custom_call" | custom-call | tf_op jit(solution)/shard_map/layer_backward/pallas_call | solution.py:1762
  318.6 0.0 copy-start.2
  318.6 0.0 copy-start.3
  318.6 74.0 %layer_backward.3 = (f32[128,1536]{1,0:T(8,128)}, bf16[128,1536]{1,0:T(8,128)(2,1)}, bf16[576,1536]{1,0:T(8,128)(2,1)}, bf16[576,768]{1,0:T(8,128)(2,1)}, bf16[5...) custom-call(f32[128,1536]{1,0:T(8,128)} %get-tuple-element.92.refs_0, ...), custom_call_target="tpu_custom_call" | custom-call | tf_op jit(solution)/shard_map/layer_backward/pallas_call | solution.py:1762
  392.7 0.0 copy-done.2
  392.7 0.0 copy-done.3
  392.7 0.9 pad_maximum_fusion
  393.6 0.0 all-gather.5.cloned.1.call-done
  393.6 0.9 all-gather.7.cloned.1.call-done
  394.6 0.0 copy-start.1
  394.6 137.2 %tail.1 = (f32[2,2,384,768]{3,2,1,0:T(8,128)}, f32[2,2,384,768]{3,2,1,0:T(8,128)}, f32[2,2,768,384]{3,2,1,0:T(8,128)}, bf16[4,8,128,1536]{3,2,1,0:T(8,128)(2,1)}...) custom-call(bf16[4,4,128,1536]{3,2,1,0:T(8,128)(2,1)} %bitcast.71, ...), custom_call_target="tpu_custom_call" | custom-call | tf_op jit(solution)/shard_map/tail/pallas_call | solution.py:910
  531.8 0.8 fusion.10
  532.5 0.1 copy.52
  532.6 0.6 slice.70
  533.2 0.6 slice_bitcast_fusion
  533.8 0.0 copy-done.1
  533.8 0.9 copy.61
  534.7 2.1 copy.62
  536.8 1.9 copy.63
  538.7 0.0 copy-start
  538.7 0.0 slice-start
  538.7 5.2 copy.64
  543.9 0.0 copy-done
  543.9 0.0 slice-start.1
  543.9 2.4 copy.65
  546.3 0.4 slice-done
  546.7 0.6 slice-done.1
  547.3 2.2 copy.66
  (8 shorter events, 0.0 us)
Async XLA Ops:
  7.2 386.4 %all-gather.5.cloned.1.call-start = ((), (), s32[]{:S(2)}) async-start(), calls=%async_computation | async-start | bytes 7864320 | tf_op jit(solution)/shard_map/all_gather | solution.py:2057
  163.7 230.8 %all-gather.7.cloned.1.call-start = ((), (), s32[]{:S(2)}) async-start(), calls=%async_computation.1 | async-start | bytes 7864320 | tf_op jit(solution)/shard_map/all_gather | solution.py:2057
  318.6 74.0 %copy-start.2 = (bf16[128,1536]{1,0:T(8,128)(2,1)S(1)}, bf16[128,1536]{1,0:T(8,128)(2,1)}, u32[]{:S(2)}) copy-start(bf16[128,1536]{1,0:T(8,128)(2,1)} %get-tuple-element.72) | copy-start | bytes 1179652
  318.6 74.0 %copy-start.3 = (bf16[128,1536]{1,0:T(8,128)(2,1)S(1)}, bf16[128,1536]{1,0:T(8,128)(2,1)}, u32[]{:S(2)}) copy-start(bf16[128,1536]{1,0:T(8,128)(2,1)} %get-tuple-element.82) | copy-start | bytes 1179652
  394.6 139.3 %copy-start.1 = (f32[128,1536]{1,0:T(8,128)S(1)}, f32[128,1536]{1,0:T(8,128)}, u32[]{:S(2)}) copy-start(f32[128,1536]{1,0:T(8,128)} %get-tuple-element.162) | copy-start | bytes 2359300
  538.7 5.2 copy-start
  538.7 8.0 %slice-start = ((s8[4718592]{0:T(1024)(128)(4,1)}), s8[4194304]{0:T(1024)(128)(4,1)S(1)}, s32[]{:S(2)}) async-start(s8[4718592]{0:T(1024)(128)(4,1)} %bitcast.73), calls=%async_computation.2 | async-start | bytes 8388608
  543.9 3.4 slice-start.1
Sparse Core Ops, SparseCore 0:
  163.8 115.4 all-gather.4
  280.9 113.6 all-gather.6
